TPU v7x, 128 devices: a whole 4x4x4 slice. The times are simulated.
128 devices in a mesh: psg: 32 (over z, x, core), head: 4 (over y).
Axes of the slice: x: 4, y: 4, z: 4, core: 2. Of those that a mesh axis runs over, the one named last changes fastest.
Arguments:
- q_psg: bfloat16 [8192, 8192], P('psg', 'head'), may hold values from -10 to 10
- k_psg: bfloat16 [8192, 1024], P('psg', 'head'), may hold values from -10 to 10
- v_psg: bfloat16 [8192, 1024], P('psg', 'head'), may hold values from -6 to 6
- do_psg: bfloat16 [8192, 8192], P('psg', 'head'), may hold values from -6 to 6
- q_qry: bfloat16 [4096, 8192], P('psg', 'head'), may hold values from -10 to 10
- k_qry: bfloat16 [4096, 1024], P('psg', 'head'), may hold values from -10 to 10
- v_qry: bfloat16 [4096, 1024], P('psg', 'head'), may hold values from -6 to 6
- do_qry: bfloat16 [4096, 8192], P('psg', 'head'), may hold values from -6 to 6
- w_key: bfloat16 [8192, 1024], P(None, 'head'), may hold values from -0.1875 to 0.1875
- w_value: bfloat16 [8192, 1024], P(None, 'head'), may hold values from -0.1875 to 0.1875
- req_passages: int32 [32, 16], replicated, may hold values from 0 to 63, as said below
- passage_slot: int32 [64], replicated, may hold values from 0 to 63, as said below
- query_owner: int32 [32], replicated, may hold values from 0 to 31, each once
Outputs:
- dq_psg: bfloat16 [8192, 8192], P('psg', 'head')
- dq_qry: bfloat16 [4096, 8192], P('psg', 'head')
- dx_psg: bfloat16 [8192, 8192], P(('psg', 'head'))
- dx_qry: bfloat16 [4096, 8192], P(('psg', 'head'))
Inputs may be any that keep to these rules, and one draw needn't show every extreme that they name: `req_passages`: the 16 passages of one request lie in 16 different row blocks of 2 passages each, passage_slot[id] // 2 being all different within the request. `passage_slot`: A permutation of the passage ids.
All inputs are finite; a program needn't handle non-finite values.
Results may differ from a plain program's by a relative error of at most 0.018.
Values may be sent and summed in bfloat16 or wider, within the bound.
A program may use at most 128 MiB of HBM per device.

v0:
```python
import jax
import jax.numpy as jnp
from jax import lax
from jax.sharding import PartitionSpec as P

HEADS = 64
KV_HEADS = 8
HEAD_DIM = 128
PLEN = 128
PSG_DEV = 2
QLEN = 128


def attend_back(query_rows, key_rows, value_rows, cotangent, allowed, softmax_scale):
    scores = (
        jnp.einsum("qhgd,khd->hgqk", query_rows, key_rows, preferred_element_type=jnp.float32)
        * softmax_scale
    )
    scores = jnp.where(allowed, scores, -1e30)
    row_max = jnp.max(scores, axis=-1, keepdims=True)
    weights = jnp.exp(scores - row_max)
    probs = weights / jnp.sum(weights, axis=-1, keepdims=True)
    probs_low = probs.astype(jnp.bfloat16)
    dprobs = jnp.einsum("qhgd,khd->hgqk", cotangent, value_rows, preferred_element_type=jnp.float32)
    delta_rows = jnp.sum(probs * dprobs, axis=-1, keepdims=True)
    dscore = (probs * (dprobs - delta_rows) * softmax_scale).astype(jnp.bfloat16)
    grad_q = jnp.einsum("hgqk,khd->qhgd", dscore, key_rows, preferred_element_type=jnp.float32)
    grad_k = jnp.einsum("hgqk,qhgd->khd", dscore, query_rows, preferred_element_type=jnp.float32)
    grad_v = jnp.einsum("hgqk,qhgd->khd", probs_low, cotangent, preferred_element_type=jnp.float32)
    return (grad_q, grad_k, grad_v)


def term_maker(rows_k, rows_v, w_key, w_value):
    contract = (((1,), (1,)), ((), ()))
    product = lax.dot_general(rows_k, w_key, contract, preferred_element_type=jnp.float32)
    return product + lax.dot_general(rows_v, w_value, contract, preferred_element_type=jnp.float32)


def local(
    q_psg,
    k_psg,
    v_psg,
    do_psg,
    q_qry,
    k_qry,
    v_qry,
    do_qry,
    w_key,
    w_value,
    req_passages,
    passage_slot,
    query_owner,
):
    kv_cols = k_psg.shape[1]
    kv_local = kv_cols // HEAD_DIM
    group_size = HEADS // KV_HEADS
    psg_rows = q_psg.shape[0]
    softmax_scale = HEAD_DIM ** (-0.5)
    owners = lax.axis_size("psg")
    my_index = lax.axis_index("psg")
    request_count = query_owner.shape[0]
    per_request = req_passages.shape[1]
    front_keys = per_request * PLEN
    causal = jnp.arange(PLEN)[None, :] <= jnp.arange(PLEN)[:, None]

    def passage_back(query_rows, key_rows, value_rows, cotangent):
        return attend_back(query_rows, key_rows, value_rows, cotangent, causal, softmax_scale)

    grad_qp, own_k, own_v = jax.vmap(passage_back)(
        q_psg.reshape(PSG_DEV, PLEN, kv_local, group_size, HEAD_DIM),
        k_psg.reshape(PSG_DEV, PLEN, kv_local, HEAD_DIM),
        v_psg.reshape(PSG_DEV, PLEN, kv_local, HEAD_DIM),
        do_psg.reshape(PSG_DEV, PLEN, kv_local, group_size, HEAD_DIM),
    )
    dq_psg = grad_qp.reshape(psg_rows, -1).astype(jnp.bfloat16)
    req_ids = jnp.arange(request_count, dtype=jnp.int32)
    my_request = jnp.sum(jnp.where(query_owner == my_index, req_ids, 0))
    all_slots = jnp.take(passage_slot, req_passages)
    my_slots = jnp.take(all_slots, my_request, axis=0)
    every_k, every_v = (
        lax.all_gather(k_psg, "psg", axis=0, tiled=True),
        lax.all_gather(v_psg, "psg", axis=0, tiled=True),
    )
    picked_k = jnp.take(every_k.reshape(-1, PLEN, kv_cols), my_slots, axis=0)
    picked_v = jnp.take(every_v.reshape(-1, PLEN, kv_cols), my_slots, axis=0)
    key_rows = jnp.concatenate([picked_k.reshape(front_keys, kv_cols), k_qry], 0).reshape(
        -1, kv_local, HEAD_DIM
    )
    value_rows = jnp.concatenate([picked_v.reshape(front_keys, kv_cols), v_qry], 0).reshape(
        -1, kv_local, HEAD_DIM
    )
    query_rows = q_qry.reshape(QLEN, kv_local, group_size, HEAD_DIM)
    cotangent = do_qry.reshape(QLEN, kv_local, group_size, HEAD_DIM)
    row_ids = jnp.arange(QLEN)[:, None]
    col_ids = jnp.arange(front_keys + QLEN)[None, :]
    allowed = (col_ids < front_keys) | (col_ids - front_keys <= row_ids)
    list_q = []
    list_k = []
    list_v = []
    for head_index in range(kv_local):
        grad_q, grad_k, grad_v = attend_back(
            query_rows[:, head_index : head_index + 1],
            key_rows[:, head_index : head_index + 1],
            value_rows[:, head_index : head_index + 1],
            cotangent[:, head_index : head_index + 1],
            allowed,
            softmax_scale,
        )
        list_q.append(grad_q)
        list_k.append(grad_k)
        list_v.append(grad_v)
    dq_qry = jnp.concatenate(list_q, 1).reshape(QLEN, -1).astype(jnp.bfloat16)
    grad_kq = jnp.concatenate(list_k, 1).reshape(-1, kv_cols)
    grad_vq = jnp.concatenate(list_v, 1).reshape(-1, kv_cols)
    part_k = grad_kq[:front_keys].astype(jnp.bfloat16).reshape(per_request, PLEN, kv_cols)
    part_v = grad_vq[:front_keys].astype(jnp.bfloat16).reshape(per_request, PLEN, kv_cols)
    key_grad_qry = grad_kq[front_keys:].astype(jnp.bfloat16)
    value_grad_qry = grad_vq[front_keys:].astype(jnp.bfloat16)
    passage_total = psg_rows // PLEN * owners
    full_k = jnp.zeros((passage_total, PLEN, kv_cols), jnp.bfloat16).at[my_slots].set(part_k)
    full_v = jnp.zeros((passage_total, PLEN, kv_cols), jnp.bfloat16).at[my_slots].set(part_v)
    summed_k, summed_v = (
        lax.psum_scatter(
            full_k.reshape(-1, kv_cols).astype(jnp.float32).astype(jnp.bfloat16),
            "psg",
            scatter_dimension=0,
            tiled=True,
        ).astype(jnp.float32),
        lax.psum_scatter(
            full_v.reshape(-1, kv_cols).astype(jnp.float32).astype(jnp.bfloat16),
            "psg",
            scatter_dimension=0,
            tiled=True,
        ).astype(jnp.float32),
    )
    key_grad_psg = (own_k.reshape(psg_rows, kv_cols) + summed_k).astype(jnp.bfloat16)
    value_grad_psg = (own_v.reshape(psg_rows, kv_cols) + summed_v).astype(jnp.bfloat16)
    dx_qry = lax.psum_scatter(
        term_maker(key_grad_qry, value_grad_qry, w_key, w_value).astype(jnp.bfloat16),
        "head",
        scatter_dimension=0,
        tiled=True,
    )
    dx_psg = lax.psum_scatter(
        term_maker(key_grad_psg, value_grad_psg, w_key, w_value).astype(jnp.bfloat16),
        "head",
        scatter_dimension=0,
        tiled=True,
    )
    return (dq_psg, dq_qry, dx_psg, dx_qry)


def solution(mesh):
    return jax.shard_map(
        local,
        mesh=mesh,
        in_specs=(
            P("psg", "head"),
            P("psg", "head"),
            P("psg", "head"),
            P("psg", "head"),
            P("psg", "head"),
            P("psg", "head"),
            P("psg", "head"),
            P("psg", "head"),
            P(None, "head"),
            P(None, "head"),
            P(),
            P(),
            P(),
        ),
        out_specs=(
            P("psg", "head"),
            P("psg", "head"),
            P(("psg", "head"), None),
            P(("psg", "head"), None),
        ),
        check_vma=False,
    )
```

profile of v0, /device:TPU:1, one launch (start us, length us, event | category | flops | bytes accessed | tf_op | source)
XLA Modules:
  0.0 418.3 jit_solution(2658014772859177986)
XLA Ops:
  12.9 3.3 gather_fusion
  21.1 39.2 %all-gather.3.cloned.1.call-done = bf16[8192,256]{1,0:T(8,128)(2,1)} async-done(((bf16[256,256]{1,0:T(8,128)(2,1)}), bf16[8192,256]{1,0:T(8,128)(2,1)}) %all-gather.3.cloned.1.call-update) | async-done | bytes 4194320 | tf_op jit(solution)/shard_map/all_gather | solution.py:81
  60.3 2.8 gather_fusion.1
  63.1 45.2 %all-gather.5.cloned.1.call-done = bf16[8192,256]{1,0:T(8,128)(2,1)} async-done(((bf16[256,256]{1,0:T(8,128)(2,1)}), bf16[8192,256]{1,0:T(8,128)(2,1)}) %all-gather.5.cloned.1.call-update) | async-done | bytes 4194320 | tf_op jit(solution)/shard_map/all_gather | solution.py:82
  108.3 2.8 gather_fusion.2
  113.8 5.8 %fusion.104 = (f32[8,128]{1,0:T(8,128)S(1)}, f32[1,8,128,2176]{2,3,1,0:T(8,128)}) fusion(bf16[128,2,8,128]{0,3,2,1:T(8,128)(2,1)} %bitcast.267, bf16[2048,2,128]{2,0,1:T(8,128)(2,1)S(1)} %copy.91, bf16[128,2,128]{2,0,1:T(8,128)(2,1)S(1)} %copy.92, pred[128,2176]{0,1:T(8,128)(4,1)S(1)} %fusion.37), kind=kOutput, calls=%fused_computation.133 | convolution fusion | flops 578223104 | bytes 10571776 | tf_op jit(solution)/shard_map/qhgd,khd->hgqk/dot_general | solution.py:16
  119.7 4.8 %fusion.103 = (f32[8,128]{1,0:T(8,128)S(1)}, f32[1,8,128,2176]{2,3,1,0:T(8,128)}) fusion(bf16[128,2,8,128]{0,3,2,1:T(8,128)(2,1)S(1)} %bitcast.268, bf16[128,2,128]{2,0,1:T(8,128)(2,1)S(1)} %copy.92, bf16[2048,2,128]{2,0,1:T(8,128)(2,1)S(1)} %copy.91, pred[128,2176]{0,1:T(8,128)(4,1)S(1)} %fusion.37), kind=kOutput, calls=%fused_computation.132 | convolution fusion | flops 578223104 | bytes 10571776 | tf_op jit(solution)/shard_map/qhgd,khd->hgqk/dot_general | solution.py:16
  124.9 4.9 %fusion.13 = f32[8,128]{1,0:T(8,128)S(1)} fusion(f32[1,8,128,2176]{2,3,1,0:T(8,128)} %get-tuple-element.39, f32[8,128]{1,0:T(8,128)S(1)} %get-tuple-element.38), kind=kLoop, calls=%fused_computation.28 | loop fusion | flops 4455424 | bytes 8921088 | tf_op jit(solution)/shard_map/reduce_sum | solution.py:22
  131.1 5.0 %fusion.8 = (f32[8,128]{1,0:T(8,128)S(1)}, f32[2176,128,8]{1,0,2:T(8,128)}) fusion(f32[8,128]{1,0:T(8,128)S(1)} %fusion.13, f32[1,8,128,2176]{2,3,1,0:T(8,128)S(1)} %copy-done.2, f32[8,128]{1,0:T(8,128)S(1)} %get-tuple-element.38, bf16[128,2,8,128]{0,3,2,1:T(8,128)(2,1)S(1)} %bitcast.278, bf16[2048,2,128]{2,0,1:T(8,128)(2,1)S(1)} %copy.97, ...), kind=kOutput, calls=%fused_computation.21 | convolution fusion | flops 580451328 | bytes 19214336 | tf_op jit(solution)/shard_map/qhgd,khd->hgqk/dot_general | solution.py:24
  136.1 5.0 %fusion.16 = bf16[8,128,2176]{1,2,0:T(8,128)(2,1)S(1)} fusion(f32[2176,128,8]{1,0,2:T(8,128)} %get-tuple-element.41, f32[8,128]{1,0:T(8,128)S(1)} %get-tuple-element.40, f32[8,128]{1,0:T(8,128)S(1)} %fusion.13, f32[1,8,128,2176]{2,3,1,0:T(8,128)S(1)} %copy-done.2, f32[8,128]{1,0:T(8,128)S(1)} %get-tuple-element.38), kind=kLoop, calls=%fused_computation.31 | loop fusion | flops 13369344 | bytes 22294528 | tf_op jit(solution)/shard_map/reshape.13
  144.4 5.2 %fusion.4 = (f32[8,128]{1,0:T(8,128)S(1)}, f32[2176,128,8]{1,0,2:T(8,128)}) fusion(f32[8,128]{1,0:T(8,128)S(1)} %fusion.15, f32[1,8,128,2176]{2,3,1,0:T(8,128)S(1)} %bitcast.257, f32[8,128]{1,0:T(8,128)S(1)} %get-tuple-element.34, bf16[128,2,8,128]{0,3,2,1:T(8,128)(2,1)S(1)} %bitcast.279, bf16[128,2,128]{2,0,1:T(8,128)(2,1)S(1)} %copy-done.28, ...), kind=kOutput, calls=%fused_computation.15 | convolution fusion | flops 580451328 | bytes 19214336 | tf_op jit(solution)/shard_map/qhgd,khd->hgqk/dot_general | solution.py:24
  149.6 4.8 %fusion.17 = bf16[8,128,2176]{1,2,0:T(8,128)(2,1)S(1)} fusion(f32[2176,128,8]{1,0,2:T(8,128)} %get-tuple-element.37, f32[8,128]{1,0:T(8,128)S(1)} %get-tuple-element.36, f32[8,128]{1,0:T(8,128)S(1)} %fusion.15, f32[1,8,128,2176]{2,3,1,0:T(8,128)S(1)} %bitcast.257, f32[8,128]{1,0:T(8,128)S(1)} %get-tuple-element.34), kind=kLoop, calls=%fused_computation.32 | loop fusion | flops 13369344 | bytes 22294528 | tf_op jit(solution)/shard_map/reshape.47
  158.1 2.5 broadcast.114.clone
  160.7 3.0 scatter_fusion
  163.7 5.4 %fusion.24 = bf16[2176,1,128]{0,2,1:T(8,128)(2,1)S(1)} fusion(bf16[128,2,8,128]{0,3,2,1:T(8,128)(2,1)S(1)} %bitcast.280, f32[1,8,128,2176]{2,3,1,0:T(8,128)} %get-tuple-element.39, f32[8,128]{1,0:T(8,128)S(1)} %fusion.13, f32[8,128]{1,0:T(8,128)S(1)} %get-tuple-element.38), kind=kOutput, calls=%fused_computation.39 | convolution fusion | flops 577110016 | bytes 9740288 | tf_op jit(solution)/shard_map/hgqk,qhgd->khd/dot_general | solution.py:29
  169.1 5.7 %fusion.27 = bf16[2176,1,128]{0,2,1:T(8,128)(2,1)S(1)} fusion(bf16[128,2,8,128]{0,3,2,1:T(8,128)(2,1)S(1)} %bitcast.281, f32[1,8,128,2176]{2,3,1,0:T(8,128)} %get-tuple-element.35, f32[8,128]{1,0:T(8,128)S(1)} %fusion.15, f32[8,128]{1,0:T(8,128)S(1)} %get-tuple-element.34), kind=kOutput, calls=%fused_computation.40 | convolution fusion | flops 577110016 | bytes 9740288 | tf_op jit(solution)/shard_map/hgqk,qhgd->khd/dot_general | solution.py:29
  176.4 2.5 broadcast.114.clone.1
  178.9 3.0 scatter_fusion.1
  183.8 4.0 fusion.105
  187.8 2.8 fusion.3
  194.9 3.4 fusion.98
  198.4 4.4 %convolution_bitcast_fusion.3 = f32[2,128,2,128]{3,1,2,0:T(8,128)S(1)} fusion(f32[2,2,128,128,8]{3,2,4,1,0:T(8,128)} %fusion.44, bf16[2,128,2,8,128]{4,3,2,1,0:T(8,128)(2,1)S(1)} %bitcast.276, f32[2,2,8,128,128]{3,4,2,1,0:T(8,128)} %get-tuple-element.33, f32[2,2,8,128]{3,2,1,0:T(8,128)S(1)} %get-tuple-element.32), kind=kOutput, calls=%fused_computation.60 | convolution fusion | flops 137891968 | bytes 5521408 | tf_op jit(solution)/shard_map/vmap(hgqk,qhgd->khd)/dot_general | solution.py:28
  202.9 2.0 convolution_bitcast_fusion.2
  205.2 38.0 %reduce-scatter.5.cloned.1.call-done = bf16[256,256]{1,0:T(8,128)(2,1)} async-done(((bf16[8192,256]{1,0:T(8,128)(2,1)}), bf16[256,256]{1,0:T(8,128)(2,1)}) %reduce-scatter.5.cloned.1.call-update) | async-done | bytes 131088 | tf_op jit(solution)/shard_map/reduce_scatter | solution.py:123
  243.1 6.8 %fusion.62 = f32[256,8192]{1,0:T(8,128)} fusion(bf16[8192,256]{1,0:T(8,128)(2,1)} %param.23, f32[32,8,2,128]{3,2,1,0:T(2,128)S(1)} %bitcast.272, bf16[256,256]{1,0:T(8,128)(2,1)} %reduce-scatter.5.cloned.1.call-done), kind=kOutput, calls=%fused_computation.101 | convolution fusion | flops 1073938432 | bytes 12976128 | tf_op jit(solution)/shard_map/dot_general | solution.py:35
  249.9 78.5 %reduce-scatter.7.cloned.1.call-done = bf16[256,256]{1,0:T(8,128)(2,1)} async-done(((bf16[8192,256]{1,0:T(8,128)(2,1)}), bf16[256,256]{1,0:T(8,128)(2,1)}) %reduce-scatter.7.cloned.1.call-update) | async-done | bytes 131088 | tf_op jit(solution)/shard_map/reduce_scatter | solution.py:129
  328.5 8.0 %fusion.2 = bf16[256,8192]{1,0:T(8,128)(2,1)} fusion(f32[256,8192]{1,0:T(8,128)} %fusion.62, bf16[8192,256]{1,0:T(8,128)(2,1)} %param.24, f32[32,8,2,128]{3,2,1,0:T(2,128)S(1)} %bitcast.271, bf16[256,256]{1,0:T(8,128)(2,1)} %reduce-scatter.7.cloned.1.call-done), kind=kOutput, calls=%fused_computation.8 | convolution fusion | flops 1078132736 | bytes 17170432 | tf_op jit(solution)/shard_map/dot_general | solution.py:36
  337.4 4.4 %fusion.34 = bf16[2,128,2,8,128]{4,1,3,2,0:T(8,128)(2,1)S(1)} fusion(f32[2,2,128,128,8]{3,2,4,1,0:T(8,128)} %fusion.44, bf16[2,128,2,128,1]{3,2,1,0,4:T(2,128)(2,1)S(1)} %bitcast.289, f32[2,2,8,128,128]{3,4,2,1,0:T(8,128)} %get-tuple-element.33, f32[2,2,8,128]{3,2,1,0:T(8,128)S(1)} %get-tuple-element.32), kind=kOutput, calls=%fused_computation.54 | convolution fusion | flops 138416256 | bytes 5390336 | tf_op jit(solution)/shard_map/vmap(hgqk,khd->qhgd)/dot_general | solution.py:27
  343.7 3.1 fusion.36
  346.8 3.1 fusion.35
  351.1 10.8 %reduce-scatter.11.cloned.1.call-done = bf16[32,8192]{1,0:T(8,128)(2,1)} async-done(((bf16[128,8192]{1,0:T(8,128)(2,1)}), bf16[32,8192]{1,0:T(8,128)(2,1)}) %reduce-scatter.11.cloned.1.call-update) | async-done | bytes 524304 | tf_op jit(solution)/shard_map/reduce_scatter | solution.py:138
  361.9 49.5 %reduce-scatter.9.cloned.1.call-done = bf16[64,8192]{1,0:T(8,128)(2,1)} async-done(((bf16[256,8192]{1,0:T(8,128)(2,1)}), bf16[64,8192]{1,0:T(8,128)(2,1)}) %reduce-scatter.9.cloned.1.call-update) | async-done | bytes 1048592 | tf_op jit(solution)/shard_map/reduce_scatter | solution.py:144
  (126 shorter events, 31.8 us)
Async XLA Ops:
  7.2 5.7 %copy-start = (s32[64]{0:T(128)S(1)}, s32[64]{0:T(128)}, u32[]{:S(2)}) copy-start(s32[64]{0:T(128)} %param.26) | copy-start | bytes 772
  7.2 53.2 %all-gather.3.cloned.1.call-start = ((), (), s32[]{:S(2)}) async-start(), calls=%async_computation.4 | async-start | bytes 4325376 | tf_op jit(solution)/shard_map/all_gather | solution.py:81
  7.9 100.4 %all-gather.5.cloned.1.call-start = ((), (), s32[]{:S(2)}) async-start(), calls=%async_computation.5 | async-start | bytes 4325376 | tf_op jit(solution)/shard_map/all_gather | solution.py:82
  8.7 234.5 %reduce-scatter.5.cloned.1.call-start = ((), (), s32[]{:S(2)}) async-start(), calls=%async_computation.6 | async-start | bytes 4325376 | tf_op jit(solution)/shard_map/reduce_scatter | solution.py:123
  12.8 3.5 copy-start.18
  12.9 4.5 %copy-start.26 = (bf16[128,256]{1,0:T(8,128)(2,1)S(1)}, bf16[128,256]{1,0:T(8,128)(2,1)}, u32[]{:S(2)}) copy-start(bf16[128,256]{1,0:T(8,128)(2,1)} %param.20) | copy-start | bytes 196612
  12.9 4.7 %copy-start.19 = (bf16[128,2048]{1,0:T(8,128)(2,1)S(1)}, bf16[128,2048]{1,0:T(8,128)(2,1)}, u32[]{:S(2)}) copy-start(bf16[128,2048]{1,0:T(8,128)(2,1)} %param.22) | copy-start | bytes 1572868
  12.9 5.7 %copy-start.27 = (bf16[128,256]{1,0:T(8,128)(2,1)S(1)}, bf16[128,256]{1,0:T(8,128)(2,1)}, u32[]{:S(2)}) copy-start(bf16[128,256]{1,0:T(8,128)(2,1)} %param.21) | copy-start | bytes 196612
  113.8 5.8 %copy-start.13 = (bf16[128,2048]{0,1:T(8,128)(2,1)S(1)}, bf16[128,2048]{0,1:T(8,128)(2,1)}, u32[]{:S(2)}) copy-start(bf16[128,2048]{0,1:T(8,128)(2,1)} %copy.93) | copy-start | bytes 1572868
  124.8 5.1 %copy-start.20 = (bf16[128,2048]{0,1:T(8,128)(2,1)S(1)}, bf16[128,2048]{0,1:T(8,128)(2,1)}, u32[]{:S(2)}) copy-start(bf16[128,2048]{0,1:T(8,128)(2,1)} %copy.99) | copy-start | bytes 1572868
  124.8 5.1 %copy-start.28 = (bf16[128,2,128]{2,0,1:T(8,128)(2,1)S(1)}, bf16[128,2,128]{2,0,1:T(8,128)(2,1)}, u32[]{:S(2)}) copy-start(bf16[128,2,128]{2,0,1:T(8,128)(2,1)} %copy.98) | copy-start | bytes 196612
  124.9 6.1 %copy-start.2 = (f32[1,8,128,2176]{2,3,1,0:T(8,128)S(1)}, f32[1,8,128,2176]{2,3,1,0:T(8,128)}, u32[]{:S(2)}) copy-start(f32[1,8,128,2176]{2,3,1,0:T(8,128)} %get-tuple-element.39) | copy-start | bytes 26738692
  136.1 6.6 %slice-start = ((s8[8912896]{0:T(1024)(128)(4,1)}), s8[4194304]{0:T(1024)(128)(4,1)S(1)}, s32[]{:S(2)}) async-start(s8[8912896]{0:T(1024)(128)(4,1)} %bitcast.256), calls=%async_computation.10 | async-start | bytes 8388608
  136.1 5.0 %copy-start.14 = (bf16[128,2048]{0,1:T(8,128)(2,1)S(1)}, bf16[128,2048]{0,1:T(8,128)(2,1)}, u32[]{:S(2)}) copy-start(bf16[128,2048]{0,1:T(8,128)(2,1)} %copy.93) | copy-start | bytes 1572868
  136.1 6.7 %slice-start.1 = ((s8[8912896]{0:T(1024)(128)(4,1)}), s8[4194304]{0:T(1024)(128)(4,1)S(1)}, s32[]{:S(2)}) async-start(s8[8912896]{0:T(1024)(128)(4,1)} %bitcast.256), calls=%async_computation.11 | async-start | bytes 8388608
  136.1 7.2 %slice-start.2 = ((s8[8912896]{0:T(1024)(128)(4,1)}), s8[524288]{0:T(1024)(128)(4,1)S(1)}, s32[]{:S(2)}) async-start(s8[8912896]{0:T(1024)(128)(4,1)} %bitcast.256), calls=%async_computation.12 | async-start | bytes 1048576
  141.1 3.4 copy-start.3
  142.6 13.4 %copy-start.6 = (bf16[2176,1,128]{0,2,1:T(8,128)(2,1)}, bf16[2176,1,128]{0,2,1:T(8,128)(2,1)S(1)}, u32[]{:S(2)}) copy-start(bf16[2176,1,128]{0,2,1:T(8,128)(2,1)S(1)} %convolution_bitcast_fusion.1) | copy-start | bytes 1671172
  160.7 3.1 copy-start.21
  163.7 164.8 %reduce-scatter.7.cloned.1.call-start = ((), (), s32[]{:S(2)}) async-start(), calls=%async_computation.7 | async-start | bytes 4325376 | tf_op jit(solution)/shard_map/reduce_scatter | solution.py:129
  169.1 5.7 %copy-start.10 = (bf16[2176,1,128]{0,2,1:T(8,128)(2,1)}, bf16[2176,1,128]{0,2,1:T(8,128)(2,1)S(1)}, u32[]{:S(2)}) copy-start(bf16[2176,1,128]{0,2,1:T(8,128)(2,1)S(1)} %fusion.24) | copy-start | bytes 1671172
  178.9 4.8 %copy-start.7 = (bf16[2176,1,128]{0,2,1:T(8,128)(2,1)S(1)}, bf16[2176,1,128]{0,2,1:T(8,128)(2,1)}, u32[]{:S(2)}) copy-start(bf16[2176,1,128]{0,2,1:T(8,128)(2,1)} %copy-done.6) | copy-start | bytes 1671172
  178.9 4.8 %copy-start.9 = (bf16[2176,1,128]{0,2,1:T(8,128)(2,1)S(1)}, bf16[2176,1,128]{0,2,1:T(8,128)(2,1)}, u32[]{:S(2)}) copy-start(bf16[2176,1,128]{0,2,1:T(8,128)(2,1)} %copy-done.8) | copy-start | bytes 1671172
  181.9 180.0 %reduce-scatter.11.cloned.1.call-start = ((), (), s32[]{:S(2)}) async-start(), calls=%async_computation.9 | async-start | bytes 2621440 | tf_op jit(solution)/shard_map/reduce_scatter | solution.py:138
  183.8 4.0 copy-start.5
  187.7 3.2 copy-start.22
  187.8 3.9 copy-start.23
  187.8 3.9 copy-start.15
  190.6 220.8 %reduce-scatter.9.cloned.1.call-start = ((), (), s32[]{:S(2)}) async-start(), calls=%async_computation.8 | async-start | bytes 5242880 | tf_op jit(solution)/shard_map/reduce_scatter | solution.py:144
  191.7 3.2 copy-start.24
  193.1 5.2 %copy-start.17 = (bf16[32,8,16,128]{3,2,1,0:T(8,128)(2,1)S(1)}, bf16[32,8,16,128]{3,2,1,0:T(8,128)(2,1)}, u32[]{:S(2)}) copy-start(bf16[32,8,16,128]{3,2,1,0:T(8,128)(2,1)} %copy.156) | copy-start | bytes 3145732
  343.7 67.7 %copy-start.1 = (s32[64]{0:T(128)S(1)}, s32[64]{0:T(128)}, u32[]{:S(2)}) copy-start(s32[64]{0:T(128)} %param.26) | copy-start | bytes 772
  (6 other events, 8.3 us)
Sparse Core Ops, SparseCore 0:
  10.3 50.0 all-gather.2
  62.6 45.6 all-gather.4
  163.8 79.3 reduce-scatter.4
  247.1 81.3 reduce-scatter.6
  331.3 30.5 reduce-scatter.10
  364.9 46.5 reduce-scatter.8
where the time goes:
time: 419 us; the launch traced here: 418 us
  waiting for transfers between devices  263 us (63%)
  matrix products  78.8 us (19%)
  local copies, waits for them, and re-layouts  38.6 us (9%)
  other arithmetic  21 us (5%)
  between operations  16.7 us (4%)
    reduce_scatter x1, waiting for transfers between devices, local(): lax.psum_scatter(full_v.reshape(-1, kv_cols).astype(jnp.float32).astype(j...  78.5 us
    reduce_scatter x1, waiting for transfers between devices, local(): lax.psum_scatter(term_maker(key_grad_psg, value_grad_psg, w_key, w_value)...  49.5 us
    all_gather x1, waiting for transfers between devices, local(): lax.all_gather(v_psg, 'psg', axis=0, tiled=True)  45.2 us
    all_gather x1, waiting for transfers between devices, local(): lax.all_gather(k_psg, 'psg', axis=0, tiled=True)  39.2 us
    reduce_scatter x1, waiting for transfers between devices, local(): lax.psum_scatter(full_k.reshape(-1, kv_cols).astype(jnp.float32).astype(j...  38 us
    dot_general x3, matrix products, attend_back(): jnp.einsum('hgqk,qhgd->khd', probs_low, cotangent, preferred_element_type...  13.1 us
    dot_general x3, matrix products, attend_back(): jnp.einsum('qhgd,khd->hgqk', cotangent, value_rows, preferred_element_typ...  12 us
    dot_general x2, matrix products, term_maker(): lax.dot_general(rows_v, w_value, contract, preferred_element_type=jnp.flo...  10.9 us
  transfers between devices with their start and end apart: 6, of which 6 were waited for; matrix products, arithmetic and copies ran while one was open for 19% of the time, Pallas kernels for 0%

commit v1 on v0

v1 whole, which is shorter than its diff:
```python
import functools

import jax
import jax.numpy as jnp
from jax import lax
from jax.experimental import pallas as pl
from jax.experimental.pallas import tpu as pltpu
from jax.sharding import PartitionSpec as P

D = 128
G = 8
PLEN = 128
KV = 2
NPSG = 64
REQ = 32
P_REQ = 16
CB = 256
C = D ** -0.5
C2 = C * 1.4426950408889634
F32 = jnp.float32
BF16 = jnp.bfloat16


def stack(x):
    return jnp.concatenate([x[:, g * D:(g + 1) * D] for g in range(G)], axis=0)


def dot(a, b):
    return jnp.dot(a, b, preferred_element_type=F32)


def dot_t(a, b):
    return lax.dot_general(a, b, (((1,), (1,)), ((), ())), preferred_element_type=F32)


def causal_cols(shape):
    key = lax.broadcasted_iota(jnp.int32, shape, 0)
    qry = lax.broadcasted_iota(jnp.int32, shape, 1) % PLEN
    return key <= qry


def psg_kernel(q_ref, k_ref, v_ref, do_ref, dq_ref, gk_ref, gv_ref):
    qs = stack(q_ref[...])
    dos = stack(do_ref[...])
    k = k_ref[...]
    v = v_ref[...]
    kt = k.T
    gk = jnp.zeros((PLEN, D), F32)
    gv = jnp.zeros((PLEN, D), F32)
    for b in range(G * PLEN // CB):
        cols = slice(b * CB, (b + 1) * CB)
        s = dot_t(k, qs[cols])
        s = jnp.where(causal_cols(s.shape), s, -1e30)
        e = jnp.exp2((s - jnp.max(s, axis=0, keepdims=True)) * C2)
        inv = 1.0 / jnp.sum(e, axis=0, keepdims=True)
        dp = dot_t(v, dos[cols])
        p = e * inv
        delta = jnp.sum(p * dp, axis=0, keepdims=True)
        ds = (p * (dp - delta)).astype(BF16)
        gk += dot(ds, qs[cols])
        gv += dot(p.astype(BF16), dos[cols])
        dqt = dot(kt, ds) * C
        for i in range(CB // PLEN):
            g = b * (CB // PLEN) + i
            dq_ref[:, g * D:(g + 1) * D] = dqt[:, i * PLEN:(i + 1) * PLEN].T.astype(BF16)
    gk_ref[...] = gk * C
    gv_ref[...] = gv


def psg_back(q, k, v, do):
    rows = q.shape[0]
    wide = pl.BlockSpec((PLEN, G * D), lambda n, h: (n, h))
    thin = pl.BlockSpec((PLEN, D), lambda n, h: (n, h))
    return pl.pallas_call(
        psg_kernel,
        grid=(rows // PLEN, KV),
        in_specs=[wide, thin, thin, wide],
        out_specs=[wide, thin, thin],
        out_shape=[
            jax.ShapeDtypeStruct(q.shape, BF16),
            jax.ShapeDtypeStruct(k.shape, F32),
            jax.ShapeDtypeStruct(v.shape, F32),
        ],
        compiler_params=pltpu.CompilerParams(vmem_limit_bytes=40 * 1024 * 1024),
        cost_estimate=pl.CostEstimate(flops=4 * 5 * 2 * 1024 * 128 * 128, bytes_accessed=4 * 1024 * 1024, transcendentals=4 * 1024 * 128),
        name="psg_back",
    )(q, k, v, do)


TK = 256
NT = P_REQ * PLEN // TK


def qry_kernel(
    req_ref, slot_ref, owner_ref, kvg_ref, q_ref, do_ref, kq_ref, vq_ref, me_ref,
    dq_ref, gk_ref, gv_ref, full_ref,
    qs, dos, qst, dost, kbuf, vbuf, ktbuf, ebuf, dpbuf, mt, dqt, gkbuf, gvbuf, zeros, slots, mask,
    in_sem, out_sem, zero_sem,
):
    h = pl.program_id(0)
    me = me_ref[0]

    @pl.when(h == 0)
    def _():
        zeros[...] = jnp.zeros_like(zeros)
        request = jnp.int32(0)
        for r in range(REQ):
            request = jnp.where(owner_ref[r] == me, r, request)

        def clear(i, c):
            mask[i] = 0
            return c

        lax.fori_loop(0, NPSG, clear, 0)

        def pick(j, c):
            slot = slot_ref[req_ref[request, j]]
            slots[j] = slot
            mask[slot] = 1
            return c

        lax.fori_loop(0, P_REQ, pick, 0)

        def blank(i, c):
            @pl.when(mask[i] == 0)
            def _():
                pltpu.make_async_copy(zeros, full_ref.at[i], zero_sem).start()

            return c

        lax.fori_loop(0, NPSG, blank, 0)

    kcols = pl.ds(pl.multiple_of(h * D, D), D)
    vcols = pl.ds(pl.multiple_of(KV * D + h * D, D), D)
    copies = []
    for j in range(P_REQ):
        rows = pl.ds(j * PLEN, PLEN)
        copies.append(pltpu.make_async_copy(kvg_ref.at[slots[j], :, kcols], kbuf.at[rows], in_sem.at[0]))
        copies.append(pltpu.make_async_copy(kvg_ref.at[slots[j], :, vcols], vbuf.at[rows], in_sem.at[1]))
    for copy in copies:
        copy.start()
    qs[...] = stack(q_ref[...])
    dos[...] = stack(do_ref[...])
    qst[...] = qs[...].T
    dost[...] = dos[...].T

    def first(t, keys, values, rows, masked, carry):
        m, l, num = carry
        ms, ls, nums = [], [], []
        for b in range(G * PLEN // CB):
            cols = slice(b * CB, (b + 1) * CB)
            s = dot(keys, qst[:, cols])
            if masked:
                s = jnp.where(causal_cols(s.shape), s, -1e30)
            m_old = m[:, cols]
            m_new = jnp.maximum(m_old, jnp.max(s, axis=0, keepdims=True))
            alpha = jnp.exp2((m_old - m_new) * C2)
            e = jnp.exp2((s - m_new) * C2)
            dp = dot(values, dost[:, cols])
            ebuf[rows, cols] = e
            dpbuf[rows, cols] = dp
            ms.append(m_new)
            ls.append(l[:, cols] * alpha + jnp.sum(e, axis=0, keepdims=True))
            nums.append(num[:, cols] * alpha + jnp.sum(e * dp, axis=0, keepdims=True))
        m = jnp.concatenate(ms, axis=1)
        mt[t] = m
        return m, jnp.concatenate(ls, axis=1), jnp.concatenate(nums, axis=1)

    wide = (1, G * PLEN)
    own = slice(P_REQ * PLEN, P_REQ * PLEN + PLEN)
    carry = (jnp.full(wide, -1e30, F32), jnp.zeros(wide, F32), jnp.zeros(wide, F32))
    carry = first(NT, kq_ref[...], vq_ref[...], own, True, carry)
    for copy in copies:
        copy.wait()

    def step(t, carry):
        rows = pl.ds(pl.multiple_of(t * TK, TK), TK)
        keys = kbuf[rows, :]
        ktbuf[t] = keys.T
        return first(t, keys, vbuf[rows, :], rows, False, carry)

    m, l, num = lax.fori_loop(0, NT, step, carry)
    inv = 1.0 / l
    delta = num * inv

    def second(t, kt, rows, out_rows, acc):
        scale = jnp.exp2((mt[t] - m) * C2) * inv
        gk = gv = None
        for b in range(G * PLEN // CB):
            cols = slice(b * CB, (b + 1) * CB)
            p = ebuf[rows, cols] * scale[:, cols]
            ds = (p * (dpbuf[rows, cols] - delta[:, cols])).astype(BF16)
            dk = dot(ds, qs[cols, :])
            dv = dot(p.astype(BF16), dos[cols, :])
            gk = dk if gk is None else gk + dk
            gv = dv if gv is None else gv + dv
            more = dot(kt, ds)
            dqt[:, cols] = dqt[:, cols] + more if acc else more
        return (gk * C).astype(BF16), gv.astype(BF16)

    gk, gv = second(NT, kq_ref[...].T, own, None, False)
    gk_ref[...] = gk
    gv_ref[...] = gv

    def back(t, c):
        rows = pl.ds(pl.multiple_of(t * TK, TK), TK)
        gk, gv = second(t, ktbuf[t], rows, rows, True)
        gkbuf[rows, :] = gk
        gvbuf[rows, :] = gv
        for i in range(TK // PLEN):
            j = t * (TK // PLEN) + i
            part = pl.ds(pl.multiple_of(j * PLEN, PLEN), PLEN)
            slot = slots[j]
            pltpu.make_async_copy(gkbuf.at[part], full_ref.at[slot, :, kcols], out_sem.at[0]).start()
            pltpu.make_async_copy(gvbuf.at[part], full_ref.at[slot, :, vcols], out_sem.at[1]).start()
        return c

    lax.fori_loop(0, NT, back, 0)
    for g in range(G):
        dq_ref[:, g * D:(g + 1) * D] = (dqt[:, g * PLEN:(g + 1) * PLEN] * C).T.astype(BF16)

    def drain(j, c):
        rows = pl.ds(pl.multiple_of(j * PLEN, PLEN), PLEN)
        pltpu.make_async_copy(gkbuf.at[rows], full_ref.at[slots[j], :, kcols], out_sem.at[0]).wait()
        pltpu.make_async_copy(gvbuf.at[rows], full_ref.at[slots[j], :, vcols], out_sem.at[1]).wait()
        return c

    lax.fori_loop(0, P_REQ, drain, 0)

    @pl.when(h == KV - 1)
    def _():
        def blanked(i, c):
            @pl.when(mask[i] == 0)
            def _():
                pltpu.make_async_copy(zeros, full_ref.at[i], zero_sem).wait()

            return c

        lax.fori_loop(0, NPSG, blanked, 0)


def qry_back(req, slot, owner, kvg, q, do, kq, vq, me):
    keys = P_REQ * PLEN + PLEN
    wide = pl.BlockSpec((PLEN, G * D), lambda h: (0, h))
    thin = pl.BlockSpec((PLEN, D), lambda h: (0, h))
    smem = pl.BlockSpec(memory_space=pltpu.SMEM)
    hbm = pl.BlockSpec(memory_space=pl.ANY)
    return pl.pallas_call(
        qry_kernel,
        grid=(KV,),
        in_specs=[smem, smem, smem, hbm, wide, wide, thin, thin, smem],
        out_specs=[wide, thin, thin, hbm],
        out_shape=[
            jax.ShapeDtypeStruct(q.shape, BF16),
            jax.ShapeDtypeStruct(kq.shape, BF16),
            jax.ShapeDtypeStruct(vq.shape, BF16),
            jax.ShapeDtypeStruct((NPSG, PLEN, 2 * KV * D), BF16),
        ],
        scratch_shapes=[
            pltpu.VMEM((G * PLEN, D), BF16),
            pltpu.VMEM((G * PLEN, D), BF16),
            pltpu.VMEM((D, G * PLEN), BF16),
            pltpu.VMEM((D, G * PLEN), BF16),
            pltpu.VMEM((P_REQ * PLEN, D), BF16),
            pltpu.VMEM((P_REQ * PLEN, D), BF16),
            pltpu.VMEM((NT, D, TK), BF16),
            pltpu.VMEM((keys, G * PLEN), F32),
            pltpu.VMEM((keys, G * PLEN), F32),
            pltpu.VMEM((NT + 1, 1, G * PLEN), F32),
            pltpu.VMEM((D, G * PLEN), F32),
            pltpu.VMEM((P_REQ * PLEN, D), BF16),
            pltpu.VMEM((P_REQ * PLEN, D), BF16),
            pltpu.VMEM((PLEN, 2 * KV * D), BF16),
            pltpu.SMEM((P_REQ,), jnp.int32),
            pltpu.SMEM((NPSG,), jnp.int32),
            pltpu.SemaphoreType.DMA((2,)),
            pltpu.SemaphoreType.DMA((2,)),
            pltpu.SemaphoreType.DMA,
        ],
        compiler_params=pltpu.CompilerParams(vmem_limit_bytes=48 * 1024 * 1024),
        cost_estimate=pl.CostEstimate(flops=2 * 5 * 2 * 1024 * 2176 * 128, bytes_accessed=16 * 1024 * 1024, transcendentals=2 * 1024 * 2176),
        name="qry_back",
    )(req, slot, owner, kvg, q, do, kq, vq, me)


WB = 1024


def term_kernel(k_ref, v_ref, wk_ref, wv_ref, out_ref):
    out_ref[...] = (dot_t(k_ref[...], wk_ref[...]) + dot_t(v_ref[...], wv_ref[...])).astype(BF16)


def term(rows_k, rows_v, w_key, w_value):
    rows = rows_k.shape[0]
    width, depth = w_key.shape
    return pl.pallas_call(
        term_kernel,
        grid=(width // WB,),
        in_specs=[
            pl.BlockSpec((rows, depth), lambda i: (0, 0)),
            pl.BlockSpec((rows, depth), lambda i: (0, 0)),
            pl.BlockSpec((WB, depth), lambda i: (i, 0)),
            pl.BlockSpec((WB, depth), lambda i: (i, 0)),
        ],
        out_specs=pl.BlockSpec((rows, WB), lambda i: (0, i)),
        out_shape=jax.ShapeDtypeStruct((rows, width), BF16),
        compiler_params=pltpu.CompilerParams(vmem_limit_bytes=32 * 1024 * 1024),
        cost_estimate=pl.CostEstimate(flops=4 * rows * width * depth, bytes_accessed=4 * width * depth + 2 * rows * width, transcendentals=0),
        name="term",
    )(rows_k, rows_v, w_key, w_value)


def local(q_psg, k_psg, v_psg, do_psg, q_qry, k_qry, v_qry, do_qry, w_key, w_value, req_passages, passage_slot, query_owner):
    me = lax.axis_index("psg").astype(jnp.int32).reshape(1)
    kv = jnp.concatenate([k_psg, v_psg], axis=1)
    every = lax.all_gather(kv, "psg", axis=0, tiled=True)
    dq_psg, own_k, own_v = psg_back(q_psg, k_psg, v_psg, do_psg)
    dq_qry, gk_qry, gv_qry, full = qry_back(
        req_passages, passage_slot, query_owner, every.reshape(NPSG, PLEN, -1), q_qry, do_qry, k_qry, v_qry, me
    )
    summed = lax.psum_scatter(full.reshape(NPSG * PLEN, -1), "psg", scatter_dimension=0, tiled=True)
    dx_qry = lax.psum_scatter(term(gk_qry, gv_qry, w_key, w_value), "head", scatter_dimension=0, tiled=True)
    cols = KV * D
    gk = (own_k + summed[:, :cols].astype(F32)).astype(BF16)
    gv = (own_v + summed[:, cols:].astype(F32)).astype(BF16)
    dx_psg = lax.psum_scatter(term(gk, gv, w_key, w_value), "head", scatter_dimension=0, tiled=True)
    return dq_psg, dq_qry, dx_psg, dx_qry


def solution(mesh):
    rows = P("psg", "head")
    return jax.shard_map(
        local,
        mesh=mesh,
        in_specs=(rows,) * 8 + (P(None, "head"),) * 2 + (P(),) * 3,
        out_specs=(rows, rows, P(("psg", "head"), None), P(("psg", "head"), None)),
        check_vma=False,
    )
```

time: 419 us -> 280 us (0.67)
  matrix products: 78.8 us -> 0 us
  waiting for transfers between devices: 263 us -> 204 us
  Pallas kernels: 0 us -> 41.7 us
  local copies, waits for them, and re-layouts: 38.6 us -> 16.5 us
  other arithmetic: 21 us -> 2.71 us
    dot_general x18 -> x0, matrix products: 75.3 us -> none  [the longest x3 13.1 us: attend_back(): jnp.einsum('hgqk,qhgd->khd', probs_low, cotangent, preferred_element_type...]
    pallas_call x0 -> x4, Pallas kernels: none -> 41.7 us  [the longest x1 26.4 us: qry_back(): pl.pallas_call(qry_kernel, grid=(KV,), in_specs=[smem, smem, smem, hbm, w...]
    reduce_scatter x4 -> x3, waiting for transfers between devices: 177 us -> 146 us  [the longest x1 74.5 us: local(): lax.psum_scatter(full.reshape(NPSG * PLEN, -1), 'psg', scatter_dimension=...]
    all_gather x2 -> x1, waiting for transfers between devices: 84.4 us -> 57.8 us  [local(): every = lax.all_gather(kv, 'psg', axis=0, tiled=True)]
    another operation x4 -> x0, other arithmetic: 10 us -> none
    gather x4 -> x0, local copies, waits for them, and re-layouts: 9.02 us -> none  [the longest x2 3.43 us: local(): all_slots = jnp.take(passage_slot, req_passages)]
    reduce_sum x3 -> x0, other arithmetic: 7.34 us -> none  [the longest x2 6.05 us: attend_back(): probs = weights / jnp.sum(weights, axis=-1, keepdims=True)]
    scatter x2 -> x0, local copies, waits for them, and re-layouts: 6 us -> none  [local(): jnp.zeros((passage_total, PLEN, kv_cols), jnp.bfloat16).at[my_slots]]
  transfers between devices with their start and end apart: 6 -> 4, of which waited for: 6 -> 4; matrix products, arithmetic and copies ran while one was open for 19% -> 1% of each run, Pallas kernels for 0% -> 5%
where the time goes in v1:
time: 280 us; the launch traced here: 279 us
  waiting for transfers between devices  204 us (73%)
  Pallas kernels  41.7 us (15%)
  local copies, waits for them, and re-layouts  16.5 us (6%)
  between operations  13.9 us (5%)
    reduce_scatter x1, waiting for transfers between devices, local(): lax.psum_scatter(full.reshape(NPSG * PLEN, -1), 'psg', scatter_dimension=...  74.5 us
    all_gather x1, waiting for transfers between devices, local(): every = lax.all_gather(kv, 'psg', axis=0, tiled=True)  57.8 us
    reduce_scatter x1, waiting for transfers between devices, local(): lax.psum_scatter(term(gk, gv, w_key, w_value), 'head', scatter_dimension=...  49.4 us
    pallas_call x1, Pallas kernels, qry_back(): pl.pallas_call(qry_kernel, grid=(KV,), in_specs=[smem, smem, smem, hbm, w...  26.4 us
    reduce_scatter x1, waiting for transfers between devices, local(): lax.psum_scatter(term(gk_qry, gv_qry, w_key, w_value), 'head', scatter_di...  22.4 us
    unnamed x31, local copies, waits for them, and re-layouts  16.5 us
    pallas_call x2, Pallas kernels, term(): pl.pallas_call(term_kernel, grid=(width // WB,), in_specs=[pl.BlockSpec((...  9.31 us
    pallas_call x1, Pallas kernels, psg_back(): pl.pallas_call(psg_kernel, grid=(rows // PLEN, KV), in_specs=[wide, thin,...  6 us
  transfers between devices with their start and end apart: 4, of which 4 were waited for; matrix products, arithmetic and copies ran while one was open for 1% of the time, Pallas kernels for 5%

profile of v1, /device:TPU:1, one launch (start us, length us, event | category | flops | bytes accessed | tf_op | source)
XLA Modules:
  0.0 279.1 jit_solution(10550246523233083046)
XLA Ops:
  7.2 0.0 all-gather.2.cloned.1.call-start
  7.2 1.7 pad_maximum_fusion
  8.9 0.0 all-gather.2.cloned.1.call-update
  8.9 0.0 reduce-scatter.4.cloned.1.call-start
  9.0 0.8 copy.17.req_ref
  9.8 57.8 %all-gather.2.cloned.1.call-done = bf16[8192,512]{1,0:T(8,128)(2,1)} async-done(((bf16[256,512]{1,0:T(8,128)(2,1)}), bf16[8192,512]{1,0:T(8,128)(2,1)}) %all-gather.2.cloned.1.call-update) | async-done | bytes 8388624 | tf_op jit(solution)/shard_map/all_gather | solution.py:316
  67.5 1.0 copy-done.9
  68.6 1.0 copy-done.10
  69.6 0.8 copy-done.11
  70.5 0.8 copy-done.12
  71.3 0.7 copy-done.13
  72.0 0.7 copy-done.14
  72.6 26.4 %qry_back.1 = (bf16[128,2048]{1,0:T(8,128)(2,1)}, bf16[128,256]{1,0:T(8,128)(2,1)S(1)}, bf16[128,256]{1,0:T(8,128)(2,1)S(1)}, bf16[64,128,512]{2,1,0:T(8,128)(2,1)}) custom-call(s32[32,16]{1,0:T(8,128)S(1)} %copy.17.req_ref, s32[64]{0:T(128)S(1)} %copy-done.13, s32[32]{0:T(128)S(1)} %copy-done.14, bf16[64,128,512]{2,1,0:T(8,128)(2,1)} %bitcast.4, ...), custom_call_target="tpu_custom_call" | custom-call | flops 5704253440 | bytes 16777216 | tf_op jit(solution)/shard_map/qry_back/pallas_call | solution.py:248
  99.0 0.0 reduce-scatter.4.cloned.1.call-update
  99.1 0.0 reduce-scatter.8.cloned.1.call-start
  99.1 0.0 copy-start.1
  99.1 2.2 copy-done.1
  101.3 2.2 copy-done.3
  103.5 5.3 %term.3 = bf16[128,8192]{1,0:T(8,128)(2,1)} custom-call(bf16[128,256]{1,0:T(8,128)(2,1)S(1)} %get-tuple-element.16.k_ref, bf16[128,256]{1,0:T(8,128)(2,1)S(1)} %get-tuple-element.17.v_ref, bf16[8192,256]{1,0:T(8,128)(2,1)S(1)} %copy-done.1, bf16[8192,256]{1,0:T(8,128)(2,1)S(1)} %copy-done.3), custom_call_target="tpu_custom_call" | custom-call | flops 1073741824 | bytes 10485760 | tf_op jit(solution)/shard_map/term/pallas_call | solution.py:296
  108.8 0.0 reduce-scatter.8.cloned.1.call-update
  108.8 0.0 reduce-scatter.6.cloned.1.call-start
  108.9 6.0 %psg_back.1 = (bf16[256,2048]{1,0:T(8,128)(2,1)}, f32[256,256]{1,0:T(8,128)S(1)}, f32[256,256]{1,0:T(8,128)S(1)}) custom-call(bf16[256,2048]{1,0:T(8,128)(2,1)S(1)} %copy-done.7, bf16[256,256]{1,0:T(8,128)(2,1)S(1)} %copy-done.5, bf16[256,256]{1,0:T(8,128)(2,1)S(1)} %copy-done.6, bf16[256,2048]{1,0:T(8,128)(2,1)S(1)} %copy-done.8), custom_call_target="tpu_custom_call" | custom-call | flops 671088640 | bytes 4194304 | tf_op jit(solution)/shard_map/psg_back/pallas_call | solution.py:74
  114.9 74.5 %reduce-scatter.4.cloned.1.call-done = bf16[256,512]{1,0:T(8,128)(2,1)} async-done(((bf16[8192,512]{1,0:T(8,128)(2,1)}), bf16[256,512]{1,0:T(8,128)(2,1)}) %reduce-scatter.4.cloned.1.call-update) | async-done | bytes 262160 | tf_op jit(solution)/shard_map/reduce_scatter | solution.py:321
  189.4 1.0 add_convert_fusion
  190.4 0.0 copy-start.2
  190.4 2.2 copy-done.2
  192.6 2.2 copy-done.4
  194.8 4.0 %term.2 = bf16[256,8192]{1,0:T(8,128)(2,1)S(1)} custom-call(bf16[256,256]{1,0:T(8,128)(2,1)S(1)} %get-tuple-element.19.k_ref, bf16[256,256]{1,0:T(8,128)(2,1)S(1)} %get-tuple-element.18.v_ref, bf16[8192,256]{1,0:T(8,128)(2,1)S(1)} %copy-done.2, bf16[8192,256]{1,0:T(8,128)(2,1)S(1)} %copy-done.4), custom_call_target="tpu_custom_call" | custom-call | flops 2147483648 | bytes 12582912 | tf_op jit(solution)/shard_map/term/pallas_call | solution.py:296
  198.8 1.9 copy-done
  200.7 0.0 reduce-scatter.6.cloned.1.call-update
  200.8 22.4 %reduce-scatter.8.cloned.1.call-done = bf16[32,8192]{1,0:T(8,128)(2,1)} async-done(((bf16[128,8192]{1,0:T(8,128)(2,1)}), bf16[32,8192]{1,0:T(8,128)(2,1)}) %reduce-scatter.8.cloned.1.call-update) | async-done | bytes 524304 | tf_op jit(solution)/shard_map/reduce_scatter | solution.py:322
  223.2 49.4 %reduce-scatter.6.cloned.1.call-done = bf16[64,8192]{1,0:T(8,128)(2,1)} async-done(((bf16[256,8192]{1,0:T(8,128)(2,1)}), bf16[64,8192]{1,0:T(8,128)(2,1)}) %reduce-scatter.6.cloned.1.call-update) | async-done | bytes 1048592 | tf_op jit(solution)/shard_map/reduce_scatter | solution.py:326
  (17 shorter events, 0.0 us)
Async XLA Ops:
  7.2 60.4 %all-gather.2.cloned.1.call-start = ((), (), s32[]{:S(2)}) async-start(), calls=%async_computation.3 | async-start | bytes 8650752 | tf_op jit(solution)/shard_map/all_gather | solution.py:316
  8.9 180.5 %reduce-scatter.4.cloned.1.call-start = ((), (), s32[]{:S(2)}) async-start(), calls=%async_computation.4 | async-start | bytes 8650752 | tf_op jit(solution)/shard_map/reduce_scatter | solution.py:321
  67.5 1.0 copy-start.9
  68.6 1.0 copy-start.10
  69.6 0.8 copy-start.11
  70.5 0.8 copy-start.12
  71.3 0.7 copy-start.13
  72.0 0.7 copy-start.14
  99.1 124.1 %reduce-scatter.8.cloned.1.call-start = ((), (), s32[]{:S(2)}) async-start(), calls=%async_computation.6 | async-start | bytes 2621440 | tf_op jit(solution)/shard_map/reduce_scatter | solution.py:322
  99.1 2.2 copy-start.1
  101.3 2.2 copy-start.3
  103.5 5.4 %copy-start.5 = (bf16[256,256]{1,0:T(8,128)(2,1)S(1)}, bf16[256,256]{1,0:T(8,128)(2,1)}, u32[]{:S(2)}) copy-start(bf16[256,256]{1,0:T(8,128)(2,1)} %k_ref.1) | copy-start | bytes 393220
  103.5 5.4 %copy-start.6 = (bf16[256,256]{1,0:T(8,128)(2,1)S(1)}, bf16[256,256]{1,0:T(8,128)(2,1)}, u32[]{:S(2)}) copy-start(bf16[256,256]{1,0:T(8,128)(2,1)} %v_ref.1) | copy-start | bytes 393220
  103.5 5.4 %copy-start.7 = (bf16[256,2048]{1,0:T(8,128)(2,1)S(1)}, bf16[256,2048]{1,0:T(8,128)(2,1)}, u32[]{:S(2)}) copy-start(bf16[256,2048]{1,0:T(8,128)(2,1)} %q_ref.2) | copy-start | bytes 3145732
  103.5 5.4 %copy-start.8 = (bf16[256,2048]{1,0:T(8,128)(2,1)S(1)}, bf16[256,2048]{1,0:T(8,128)(2,1)}, u32[]{:S(2)}) copy-start(bf16[256,2048]{1,0:T(8,128)(2,1)} %do_ref.2) | copy-start | bytes 3145732
  108.8 163.7 %reduce-scatter.6.cloned.1.call-start = ((), (), s32[]{:S(2)}) async-start(), calls=%async_computation.5 | async-start | bytes 5242880 | tf_op jit(solution)/shard_map/reduce_scatter | solution.py:326
  190.4 2.2 copy-start.2
  192.6 2.2 copy-start.4
  198.8 1.9 copy-start
Sparse Core Ops, SparseCore 0:
  10.8 56.6 all-gather.1
  99.2 90.1 reduce-scatter.3
  192.5 30.6 reduce-scatter.7
  226.0 46.5 reduce-scatter.5

commit v2 on v1

--- a/solution.py
+++ b/solution.py
@@ -91,6 +91,14 @@
 NT = P_REQ * PLEN // TK
 
 
+def spot(slot):
+    n = slot % 2
+    c = slot // 2 % 2
+    x = slot // 4 % 4
+    z = slot // 16
+    return jnp.where(n == 0, c * 16 + z * 4 + x, 32 + c * 16 + x * 4 + z)
+
+
 def qry_kernel(
     req_ref, slot_ref, owner_ref, kvg_ref, q_ref, do_ref, kq_ref, vq_ref, me_ref,
     dq_ref, gk_ref, gv_ref, full_ref,
@@ -114,7 +122,7 @@
         lax.fori_loop(0, NPSG, clear, 0)
 
         def pick(j, c):
-            slot = slot_ref[req_ref[request, j]]
+            slot = spot(slot_ref[req_ref[request, j]])
             slots[j] = slot
             mask[slot] = 1
             return c
@@ -130,13 +138,12 @@
 
         lax.fori_loop(0, NPSG, blank, 0)
 
-    kcols = pl.ds(pl.multiple_of(h * D, D), D)
-    vcols = pl.ds(pl.multiple_of(KV * D + h * D, D), D)
+    cols = pl.ds(pl.multiple_of(h * D, D), D)
     copies = []
     for j in range(P_REQ):
         rows = pl.ds(j * PLEN, PLEN)
-        copies.append(pltpu.make_async_copy(kvg_ref.at[slots[j], :, kcols], kbuf.at[rows], in_sem.at[0]))
-        copies.append(pltpu.make_async_copy(kvg_ref.at[slots[j], :, vcols], vbuf.at[rows], in_sem.at[1]))
+        copies.append(pltpu.make_async_copy(kvg_ref.at[slots[j], 0, :, cols], kbuf.at[rows], in_sem.at[0]))
+        copies.append(pltpu.make_async_copy(kvg_ref.at[slots[j], 1, :, cols], vbuf.at[rows], in_sem.at[1]))
     for copy in copies:
         copy.start()
     qs[...] = stack(q_ref[...])
@@ -211,8 +218,8 @@
             j = t * (TK // PLEN) + i
             part = pl.ds(pl.multiple_of(j * PLEN, PLEN), PLEN)
             slot = slots[j]
-            pltpu.make_async_copy(gkbuf.at[part], full_ref.at[slot, :, kcols], out_sem.at[0]).start()
-            pltpu.make_async_copy(gvbuf.at[part], full_ref.at[slot, :, vcols], out_sem.at[1]).start()
+            pltpu.make_async_copy(gkbuf.at[part], full_ref.at[slot, 0, :, cols], out_sem.at[0]).start()
+            pltpu.make_async_copy(gvbuf.at[part], full_ref.at[slot, 1, :, cols], out_sem.at[1]).start()
         return c
 
     lax.fori_loop(0, NT, back, 0)
@@ -221,8 +228,8 @@
 
     def drain(j, c):
         rows = pl.ds(pl.multiple_of(j * PLEN, PLEN), PLEN)
-        pltpu.make_async_copy(gkbuf.at[rows], full_ref.at[slots[j], :, kcols], out_sem.at[0]).wait()
-        pltpu.make_async_copy(gvbuf.at[rows], full_ref.at[slots[j], :, vcols], out_sem.at[1]).wait()
+        pltpu.make_async_copy(gkbuf.at[rows], full_ref.at[slots[j], 0, :, cols], out_sem.at[0]).wait()
+        pltpu.make_async_copy(gvbuf.at[rows], full_ref.at[slots[j], 1, :, cols], out_sem.at[1]).wait()
         return c
 
     lax.fori_loop(0, P_REQ, drain, 0)
@@ -254,7 +261,7 @@
             jax.ShapeDtypeStruct(q.shape, BF16),
             jax.ShapeDtypeStruct(kq.shape, BF16),
             jax.ShapeDtypeStruct(vq.shape, BF16),
-            jax.ShapeDtypeStruct((NPSG, PLEN, 2 * KV * D), BF16),
+            jax.ShapeDtypeStruct((NPSG, 2, PLEN, KV * D), BF16),
         ],
         scratch_shapes=[
             pltpu.VMEM((G * PLEN, D), BF16),
@@ -270,7 +277,7 @@
             pltpu.VMEM((D, G * PLEN), F32),
             pltpu.VMEM((P_REQ * PLEN, D), BF16),
             pltpu.VMEM((P_REQ * PLEN, D), BF16),
-            pltpu.VMEM((PLEN, 2 * KV * D), BF16),
+            pltpu.VMEM((2, PLEN, KV * D), BF16),
             pltpu.SMEM((P_REQ,), jnp.int32),
             pltpu.SMEM((NPSG,), jnp.int32),
             pltpu.SemaphoreType.DMA((2,)),
@@ -310,19 +317,309 @@
     )(rows_k, rows_v, w_key, w_value)
 
 
+MESH = pl.DeviceIdType.MESH
+
+
+def place():
+    me = lax.axis_index("psg")
+    return me // 8, lax.rem(me // 2, 4), lax.rem(me, 2)
+
+
+def at_plane(z, x, c):
+    return {"psg": (z * 4 + x) * 2 + c}
+
+
+def turn(i, by):
+    return lax.rem(i + by + 4, 4)
+
+
+def greet(devices):
+    barrier = pltpu.get_barrier_semaphore()
+    for device in devices:
+        pl.semaphore_signal(barrier, inc=1, device_id=device, device_id_type=MESH)
+    pl.semaphore_wait(barrier, len(devices))
+
+
+def plane_neighbours(z, x, c):
+    return [
+        at_plane(turn(z, 1), x, c),
+        at_plane(turn(z, -1), x, c),
+        at_plane(z, turn(x, 1), c),
+        at_plane(z, turn(x, -1), c),
+        at_plane(z, x, 1 - c),
+    ]
+
+
+class Sender:
+    def __init__(self, sems):
+        self.sems = sems
+        self.started = []
+
+    def __call__(self, src, dst, recv_sem, device):
+        copy = pltpu.make_async_remote_copy(
+            src_ref=src, dst_ref=dst, send_sem=self.sems.at[len(self.started)], recv_sem=recv_sem,
+            device_id=device, device_id_type=MESH,
+        )
+        copy.start()
+        self.started.append(copy)
+
+    def finish(self):
+        for copy in self.started:
+            copy.wait_send()
+
+
+def arrived(ref, sem):
+    pltpu.make_async_copy(ref, ref, sem).wait()
+
+
+def gather_kernel(k_ref, v_ref, all_ref, send_sem, recv_sem, core_sem, local_sem):
+    z, x, c = place()
+    greet(plane_neighbours(z, x, c))
+    send = Sender(send_sem)
+    half = k_ref.shape[0] // 2
+    own = [(z, x), (x, z)]
+    copies = []
+    for n in range(2):
+        a, b = own[n]
+        for part, ref in enumerate((k_ref, v_ref)):
+            copies.append(pltpu.make_async_copy(ref.at[pl.ds(n * half, half)], all_ref.at[n, c, a, b, part], local_sem.at[n, part]))
+    for copy in copies:
+        copy.start()
+    for copy in copies:
+        copy.wait()
+
+    def device(n, a, b, core):
+        return at_plane(a, b, core) if n == 0 else at_plane(b, a, core)
+
+    def whole(n, a, b, to):
+        block = all_ref.at[n, c, a, b]
+        send(block, block, recv_sem.at[0, n, a, b], to)
+
+    def piece(n, a, b, part, to):
+        block = all_ref.at[n, c, a, b, part]
+        send(block, block, recv_sem.at[part, n, a, b], to)
+
+    def core(n, a, b):
+        block = all_ref.at[n, c, a, b]
+        send(block, block, core_sem.at[n, a, b], device(n, own[n][0], own[n][1], 1 - c))
+
+    def wait_whole(n, a, b):
+        arrived(all_ref.at[n, c, a, b], recv_sem.at[0, n, a, b])
+
+    def wait_pieces(n, a, b):
+        for part in range(2):
+            arrived(all_ref.at[n, c, a, b, part], recv_sem.at[part, n, a, b])
+
+    def along_a(n, a, b):
+        for by in (1, -1):
+            whole(n, a, b, device(n, turn(a, by), own[n][1], c))
+
+    for n in range(2):
+        a, b = own[n]
+        for by in (1, -1):
+            whole(n, a, b, device(n, a, turn(b, by), c))
+        along_a(n, a, b)
+    for n in range(2):
+        core(n, *own[n])
+    for by, part in ((-1, 0), (1, 1)):
+        for n in range(2):
+            a, b = own[n]
+            o = turn(b, by)
+            wait_whole(n, a, o)
+            piece(n, a, o, part, device(n, a, turn(b, -by), c))
+            along_a(n, a, o)
+            core(n, a, o)
+    def far(n, bo):
+        a, b = own[n]
+        col = turn(b, bo)
+        for by, part in ((-1, 0), (1, 1)):
+            o = turn(a, by)
+            wait_whole(n, o, col)
+            piece(n, o, col, part, device(n, turn(a, -by), b, c))
+            core(n, o, col)
+
+    for n in range(2):
+        far(n, 0)
+    for n in range(2):
+        a, b = own[n]
+        o = turn(b, 2)
+        wait_pieces(n, a, o)
+        along_a(n, a, o)
+        core(n, a, o)
+    for bo in (-1, 1, 2):
+        for n in range(2):
+            far(n, bo)
+    for bo in (0, -1, 1, 2):
+        for n in range(2):
+            a, b = own[n]
+            o, col = turn(a, 2), turn(b, bo)
+            wait_pieces(n, o, col)
+            core(n, o, col)
+    for n in range(2):
+        for a in range(4):
+            for b in range(4):
+                arrived(all_ref.at[n, 1 - c, a, b], core_sem.at[n, a, b])
+    send.finish()
+
+
+def gather_plane(k, v):
+    rows, cols = k.shape
+    hbm = pl.BlockSpec(memory_space=pl.ANY)
+    return pl.pallas_call(
+        gather_kernel,
+        in_specs=[hbm, hbm],
+        out_specs=hbm,
+        out_shape=jax.ShapeDtypeStruct((2, 2, 4, 4, 2, rows // 2, cols), BF16),
+        scratch_shapes=[
+            pltpu.SemaphoreType.DMA((72,)),
+            pltpu.SemaphoreType.DMA((2, 2, 4, 4)),
+            pltpu.SemaphoreType.DMA((2, 4, 4)),
+            pltpu.SemaphoreType.DMA((2, 2)),
+        ],
+        compiler_params=pltpu.CompilerParams(collective_id=0, has_side_effects=True),
+        name="gather_plane",
+    )(k, v)
+
+
+def add(x, y):
+    return (x.astype(F32) + y.astype(F32)).astype(BF16)
+
+
+def reduce_kernel(
+    full_ref, own_k_ref, own_v_ref, gk_ref, gv_ref,
+    mine, other, relay1, side1, part, relay2, side2,
+    send_sem, core_sem, relay1_sem, side1_sem, relay2_sem, side2_sem, local_sem,
+):
+    z, x, c = place()
+    own = [(z, x), (x, z)]
+
+    def device(n, a, b, core):
+        return at_plane(a, b, core) if n == 0 else at_plane(b, a, core)
+
+    loads = {}
+    for by in (2, 1, -1, 0):
+        for n in range(2):
+            a = turn(own[n][0], by)
+            loads[n, by] = pltpu.make_async_copy(full_ref.at[n, c, a], mine.at[n, a], local_sem.at[n, a])
+            loads[n, by].start()
+    greet(plane_neighbours(z, x, c))
+    send = Sender(send_sem)
+    for by in (2, 1, -1, 0):
+        for n in range(2):
+            a = turn(own[n][0], by)
+            send(full_ref.at[n, 1 - c, a], other.at[n, a], core_sem.at[n, a], device(n, *own[n], 1 - c))
+
+    def pair(n, by):
+        a = turn(own[n][0], by)
+        loads[n, by].wait()
+        arrived(other.at[n, a], core_sem.at[n, a])
+        mine[n, a] = add(mine[n, a], other[n, a])
+        return a
+
+    halves = (pl.ds(0, 2), pl.ds(2, 2))
+    steps = (1, -1)
+    for n in range(2):
+        a = pair(n, 2)
+        for s in range(2):
+            to = device(n, turn(own[n][0], steps[s]), own[n][1], c)
+            send(mine.at[n, a, halves[s]], relay1.at[n, s], relay1_sem.at[n, s], to)
+    for s in range(2):
+        for n in range(2):
+            a = pair(n, steps[s])
+            to = device(n, a, own[n][1], c)
+            send(mine.at[n, a, halves[1 - s]], side1.at[n, s, halves[1 - s]], side1_sem.at[n, s, 1 - s], to)
+    for s in range(2):
+        for n in range(2):
+            a = turn(own[n][0], steps[s])
+            to = device(n, a, own[n][1], c)
+            arrived(relay1.at[n, s], relay1_sem.at[n, s])
+            mine[n, a, halves[s]] = add(mine[n, a, halves[s]], relay1[n, s])
+            send(mine.at[n, a, halves[s]], side1.at[n, s, halves[s]], side1_sem.at[n, s, s], to)
+    for n in range(2):
+        pair(n, 0)
+
+    def join1(n, b):
+        a = own[n][0]
+        total = mine[n, a, b].astype(F32)
+        for s in range(2):
+            total = total + side1[n, s, b].astype(F32)
+        part[n, b] = total.astype(BF16)
+
+    for n in range(2):
+        a, b = own[n]
+        for s in range(2):
+            for t in range(2):
+                arrived(side1.at[n, s, halves[t]], side1_sem.at[n, s, t])
+        far = turn(b, 2)
+        join1(n, far)
+        for s in range(2):
+            send(part.at[n, far, s], relay2.at[n, s], relay2_sem.at[n, s], device(n, a, turn(b, steps[s]), c))
+        for s in range(2):
+            near = turn(b, steps[s])
+            join1(n, near)
+            send(part.at[n, near, 1 - s], side2.at[n, s, 1 - s], side2_sem.at[n, s, 1 - s], device(n, a, near, c))
+        join1(n, b)
+    for n in range(2):
+        a, b = own[n]
+        for s in range(2):
+            near = turn(b, steps[s])
+            arrived(relay2.at[n, s], relay2_sem.at[n, s])
+            part[n, near, s] = add(part[n, near, s], relay2[n, s])
+            send(part.at[n, near, s], side2.at[n, s, s], side2_sem.at[n, s, s], device(n, a, near, c))
+    half = own_k_ref.shape[0] // 2
+    for n in range(2):
+        rows = slice(n * half, (n + 1) * half)
+        for t, (own_ref, out_ref) in enumerate(((own_k_ref, gk_ref), (own_v_ref, gv_ref))):
+            total = own_ref[rows, :] + part[n, own[n][1], t].astype(F32)
+            for s in range(2):
+                arrived(side2.at[n, s, t], side2_sem.at[n, s, t])
+                total = total + side2[n, s, t].astype(F32)
+            out_ref[rows, :] = total.astype(BF16)
+    send.finish()
+
+
+def reduce_plane(full, own_k, own_v):
+    rows, cols = own_k.shape
+    half = rows // 2
+    hbm = pl.BlockSpec(memory_space=pl.ANY)
+    vmem = pl.BlockSpec(memory_space=pltpu.VMEM)
+    dma = pltpu.SemaphoreType.DMA
+    block = (2, half, cols)
+    return pl.pallas_call(
+        reduce_kernel,
+        in_specs=[hbm, vmem, vmem],
+        out_specs=[vmem, vmem],
+        out_shape=[jax.ShapeDtypeStruct((rows, cols), BF16)] * 2,
+        scratch_shapes=[
+            pltpu.VMEM((2, 4, 4) + block, BF16),
+            pltpu.VMEM((2, 4, 4) + block, BF16),
+            pltpu.VMEM((2, 2, 2) + block, BF16),
+            pltpu.VMEM((2, 2, 4) + block, BF16),
+            pltpu.VMEM((2, 4) + block, BF16),
+            pltpu.VMEM((2, 2, half, cols), BF16),
+            pltpu.VMEM((2, 2) + block, BF16),
+            dma((32,)),
+            dma((2, 4)),
+            dma((2, 2)),
+            dma((2, 2, 2)),
+            dma((2, 2)),
+            dma((2, 2, 2)),
+            dma((2, 4)),
+        ],
+        compiler_params=pltpu.CompilerParams(collective_id=1, has_side_effects=True, vmem_limit_bytes=40 * 1024 * 1024),
+        name="reduce_plane",
+    )(full, own_k, own_v)
+
+
 def local(q_psg, k_psg, v_psg, do_psg, q_qry, k_qry, v_qry, do_qry, w_key, w_value, req_passages, passage_slot, query_owner):
     me = lax.axis_index("psg").astype(jnp.int32).reshape(1)
-    kv = jnp.concatenate([k_psg, v_psg], axis=1)
-    every = lax.all_gather(kv, "psg", axis=0, tiled=True)
+    every = gather_plane(k_psg, v_psg)
     dq_psg, own_k, own_v = psg_back(q_psg, k_psg, v_psg, do_psg)
     dq_qry, gk_qry, gv_qry, full = qry_back(
-        req_passages, passage_slot, query_owner, every.reshape(NPSG, PLEN, -1), q_qry, do_qry, k_qry, v_qry, me
+        req_passages, passage_slot, query_owner, every.reshape(NPSG, 2, PLEN, -1), q_qry, do_qry, k_qry, v_qry, me
     )
-    summed = lax.psum_scatter(full.reshape(NPSG * PLEN, -1), "psg", scatter_dimension=0, tiled=True)
     dx_qry = lax.psum_scatter(term(gk_qry, gv_qry, w_key, w_value), "head", scatter_dimension=0, tiled=True)
-    cols = KV * D
-    gk = (own_k + summed[:, :cols].astype(F32)).astype(BF16)
-    gv = (own_v + summed[:, cols:].astype(F32)).astype(BF16)
+    gk, gv = reduce_plane(full.reshape(every.shape), own_k, own_v)
     dx_psg = lax.psum_scatter(term(gk, gv, w_key, w_value), "head", scatter_dimension=0, tiled=True)
     return dq_psg, dq_qry, dx_psg, dx_qry
 

time: 280 us -> 188 us (0.67)
  waiting for transfers between devices: 204 us -> 47.9 us
  Pallas kernels: 41.7 us -> 118 us
  local copies, waits for them, and re-layouts: 16.5 us -> 6.57 us
    pallas_call x0 -> x2, Pallas kernels: none -> 75.3 us  [the longest x1 44.2 us: gather_plane(): pl.pallas_call(gather_kernel, in_specs=[hbm, hbm], out_specs=hbm, out_sha...]
    reduce_scatter x1 -> x0, waiting for transfers between devices: 74.5 us -> none  [local(): lax.psum_scatter(full.reshape(NPSG * PLEN, -1), 'psg', scatter_dimension=...]
    all_gather x1 -> x0, waiting for transfers between devices: 57.8 us -> none  [local(): every = lax.all_gather(kv, 'psg', axis=0, tiled=True)]
    reduce_scatter x1, waiting for transfers between devices: 22.4 us -> 0.02 us  [local(): lax.psum_scatter(term(gk_qry, gv_qry, w_key, w_value), 'head', scatter_di...]
    unnamed x31 -> x33, local copies, waits for them, and re-layouts: 16.5 us -> 6.57 us
  transfers between devices with their start and end apart: 4 -> 2, of which waited for: 4 -> 1; matrix products, arithmetic and copies ran while one was open for 1% -> 0% of each run, Pallas kernels for 5% -> 22%
where the time goes in v2:
time: 188 us; the launch traced here: 187 us
  Pallas kernels  118 us (63%)
  waiting for transfers between devices  47.9 us (25%)
  between operations  14.3 us (8%)
  local copies, waits for them, and re-layouts  6.57 us (3%)
    reduce_scatter x1, waiting for transfers between devices, local(): lax.psum_scatter(term(gk, gv, w_key, w_value), 'head', scatter_dimension=...  47.9 us
    pallas_call x1, Pallas kernels, gather_plane(): pl.pallas_call(gather_kernel, in_specs=[hbm, hbm], out_specs=hbm, out_sha...  44.2 us
    pallas_call x1, Pallas kernels, reduce_plane(): pl.pallas_call(reduce_kernel, in_specs=[hbm, vmem, vmem], out_specs=[vmem...  31.1 us
    pallas_call x1, Pallas kernels, qry_back(): pl.pallas_call(qry_kernel, grid=(KV,), in_specs=[smem, smem, smem, hbm, w...  27.8 us
    pallas_call x2, Pallas kernels, term(): pl.pallas_call(term_kernel, grid=(width // WB,), in_specs=[pl.BlockSpec((...  9.32 us
    unnamed x33, local copies, waits for them, and re-layouts  6.57 us
    pallas_call x1, Pallas kernels, psg_back(): pl.pallas_call(psg_kernel, grid=(rows // PLEN, KV), in_specs=[wide, thin,...  6 us
  transfers between devices with their start and end apart: 2, of which 1 were waited for; matrix products, arithmetic and copies ran while one was open for 0% of the time, Pallas kernels for 22%

profile of v2, /device:TPU:1, one launch (start us, length us, event | category | flops | bytes accessed | tf_op | source)
XLA Modules:
  0.0 187.3 jit_solution(15680446726243009036)
XLA Ops:
  7.2 0.0 reduce-scatter.5.cloned.1.call-start
  7.2 0.8 copy.17.req_ref
  8.0 0.0 copy-start.13
  8.0 0.0 copy-start.14
  8.0 0.0 copy-start.15
  8.0 44.2 %gather_plane.1 = bf16[2,2,4,4,2,128,256]{6,5,4,3,2,1,0:T(8,128)(2,1)} custom-call(bf16[256,256]{1,0:T(8,128)(2,1)} %k_ref.3, bf16[256,256]{1,0:T(8,128)(2,1)} %v_ref.3), custom_call_target="tpu_custom_call" | custom-call | tf_op jit(solution)/shard_map/gather_plane/pallas_call | solution.py:468
  52.3 0.0 copy-done.10
  52.3 0.0 copy-done.11
  52.3 0.0 copy-done.12
  52.3 0.0 copy-done.13
  52.3 0.0 copy-done.14
  52.3 0.0 copy-done.15
  52.3 0.0 copy-start.1
  52.3 0.0 copy-start.3
  52.4 27.8 %qry_back.1 = (bf16[128,2048]{1,0:T(8,128)(2,1)}, bf16[128,256]{1,0:T(8,128)(2,1)S(1)}, bf16[128,256]{1,0:T(8,128)(2,1)S(1)}, bf16[64,2,128,256]{3,2,1,0:T(8,128)(2,1)}) custom-call(s32[32,16]{1,0:T(8,128)S(1)} %copy.17.req_ref, s32[64]{0:T(128)S(1)} %copy-done.14, s32[32]{0:T(128)S(1)} %copy-done.15, bf16[64,2,128,256]{3,2,1,0:T(8,128)(2,1)} %bitcast.4, ...), custom_call_target="tpu_custom_call" | custom-call | flops 5704253440 | bytes 16777216 | tf_op jit(solution)/shard_map/qry_back/pallas_call | solution.py:255
  80.2 0.0 copy-done.1
  80.2 0.0 copy-start.6
  80.2 0.0 copy-start.7
  80.2 0.0 copy-start.8
  80.2 0.0 copy-start.9
  80.2 5.3 %term.3 = bf16[128,8192]{1,0:T(8,128)(2,1)} custom-call(bf16[128,256]{1,0:T(8,128)(2,1)S(1)} %get-tuple-element.20.k_ref, bf16[128,256]{1,0:T(8,128)(2,1)S(1)} %get-tuple-element.21.v_ref, bf16[8192,256]{1,0:T(8,128)(2,1)S(1)} %copy-done.1, bf16[8192,256]{1,0:T(8,128)(2,1)S(1)} %copy-done.3), custom_call_target="tpu_custom_call" | custom-call | flops 1073741824 | bytes 10485760 | tf_op jit(solution)/shard_map/term/pallas_call | solution.py:303
  85.6 0.0 reduce-scatter.5.cloned.1.call-update
  85.6 0.0 reduce-scatter.3.cloned.1.call-start
  85.7 6.0 %psg_back.1 = (bf16[256,2048]{1,0:T(8,128)(2,1)}, f32[256,256]{1,0:T(8,128)S(1)}, f32[256,256]{1,0:T(8,128)S(1)}) custom-call(bf16[256,2048]{1,0:T(8,128)(2,1)S(1)} %copy-done.8, bf16[256,256]{1,0:T(8,128)(2,1)S(1)} %copy-done.6, bf16[256,256]{1,0:T(8,128)(2,1)S(1)} %copy-done.7, bf16[256,2048]{1,0:T(8,128)(2,1)S(1)} %copy-done.9), custom_call_target="tpu_custom_call" | custom-call | flops 671088640 | bytes 4194304 | tf_op jit(solution)/shard_map/psg_back/pallas_call | solution.py:74
  91.7 3.8 %copy-done.5 = bf16[64,2,128,256]{3,2,1,0:T(8,128)(2,1)S(1)} copy-done((bf16[64,2,128,256]{3,2,1,0:T(8,128)(2,1)S(1)}, bf16[64,2,128,256]{3,2,1,0:T(8,128)(2,1)}, u32[]{:S(2)}) %copy-start.5) | copy-done | bytes 8388632
  95.5 31.1 %reduce_plane.1 = (bf16[256,256]{1,0:T(8,128)(2,1)S(1)}, bf16[256,256]{1,0:T(8,128)(2,1)S(1)}) custom-call(bf16[2,2,4,4,2,128,256]{6,5,4,3,2,1,0:T(8,128)(2,1)S(1)} %bitcast.3, f32[256,256]{1,0:T(8,128)S(1)} %get-tuple-element.16.own_k_ref, f32[256,256]{1,0:T(8,128)S(1)} %get-tuple-element.17.own_v_ref), custom_call_target="tpu_custom_call" | custom-call | tf_op jit(solution)/shard_map/reduce_plane/pallas_call | solution.py:588
  126.6 4.0 %term.2 = bf16[256,8192]{1,0:T(8,128)(2,1)S(1)} custom-call(bf16[256,256]{1,0:T(8,128)(2,1)S(1)} %get-tuple-element.18.k_ref, bf16[256,256]{1,0:T(8,128)(2,1)S(1)} %get-tuple-element.19.v_ref, bf16[8192,256]{1,0:T(8,128)(2,1)S(1)} %copy-done.2, bf16[8192,256]{1,0:T(8,128)(2,1)S(1)} %copy-done.4), custom_call_target="tpu_custom_call" | custom-call | flops 2147483648 | bytes 12582912 | tf_op jit(solution)/shard_map/term/pallas_call | solution.py:303
  130.6 0.0 copy-start
  130.6 1.9 %copy-done = bf16[256,8192]{1,0:T(8,128)(2,1)} copy-done((bf16[256,8192]{1,0:T(8,128)(2,1)}, bf16[256,8192]{1,0:T(8,128)(2,1)S(1)}, u32[]{:S(2)}) %copy-start) | copy-done | bytes 4194328
  132.5 0.0 reduce-scatter.3.cloned.1.call-update
  132.5 0.0 reduce-scatter.5.cloned.1.call-done
  132.6 47.9 %reduce-scatter.3.cloned.1.call-done = bf16[64,8192]{1,0:T(8,128)(2,1)} async-done(((bf16[256,8192]{1,0:T(8,128)(2,1)}), bf16[64,8192]{1,0:T(8,128)(2,1)}) %reduce-scatter.3.cloned.1.call-update) | async-done | bytes 1048592 | tf_op jit(solution)/shard_map/reduce_scatter | solution.py:623
  (13 shorter events, 0.0 us)
Async XLA Ops:
  7.2 125.4 %reduce-scatter.5.cloned.1.call-start = ((), (), s32[]{:S(2)}) async-start(), calls=%async_computation.3 | async-start | bytes 2621440 | tf_op jit(solution)/shard_map/reduce_scatter | solution.py:621
  8.0 44.3 %copy-start.10 = (bf16[128,2048]{1,0:T(8,128)(2,1)S(1)}, bf16[128,2048]{1,0:T(8,128)(2,1)}, u32[]{:S(2)}) copy-start(bf16[128,2048]{1,0:T(8,128)(2,1)} %q_ref.3) | copy-start | bytes 1572868
  8.0 44.3 %copy-start.11 = (bf16[128,2048]{1,0:T(8,128)(2,1)S(1)}, bf16[128,2048]{1,0:T(8,128)(2,1)}, u32[]{:S(2)}) copy-start(bf16[128,2048]{1,0:T(8,128)(2,1)} %do_ref.3) | copy-start | bytes 1572868
  8.0 44.3 %copy-start.12 = (bf16[128,256]{1,0:T(8,128)(2,1)S(1)}, bf16[128,256]{1,0:T(8,128)(2,1)}, u32[]{:S(2)}) copy-start(bf16[128,256]{1,0:T(8,128)(2,1)} %kq_ref.1) | copy-start | bytes 196612
  8.0 44.3 %copy-start.13 = (bf16[128,256]{1,0:T(8,128)(2,1)S(1)}, bf16[128,256]{1,0:T(8,128)(2,1)}, u32[]{:S(2)}) copy-start(bf16[128,256]{1,0:T(8,128)(2,1)} %vq_ref.1) | copy-start | bytes 196612
  8.0 44.3 %copy-start.14 = (s32[64]{0:T(128)S(1)}, s32[64]{0:T(128)}, u32[]{:S(2)}) copy-start(s32[64]{0:T(128)} %slot_ref.1) | copy-start | bytes 772
  8.0 44.3 %copy-start.15 = (s32[32]{0:T(128)S(1)}, s32[32]{0:T(128)}, u32[]{:S(2)}) copy-start(s32[32]{0:T(128)} %owner_ref.1) | copy-start | bytes 388
  52.3 27.9 %copy-start.1 = (bf16[8192,256]{1,0:T(8,128)(2,1)S(1)}, bf16[8192,256]{1,0:T(8,128)(2,1)}, u32[]{:S(2)}) copy-start(bf16[8192,256]{1,0:T(8,128)(2,1)} %wk_ref.3) | copy-start | bytes 12582916
  52.3 27.9 %copy-start.3 = (bf16[8192,256]{1,0:T(8,128)(2,1)S(1)}, bf16[8192,256]{1,0:T(8,128)(2,1)}, u32[]{:S(2)}) copy-start(bf16[8192,256]{1,0:T(8,128)(2,1)} %wv_ref.3) | copy-start | bytes 12582916
  80.2 5.4 %copy-start.6 = (bf16[256,256]{1,0:T(8,128)(2,1)S(1)}, bf16[256,256]{1,0:T(8,128)(2,1)}, u32[]{:S(2)}) copy-start(bf16[256,256]{1,0:T(8,128)(2,1)} %k_ref.3) | copy-start | bytes 393220
  80.2 5.4 %copy-start.7 = (bf16[256,256]{1,0:T(8,128)(2,1)S(1)}, bf16[256,256]{1,0:T(8,128)(2,1)}, u32[]{:S(2)}) copy-start(bf16[256,256]{1,0:T(8,128)(2,1)} %v_ref.3) | copy-start | bytes 393220
  80.2 5.4 %copy-start.8 = (bf16[256,2048]{1,0:T(8,128)(2,1)S(1)}, bf16[256,2048]{1,0:T(8,128)(2,1)}, u32[]{:S(2)}) copy-start(bf16[256,2048]{1,0:T(8,128)(2,1)} %q_ref.2) | copy-start | bytes 3145732
  80.2 5.4 %copy-start.9 = (bf16[256,2048]{1,0:T(8,128)(2,1)S(1)}, bf16[256,2048]{1,0:T(8,128)(2,1)}, u32[]{:S(2)}) copy-start(bf16[256,2048]{1,0:T(8,128)(2,1)} %do_ref.2) | copy-start | bytes 3145732
  85.6 94.9 %reduce-scatter.3.cloned.1.call-start = ((), (), s32[]{:S(2)}) async-start(), calls=%async_computation.2 | async-start | bytes 5242880 | tf_op jit(solution)/shard_map/reduce_scatter | solution.py:623
  91.7 3.8 %copy-start.5 = (bf16[64,2,128,256]{3,2,1,0:T(8,128)(2,1)S(1)}, bf16[64,2,128,256]{3,2,1,0:T(8,128)(2,1)}, u32[]{:S(2)}) copy-start(bf16[64,2,128,256]{3,2,1,0:T(8,128)(2,1)} %get-tuple-element.15) | copy-start | bytes 25165828
  95.5 31.1 %copy-start.2 = (bf16[8192,256]{1,0:T(8,128)(2,1)S(1)}, bf16[8192,256]{1,0:T(8,128)(2,1)}, u32[]{:S(2)}) copy-start(bf16[8192,256]{1,0:T(8,128)(2,1)} %wk_ref.3) | copy-start | bytes 12582916
  95.5 31.1 %copy-start.4 = (bf16[8192,256]{1,0:T(8,128)(2,1)S(1)}, bf16[8192,256]{1,0:T(8,128)(2,1)}, u32[]{:S(2)}) copy-start(bf16[8192,256]{1,0:T(8,128)(2,1)} %wv_ref.3) | copy-start | bytes 12582916
  130.6 2.0 %copy-start = (bf16[256,8192]{1,0:T(8,128)(2,1)}, bf16[256,8192]{1,0:T(8,128)(2,1)S(1)}, u32[]{:S(2)}) copy-start(bf16[256,8192]{1,0:T(8,128)(2,1)S(1)} %term.2) | copy-start | bytes 12582916
Sparse Core Ops, SparseCore 0:
  85.7 28.8 reduce-scatter.4
  132.7 47.7 reduce-scatter.2

commit v3 on v1

--- a/solution.py
+++ b/solution.py
@@ -91,6 +91,14 @@
 NT = P_REQ * PLEN // TK
 
 
+def spot(slot):
+    n = slot % 2
+    c = slot // 2 % 2
+    x = slot // 4 % 4
+    z = slot // 16
+    return n * 32 + jnp.where(n == 0, z * 4 + x, x * 4 + z) * 2 + c
+
+
 def qry_kernel(
     req_ref, slot_ref, owner_ref, kvg_ref, q_ref, do_ref, kq_ref, vq_ref, me_ref,
     dq_ref, gk_ref, gv_ref, full_ref,
@@ -114,7 +122,7 @@
         lax.fori_loop(0, NPSG, clear, 0)
 
         def pick(j, c):
-            slot = slot_ref[req_ref[request, j]]
+            slot = spot(slot_ref[req_ref[request, j]])
             slots[j] = slot
             mask[slot] = 1
             return c
@@ -130,13 +138,12 @@
 
         lax.fori_loop(0, NPSG, blank, 0)
 
-    kcols = pl.ds(pl.multiple_of(h * D, D), D)
-    vcols = pl.ds(pl.multiple_of(KV * D + h * D, D), D)
+    cols = pl.ds(pl.multiple_of(h * D, D), D)
     copies = []
     for j in range(P_REQ):
         rows = pl.ds(j * PLEN, PLEN)
-        copies.append(pltpu.make_async_copy(kvg_ref.at[slots[j], :, kcols], kbuf.at[rows], in_sem.at[0]))
-        copies.append(pltpu.make_async_copy(kvg_ref.at[slots[j], :, vcols], vbuf.at[rows], in_sem.at[1]))
+        copies.append(pltpu.make_async_copy(kvg_ref.at[slots[j], 0, :, cols], kbuf.at[rows], in_sem.at[0]))
+        copies.append(pltpu.make_async_copy(kvg_ref.at[slots[j], 1, :, cols], vbuf.at[rows], in_sem.at[1]))
     for copy in copies:
         copy.start()
     qs[...] = stack(q_ref[...])
@@ -211,8 +218,8 @@
             j = t * (TK // PLEN) + i
             part = pl.ds(pl.multiple_of(j * PLEN, PLEN), PLEN)
             slot = slots[j]
-            pltpu.make_async_copy(gkbuf.at[part], full_ref.at[slot, :, kcols], out_sem.at[0]).start()
-            pltpu.make_async_copy(gvbuf.at[part], full_ref.at[slot, :, vcols], out_sem.at[1]).start()
+            pltpu.make_async_copy(gkbuf.at[part], full_ref.at[slot, 0, :, cols], out_sem.at[0]).start()
+            pltpu.make_async_copy(gvbuf.at[part], full_ref.at[slot, 1, :, cols], out_sem.at[1]).start()
         return c
 
     lax.fori_loop(0, NT, back, 0)
@@ -221,8 +228,8 @@
 
     def drain(j, c):
         rows = pl.ds(pl.multiple_of(j * PLEN, PLEN), PLEN)
-        pltpu.make_async_copy(gkbuf.at[rows], full_ref.at[slots[j], :, kcols], out_sem.at[0]).wait()
-        pltpu.make_async_copy(gvbuf.at[rows], full_ref.at[slots[j], :, vcols], out_sem.at[1]).wait()
+        pltpu.make_async_copy(gkbuf.at[rows], full_ref.at[slots[j], 0, :, cols], out_sem.at[0]).wait()
+        pltpu.make_async_copy(gvbuf.at[rows], full_ref.at[slots[j], 1, :, cols], out_sem.at[1]).wait()
         return c
 
     lax.fori_loop(0, P_REQ, drain, 0)
@@ -254,7 +261,7 @@
             jax.ShapeDtypeStruct(q.shape, BF16),
             jax.ShapeDtypeStruct(kq.shape, BF16),
             jax.ShapeDtypeStruct(vq.shape, BF16),
-            jax.ShapeDtypeStruct((NPSG, PLEN, 2 * KV * D), BF16),
+            jax.ShapeDtypeStruct((NPSG, 2, PLEN, KV * D), BF16),
         ],
         scratch_shapes=[
             pltpu.VMEM((G * PLEN, D), BF16),
@@ -270,7 +277,7 @@
             pltpu.VMEM((D, G * PLEN), F32),
             pltpu.VMEM((P_REQ * PLEN, D), BF16),
             pltpu.VMEM((P_REQ * PLEN, D), BF16),
-            pltpu.VMEM((PLEN, 2 * KV * D), BF16),
+            pltpu.VMEM((2, PLEN, KV * D), BF16),
             pltpu.SMEM((P_REQ,), jnp.int32),
             pltpu.SMEM((NPSG,), jnp.int32),
             pltpu.SemaphoreType.DMA((2,)),
@@ -283,47 +290,429 @@
     )(req, slot, owner, kvg, q, do, kq, vq, me)
 
 
-WB = 1024
-
-
-def term_kernel(k_ref, v_ref, wk_ref, wv_ref, out_ref):
-    out_ref[...] = (dot_t(k_ref[...], wk_ref[...]) + dot_t(v_ref[...], wv_ref[...])).astype(BF16)
-
-
-def term(rows_k, rows_v, w_key, w_value):
-    rows = rows_k.shape[0]
+MESH = pl.DeviceIdType.MESH
+
+
+def place():
+    me = lax.axis_index("psg")
+    return me // 8, lax.rem(me // 2, 4), lax.rem(me, 2)
+
+
+def at_plane(z, x, c):
+    return {"psg": (z * 4 + x) * 2 + c}
+
+
+def turn(i, by):
+    return lax.rem(i + by + 4, 4)
+
+
+def greet(devices):
+    barrier = pltpu.get_barrier_semaphore()
+    for device in devices:
+        pl.semaphore_signal(barrier, inc=1, device_id=device, device_id_type=MESH)
+    pl.semaphore_wait(barrier, len(devices))
+
+
+def plane_neighbours(z, x, c):
+    return [
+        at_plane(turn(z, 1), x, c),
+        at_plane(turn(z, -1), x, c),
+        at_plane(z, turn(x, 1), c),
+        at_plane(z, turn(x, -1), c),
+        at_plane(z, x, 1 - c),
+    ]
+
+
+class Sender:
+    def __init__(self, sems):
+        self.sems = sems
+        self.started = []
+
+    def __call__(self, src, dst, recv_sem, device):
+        copy = pltpu.make_async_remote_copy(
+            src_ref=src, dst_ref=dst, send_sem=self.sems.at[len(self.started)], recv_sem=recv_sem,
+            device_id=device, device_id_type=MESH,
+        )
+        copy.start()
+        self.started.append(copy)
+
+    def finish(self):
+        for copy in self.started:
+            copy.wait_send()
+
+
+def arrived(ref, sem):
+    pltpu.make_async_copy(ref, ref, sem).wait()
+
+
+def lane_device(a, b, c):
+    return at_plane(a * (1 - c) + b * c, b * (1 - c) + a * c, c)
+
+
+def gather_kernel(
+    k_ref, v_ref, wk_ref, wv_ref, all_ref, near_ref, far_ref,
+    send_sem, recv_sem, core_sem, local_sem, swap_sem, near_sem, near_core_sem, far_sem,
+):
+    z, x, c = place()
+    y = lax.axis_index("head")
+    a = z * (1 - c) + x * c
+    b = x * (1 - c) + z * c
+    half = k_ref.shape[0] // 2
+    share = far_ref.shape[1]
+    refs = (k_ref, v_ref)
+    weights = (wk_ref, wv_ref)
+    mine = [pltpu.make_async_copy(ref.at[pl.ds(c * half, half)], all_ref.at[c, a, b, c, i], local_sem.at[i]) for i, ref in enumerate(refs)]
+    for copy in mine:
+        copy.start()
+    greet(plane_neighbours(z, x, c) + [{"head": turn(y, 1)}, {"head": turn(y, -1)}])
+    send = Sender(send_sem)
+    partner = at_plane(z, x, 1 - c)
+    for i, ref in enumerate(refs):
+        send(ref.at[pl.ds((1 - c) * half, half)], all_ref.at[1 - c, b, a, c, i], swap_sem.at[i], partner)
+
+    def columns(head):
+        return pl.ds((2 * head + c) * share, share)
+
+    for i, ref in enumerate(weights):
+        for s, by in ((1, 1), (0, -1)):
+            to = turn(y, by)
+            send(ref.at[columns(to)], near_ref.at[s, i, pl.ds(c * share, share)], near_sem.at[s, i], {"head": to})
+    for copy in mine:
+        copy.wait()
+    for i in range(2):
+        arrived(all_ref.at[c, a, b, 1 - c, i], swap_sem.at[i])
+
+    def whole(i, j, to):
+        block = all_ref.at[c, i, j]
+        send(block, block, recv_sem.at[0, i, j], to)
+
+    def piece(i, j, part, to):
+        block = all_ref.at[c, i, j, part]
+        send(block, block, recv_sem.at[part, i, j], to)
+
+    def core(i, j):
+        block = all_ref.at[c, i, j]
+        send(block, block, core_sem.at[i, j], partner)
+
+    def wait_whole(i, j):
+        arrived(all_ref.at[c, i, j], recv_sem.at[0, i, j])
+
+    def wait_pieces(i, j):
+        for part in range(2):
+            arrived(all_ref.at[c, i, j, part], recv_sem.at[part, i, j])
+
+    def along_a(i, j):
+        for by in (1, -1):
+            whole(i, j, lane_device(turn(a, by), b, c))
+
+    ways = ((-1, 0), (1, 1))
+    for by in (1, -1):
+        whole(a, b, lane_device(a, turn(b, by), c))
+    along_a(a, b)
+    across = [pltpu.make_async_copy(ref.at[columns(turn(y, 2))], far_ref.at[i], far_sem.at[i]) for i, ref in enumerate(weights)]
+    for copy in across:
+        copy.start()
+    for by, part in ways:
+        j = turn(b, by)
+        wait_whole(a, j)
+        piece(a, j, part, lane_device(a, turn(b, -by), c))
+    for by, part in ways:
+        along_a(a, turn(b, by))
+
+    def far(bo):
+        j = turn(b, bo)
+        for by, part in ways:
+            i = turn(a, by)
+            wait_whole(i, j)
+            piece(i, j, part, lane_device(turn(a, -by), b, c))
+
+    far(0)
+    wait_pieces(a, turn(b, 2))
+    along_a(a, turn(b, 2))
+    for bo in (0, -1, 1, 2):
+        core(a, turn(b, bo))
+    for by, _ in ways:
+        core(turn(a, by), b)
+    for bo in (-1, 1, 2):
+        far(bo)
+        for by, _ in ways:
+            core(turn(a, by), turn(b, bo))
+    for s in range(2):
+        for i in range(2):
+            block = near_ref.at[s, i, pl.ds(c * share, share)]
+            arrived(block, near_sem.at[s, i])
+            send(block, block, near_core_sem.at[s, i], partner)
+    for bo in (0, -1, 1, 2):
+        wait_pieces(turn(a, 2), turn(b, bo))
+        core(turn(a, 2), turn(b, bo))
+    for i in range(4):
+        for j in range(4):
+            arrived(all_ref.at[1 - c, i, j], core_sem.at[i, j])
+    for s in range(2):
+        for i in range(2):
+            arrived(near_ref.at[s, i, pl.ds((1 - c) * share, share)], near_core_sem.at[s, i])
+    for copy in across:
+        copy.wait()
+    send.finish()
+
+
+def gather_plane(k, v, w_key, w_value):
+    rows, cols = k.shape
     width, depth = w_key.shape
+    share = width // 8
+    hbm = pl.BlockSpec(memory_space=pl.ANY)
+    dma = pltpu.SemaphoreType.DMA
     return pl.pallas_call(
-        term_kernel,
-        grid=(width // WB,),
-        in_specs=[
-            pl.BlockSpec((rows, depth), lambda i: (0, 0)),
-            pl.BlockSpec((rows, depth), lambda i: (0, 0)),
-            pl.BlockSpec((WB, depth), lambda i: (i, 0)),
-            pl.BlockSpec((WB, depth), lambda i: (i, 0)),
+        gather_kernel,
+        in_specs=[hbm] * 4,
+        out_specs=[hbm] * 3,
+        out_shape=[
+            jax.ShapeDtypeStruct((2, 4, 4, 2, 2, rows // 2, cols), BF16),
+            jax.ShapeDtypeStruct((2, 2, 2 * share, depth), BF16),
+            jax.ShapeDtypeStruct((2, share, depth), BF16),
         ],
-        out_specs=pl.BlockSpec((rows, WB), lambda i: (0, i)),
-        out_shape=jax.ShapeDtypeStruct((rows, width), BF16),
-        compiler_params=pltpu.CompilerParams(vmem_limit_bytes=32 * 1024 * 1024),
-        cost_estimate=pl.CostEstimate(flops=4 * rows * width * depth, bytes_accessed=4 * width * depth + 2 * rows * width, transcendentals=0),
-        name="term",
-    )(rows_k, rows_v, w_key, w_value)
+        scratch_shapes=[dma((46,)), dma((2, 4, 4)), dma((4, 4)), dma((2,)), dma((2,)), dma((2, 2)), dma((2, 2)), dma((2,))],
+        compiler_params=pltpu.CompilerParams(collective_id=0, has_side_effects=True),
+        name="gather_plane",
+    )(k, v, w_key, w_value)
+
+
+JOBS = 3
+
+
+def tail_kernel(
+    full_ref, own_k_ref, own_v_ref, qk_ref, qv_ref, wk_ref, wv_ref, near_ref, far_ref, dx_psg_ref, dx_qry_ref,
+    mine, other, relay1, side1, part, relay2, side2, stage, swap, rows, weights, acc, terms,
+    send_sem, core_sem, relay1_sem, side1_sem, relay2_sem, side2_sem, swap_sem, local_sem,
+    load_sem, far_sem, rows_sem, out_sem,
+):
+    z, x, c = place()
+    y = lax.axis_index("head")
+    a = z * (1 - c) + x * c
+    b = x * (1 - c) + z * c
+    partner = at_plane(z, x, 1 - c)
+    steps = (1, -1)
+    halves = (pl.ds(0, 2), pl.ds(2, 2))
+    quarter = dx_qry_ref.shape[0]
+    width = dx_qry_ref.shape[1] // 4
+    share = width // 2
+    heads = [y, turn(y, 1), turn(y, -1), turn(y, 2)]
+    mirror = (0, 2, 1, 3)
+
+    loads = {}
+    for q in range(2):
+        for by in (2, 1, -1, 0):
+            i = turn(a, by)
+            loads[q, by] = pltpu.make_async_copy(full_ref.at[c, i, :, :, :, :, q], mine.at[q, i], local_sem.at[q, i])
+            loads[q, by].start()
+    weight_loads = []
+    for i, ref in enumerate((wk_ref, wv_ref)):
+        weight_loads.append(pltpu.make_async_copy(ref.at[pl.ds(y * width, width)], weights.at[0, i], load_sem.at[0, i]))
+        for s in range(2):
+            weight_loads.append(pltpu.make_async_copy(near_ref.at[s, i], weights.at[1 + s, i], load_sem.at[1 + s, i]))
+        weight_loads.append(pltpu.make_async_copy(far_ref.at[i], weights.at[3, i, pl.ds(c * share, share)], load_sem.at[3, i]))
+    for load in weight_loads:
+        load.start()
+    for i, ref in enumerate((qk_ref, qv_ref)):
+        rows[2, 0, i] = ref[...]
+    greet(plane_neighbours(z, x, c) + [{"head": head} for head in heads[1:]])
+    send = Sender(send_sem)
+
+    def spread(job):
+        for p in (3, 1, 2):
+            send(rows.at[job, 0], rows.at[job, mirror[p]], rows_sem.at[job, mirror[p]], {"head": heads[p]})
+
+    spread(2)
+    for q in range(2):
+        for by in (2, 1, -1, 0):
+            i = turn(b, by)
+            send(full_ref.at[1 - c, i, :, :, :, :, q], other.at[q, i], core_sem.at[q, i], partner)
+        if q == 0:
+            for i in range(2):
+                send(far_ref.at[i], weights.at[3, i, pl.ds(c * share, share)], far_sem.at[i], partner)
+
+    def pair(q, by):
+        i = turn(a, by)
+        loads[q, by].wait()
+        arrived(other.at[q, i], core_sem.at[q, i])
+        mine[q, i] = mine[q, i] + other[q, i]
+        return i
+
+    def ring1_first(q):
+        i = pair(q, 2)
+        for s in range(2):
+            to = lane_device(turn(a, steps[s]), b, c)
+            send(mine.at[q, i, halves[s]], relay1.at[q, s], relay1_sem.at[q, s], to)
+        for s in range(2):
+            i = pair(q, steps[s])
+            send(mine.at[q, i, halves[1 - s]], side1.at[q, s, halves[1 - s]], side1_sem.at[q, s, 1 - s], lane_device(i, b, c))
+
+    def ring1_second(q):
+        for s in range(2):
+            i = turn(a, steps[s])
+            arrived(relay1.at[q, s], relay1_sem.at[q, s])
+            mine[q, i, halves[s]] = mine[q, i, halves[s]] + relay1[q, s]
+            send(mine.at[q, i, halves[s]], side1.at[q, s, halves[s]], side1_sem.at[q, s, s], lane_device(i, b, c))
+        pair(q, 0)
+
+    def join1(q, j):
+        total = mine[q, a, j].astype(F32)
+        for s in range(2):
+            total = total + side1[q, s, j].astype(F32)
+        part[q, j] = total.astype(BF16)
+
+    def ring2_first(q):
+        for s in range(2):
+            for t in range(2):
+                arrived(side1.at[q, s, halves[t]], side1_sem.at[q, s, t])
+        j = turn(b, 2)
+        join1(q, j)
+        for s in range(2):
+            send(part.at[q, j, s], relay2.at[q, s], relay2_sem.at[q, s], lane_device(a, turn(b, steps[s]), c))
+        for s in range(2):
+            j = turn(b, steps[s])
+            join1(q, j)
+            send(part.at[q, j, 1 - s], side2.at[q, s, 1 - s], side2_sem.at[q, s, 1 - s], lane_device(a, j, c))
+        join1(q, b)
+
+    def ring2_second(q):
+        for s in range(2):
+            j = turn(b, steps[s])
+            arrived(relay2.at[q, s], relay2_sem.at[q, s])
+            part[q, j, s] = part[q, j, s] + relay2[q, s]
+            send(part.at[q, j, s], side2.at[q, s, s], side2_sem.at[q, s, s], lane_device(a, j, c))
+
+    def ring2_last(q):
+        for t in range(2):
+            total = part[q, b, t].astype(F32)
+            for s in range(2):
+                arrived(side2.at[q, s, t], side2_sem.at[q, s, t])
+                total = total + side2[q, s, t].astype(F32)
+            stage[q, t] = total.astype(BF16)
+        send(stage.at[q, 1 - c], swap.at[q], swap_sem.at[q], partner)
+
+    def close(q, n, total_of):
+        for i, own_ref in enumerate((own_k_ref, own_v_ref)):
+            for g in range(2):
+                h = 2 * n + g
+                top = pl.multiple_of((2 * h + q) * quarter, quarter)
+                grad = own_ref[pl.ds(top, quarter), :] + total_of(i, g).astype(F32)
+                rows[q, 0, i, pl.ds(pl.multiple_of(h * quarter, quarter), quarter), :] = grad.astype(BF16)
+
+    def finish_rows(q):
+        close(q, c, lambda i, g: stage[q, c, i, g])
+        arrived(swap.at[q], swap_sem.at[q])
+        close(q, 1 - c, lambda i, g: swap[q, i, g])
+        spread(q)
+
+    def product(job, p):
+        for j in range(4):
+            cols = pl.ds(j * (width // 4), width // 4)
+            total = dot_t(rows[job, p, 0], weights[p, 0, cols, :]) + dot_t(rows[job, p, 1], weights[p, 1, cols, :])
+            if p > 0:
+                total = acc[:, cols] + total
+            if p < 3:
+                acc[:, cols] = total
+            else:
+                total = total.astype(BF16)
+                for d in range(4):
+                    terms[job, d, :, cols] = total[d * quarter:(d + 1) * quarter]
+
+    def job_terms(job, out_ref, top):
+        for p in range(4):
+            if p > 0:
+                arrived(rows.at[job, p], rows_sem.at[job, p])
+            product(job, p)
+        place_of = (pl.ds(top, quarter), pl.ds(pl.multiple_of(y * width, width), width))
+        for p in (3, 1, 2):
+            send(terms.at[job, heads[p]], out_ref.at[place_of], out_sem.at[job, mirror[p]], {"head": heads[p]})
+        out_ref[place_of] = terms[job, y]
+
+    def job_wait(job, out_ref, top):
+        for p in (1, 2, 3):
+            cols = pl.ds(pl.multiple_of(heads[p] * width, width), width)
+            arrived(out_ref.at[pl.ds(top, quarter), cols], out_sem.at[job, p])
+
+    ring1_first(0)
+    for load in weight_loads:
+        load.wait()
+    for i in range(2):
+        arrived(weights.at[3, i, pl.ds((1 - c) * share, share)], far_sem.at[i])
+    job_terms(2, dx_qry_ref, 0)
+    ring1_second(0)
+    ring1_first(1)
+    ring2_first(0)
+    ring1_second(1)
+    ring2_second(0)
+    ring2_last(0)
+    finish_rows(0)
+    ring2_first(1)
+    job_terms(0, dx_psg_ref, 0)
+    ring2_second(1)
+    ring2_last(1)
+    finish_rows(1)
+    job_terms(1, dx_psg_ref, quarter)
+    job_wait(2, dx_qry_ref, 0)
+    job_wait(0, dx_psg_ref, 0)
+    job_wait(1, dx_psg_ref, quarter)
+    send.finish()
+
+
+def tail(full, own_k, own_v, gk_qry, gv_qry, w_key, w_value, near, far):
+    rows, cols = own_k.shape
+    width, depth = w_key.shape
+    quarter = rows // 8
+    hbm = pl.BlockSpec(memory_space=pl.ANY)
+    vmem = pl.BlockSpec(memory_space=pltpu.VMEM)
+    dma = pltpu.SemaphoreType.DMA
+    block = (2, 2, 2, quarter, cols)
+    full = full.reshape(2, 4, 4, 2, 2, 2, 2, quarter, cols)
+    return pl.pallas_call(
+        tail_kernel,
+        in_specs=[hbm, vmem, vmem, vmem, vmem, hbm, hbm, hbm, hbm],
+        out_specs=[vmem, vmem],
+        out_shape=[jax.ShapeDtypeStruct((2 * quarter, width), BF16), jax.ShapeDtypeStruct((quarter, width), BF16)],
+        scratch_shapes=[
+            pltpu.VMEM((2, 4, 4) + block, BF16),
+            pltpu.VMEM((2, 4, 4) + block, BF16),
+            pltpu.VMEM((2, 2, 2) + block, BF16),
+            pltpu.VMEM((2, 2, 4) + block, BF16),
+            pltpu.VMEM((2, 4) + block, BF16),
+            pltpu.VMEM((2, 2) + block[1:], BF16),
+            pltpu.VMEM((2, 2) + block, BF16),
+            pltpu.VMEM((2,) + block, BF16),
+            pltpu.VMEM((2,) + block[1:], BF16),
+            pltpu.VMEM((JOBS, 4, 2, 4 * quarter, cols), BF16),
+            pltpu.VMEM((4, 2, width // 4, depth), BF16),
+            pltpu.VMEM((4 * quarter, width // 4), F32),
+            pltpu.VMEM((JOBS, 4, quarter, width // 4), BF16),
+            dma((56,)),
+            dma((2, 4)),
+            dma((2, 2)),
+            dma((2, 2, 2)),
+            dma((2, 2)),
+            dma((2, 2, 2)),
+            dma((2,)),
+            dma((2, 4)),
+            dma((4, 2)),
+            dma((2,)),
+            dma((JOBS, 4)),
+            dma((JOBS, 4)),
+        ],
+        compiler_params=pltpu.CompilerParams(collective_id=3, has_side_effects=True, vmem_limit_bytes=48 * 1024 * 1024),
+        name="tail",
+    )(full, own_k, own_v, gk_qry, gv_qry, w_key, w_value, near, far)
 
 
 def local(q_psg, k_psg, v_psg, do_psg, q_qry, k_qry, v_qry, do_qry, w_key, w_value, req_passages, passage_slot, query_owner):
     me = lax.axis_index("psg").astype(jnp.int32).reshape(1)
-    kv = jnp.concatenate([k_psg, v_psg], axis=1)
-    every = lax.all_gather(kv, "psg", axis=0, tiled=True)
+    every, near, far = gather_plane(k_psg, v_psg, w_key, w_value)
+    far = lax.ppermute(far, "head", [(i, (i + 2) % 4) for i in range(4)])
     dq_psg, own_k, own_v = psg_back(q_psg, k_psg, v_psg, do_psg)
     dq_qry, gk_qry, gv_qry, full = qry_back(
-        req_passages, passage_slot, query_owner, every.reshape(NPSG, PLEN, -1), q_qry, do_qry, k_qry, v_qry, me
+        req_passages, passage_slot, query_owner, every.reshape(NPSG, 2, PLEN, -1), q_qry, do_qry, k_qry, v_qry, me
     )
-    summed = lax.psum_scatter(full.reshape(NPSG * PLEN, -1), "psg", scatter_dimension=0, tiled=True)
-    dx_qry = lax.psum_scatter(term(gk_qry, gv_qry, w_key, w_value), "head", scatter_dimension=0, tiled=True)
-    cols = KV * D
-    gk = (own_k + summed[:, :cols].astype(F32)).astype(BF16)
-    gv = (own_v + summed[:, cols:].astype(F32)).astype(BF16)
-    dx_psg = lax.psum_scatter(term(gk, gv, w_key, w_value), "head", scatter_dimension=0, tiled=True)
+    dx_psg, dx_qry = tail(full, own_k, own_v, gk_qry, gv_qry, w_key, w_value, near, far)
     return dq_psg, dq_qry, dx_psg, dx_qry
 
 

time: 280 us -> 148 us (0.53)
  waiting for transfers between devices: 204 us -> 0.01 us
  Pallas kernels: 41.7 us -> 138 us
  between operations: 13.9 us -> 0.74 us
  local copies, waits for them, and re-layouts: 16.5 us -> 5.95 us
  starting transfers between devices: 0.16 us -> 2.99 us
    reduce_scatter x3 -> x0, waiting for transfers between devices: 146 us -> none  [the longest x1 74.5 us: local(): lax.psum_scatter(full.reshape(NPSG * PLEN, -1), 'psg', scatter_dimension=...]
    pallas_call x2, Pallas kernels: 9.31 us -> 105 us  [the longest x1 64.5 us: tail(): pl.pallas_call(tail_kernel, in_specs=[hbm, vmem, vmem, vmem, vmem, hbm, h...]
    all_gather x1 -> x0, waiting for transfers between devices: 57.8 us -> none  [local(): every = lax.all_gather(kv, 'psg', axis=0, tiled=True)]
    unnamed x31 -> x23, local copies, waits for them, and re-layouts: 16.5 us -> 5.95 us
    ppermute x0 -> x1, starting transfers between devices: none -> 2.99 us  [local(): far = lax.ppermute(far, 'head', [(i, (i + 2) % 4) for i in range(4)])]
  transfers between devices with their start and end apart: 4 -> 1, of which waited for: 4 -> 0; matrix products, arithmetic and copies ran while one was open for 1% -> 1% of each run, Pallas kernels for 5% -> 22%
where the time goes in v3:
time: 148 us
  Pallas kernels  138 us (93%)
  local copies, waits for them, and re-layouts  5.95 us (4%)
  starting transfers between devices  2.99 us (2%)
    pallas_call x1, Pallas kernels, tail(): pl.pallas_call(tail_kernel, in_specs=[hbm, vmem, vmem, vmem, vmem, hbm, h...  64.5 us
    pallas_call x1, Pallas kernels, gather_plane(): pl.pallas_call(gather_kernel, in_specs=[hbm] * 4, out_specs=[hbm] * 3, ou...  40.7 us
    pallas_call x1, Pallas kernels, qry_back(): pl.pallas_call(qry_kernel, grid=(KV,), in_specs=[smem, smem, smem, hbm, w...  26.9 us
    pallas_call x1, Pallas kernels, psg_back(): pl.pallas_call(psg_kernel, grid=(rows // PLEN, KV), in_specs=[wide, thin,...  6 us
    unnamed x23, local copies, waits for them, and re-layouts  5.95 us
    ppermute x1, starting transfers between devices, local(): far = lax.ppermute(far, 'head', [(i, (i + 2) % 4) for i in range(4)])  2.99 us
  transfers between devices with their start and end apart: 1, of which 0 were waited for; matrix products, arithmetic and copies ran while one was open for 1% of the time, Pallas kernels for 22%

profile of v3, /device:TPU:1, one launch (start us, length us, event | category | flops | bytes accessed | tf_op | source)
XLA Modules:
  0.0 147.8 jit_solution(6417850502611914272)
XLA Ops:
  0.6 0.0 copy-start
  0.6 0.0 copy-start.1
  0.7 0.0 copy-start.2
  0.7 0.0 copy-start.3
  0.7 0.0 copy-start.6
  0.7 0.0 copy-start.7
  0.7 40.7 %gather_plane.1 = (bf16[2,4,4,2,2,128,256]{6,5,4,3,2,1,0:T(8,128)(2,1)}, bf16[2,2,2048,256]{3,2,1,0:T(8,128)(2,1)}, bf16[2,1024,256]{2,1,0:T(8,128)(2,1)}) custom-call(bf16[256,256]{1,0:T(8,128)(2,1)} %k_ref.3, bf16[256,256]{1,0:T(8,128)(2,1)} %v_ref.3, bf16[8192,256]{1,0:T(8,128)(2,1)} %wk_ref.3, bf16[8192,256]{1,0:T(8,128)(2,1)} %wv_ref.3), custom_call_target="tpu_custom_call" | custom-call | tf_op jit(solution)/shard_map/gather_plane/pallas_call | solution.py:465
  41.4 3.0 %collective-permute-start = (bf16[2,1024,256]{2,1,0:T(8,128)(2,1)}, bf16[2,1024,256]{2,1,0:T(8,128)(2,1)S(1)}, u32[]{:S(2)}, u32[]{:S(2)}) collective-permute-start(bf16[2,1024,256]{2,1,0:T(8,128)(2,1)} %get-tuple-element.25), channel_id=1, source_target_pairs={{0,2},{1,3},{2,0},{3,1},{4,6},{5,7},{6,4},{7,5},{8,10},{9,11},{10,... | collective-permute-start | bytes 3145736 | tf_op jit(solution)/shard_map/ppermute | solution.py:710
  44.4 0.8 copy.17.req_ref
  45.2 0.0 copy-done
  45.2 0.0 copy-done.1
  45.2 0.0 copy-done.2
  45.2 0.0 copy-done.3
  45.2 6.0 %psg_back.1 = (bf16[256,2048]{1,0:T(8,128)(2,1)}, f32[256,256]{1,0:T(8,128)S(1)}, f32[256,256]{1,0:T(8,128)S(1)}) custom-call(bf16[256,2048]{1,0:T(8,128)(2,1)S(1)} %copy-done.2, bf16[256,256]{1,0:T(8,128)(2,1)S(1)} %copy-done, bf16[256,256]{1,0:T(8,128)(2,1)S(1)} %copy-done.1, bf16[256,2048]{1,0:T(8,128)(2,1)S(1)} %copy-done.3), custom_call_target="tpu_custom_call" | custom-call | flops 671088640 | bytes 4194304 | tf_op jit(solution)/shard_map/psg_back/pallas_call | solution.py:74
  51.2 0.0 copy-done.6
  51.2 0.0 copy-done.7
  51.2 0.0 copy-start.4
  51.2 1.0 copy-done.4
  52.3 0.0 copy-start.5
  52.3 1.0 copy-done.5
  53.3 0.0 copy-start.8
  53.3 0.7 copy-done.8
  54.0 0.0 copy-start.9
  54.0 0.7 copy-done.9
  54.6 26.9 %qry_back.1 = (bf16[128,2048]{1,0:T(8,128)(2,1)}, bf16[128,256]{1,0:T(8,128)(2,1)S(1)}, bf16[128,256]{1,0:T(8,128)(2,1)S(1)}, bf16[64,2,128,256]{3,2,1,0:T(8,128)(2,1)}) custom-call(s32[32,16]{1,0:T(8,128)S(1)} %copy.17.req_ref, s32[64]{0:T(128)S(1)} %copy-done.8, s32[32]{0:T(128)S(1)} %copy-done.9, bf16[64,2,128,256]{3,2,1,0:T(8,128)(2,1)} %bitcast.4, ...), custom_call_target="tpu_custom_call" | custom-call | flops 5704253440 | bytes 16777216 | tf_op jit(solution)/shard_map/qry_back/pallas_call | solution.py:255
  81.5 0.0 collective-permute-done.far_ref
  81.5 64.5 %tail.1 = (bf16[64,8192]{1,0:T(8,128)(2,1)S(1)}, bf16[32,8192]{1,0:T(8,128)(2,1)S(1)}) custom-call(bf16[2,4,4,2,2,2,2,32,256]{8,7,6,5,4,3,2,1,0:T(8,128)(2,1)} %bitcast.3, f32[256,256]{1,0:T(8,128)S(1)} %get-tuple-element.20.own_k_ref, f32[256,256]{1,0:T(8,128)S(1)} %get-tuple-element.21.own_v_ref, bf16[128,256]{1,0:T(8,128)(2,1)S(1)} %get-tuple-element.22.qk_ref, ...), custom_call_target="tpu_custom_call" | custom-call | tf_op jit(solution)/shard_map/tail/pallas_call | solution.py:670
  146.1 1.0 copy.20
  147.1 0.8 copy.21
Async XLA Ops:
  0.6 44.6 %copy-start = (bf16[256,256]{1,0:T(8,128)(2,1)S(1)}, bf16[256,256]{1,0:T(8,128)(2,1)}, u32[]{:S(2)}) copy-start(bf16[256,256]{1,0:T(8,128)(2,1)} %k_ref.3) | copy-start | bytes 393220
  0.6 44.6 %copy-start.1 = (bf16[256,256]{1,0:T(8,128)(2,1)S(1)}, bf16[256,256]{1,0:T(8,128)(2,1)}, u32[]{:S(2)}) copy-start(bf16[256,256]{1,0:T(8,128)(2,1)} %v_ref.3) | copy-start | bytes 393220
  0.7 44.6 %copy-start.2 = (bf16[256,2048]{1,0:T(8,128)(2,1)S(1)}, bf16[256,2048]{1,0:T(8,128)(2,1)}, u32[]{:S(2)}) copy-start(bf16[256,2048]{1,0:T(8,128)(2,1)} %q_ref.2) | copy-start | bytes 3145732
  0.7 44.6 %copy-start.3 = (bf16[256,2048]{1,0:T(8,128)(2,1)S(1)}, bf16[256,2048]{1,0:T(8,128)(2,1)}, u32[]{:S(2)}) copy-start(bf16[256,2048]{1,0:T(8,128)(2,1)} %do_ref.2) | copy-start | bytes 3145732
  0.7 50.6 %copy-start.6 = (bf16[128,256]{1,0:T(8,128)(2,1)S(1)}, bf16[128,256]{1,0:T(8,128)(2,1)}, u32[]{:S(2)}) copy-start(bf16[128,256]{1,0:T(8,128)(2,1)} %kq_ref.1) | copy-start | bytes 196612
  0.7 50.6 %copy-start.7 = (bf16[128,256]{1,0:T(8,128)(2,1)S(1)}, bf16[128,256]{1,0:T(8,128)(2,1)}, u32[]{:S(2)}) copy-start(bf16[128,256]{1,0:T(8,128)(2,1)} %vq_ref.1) | copy-start | bytes 196612
  41.4 40.1 %collective-permute-start = (bf16[2,1024,256]{2,1,0:T(8,128)(2,1)}, bf16[2,1024,256]{2,1,0:T(8,128)(2,1)S(1)}, u32[]{:S(2)}, u32[]{:S(2)}) collective-permute-start(bf16[2,1024,256]{2,1,0:T(8,128)(2,1)} %get-tuple-element.25), channel_id=1, source_target_pairs={{0,2},{1,3},{2,0},{3,1},{4,6},{5,7},{6,4},{7,5},{8,10},{9,11},{10,... | collective-permute-start | bytes 3145736 | tf_op jit(solution)/shard_map/ppermute | solution.py:710
  51.2 1.0 copy-start.4
  52.3 1.0 copy-start.5
  53.3 0.7 copy-start.8
  54.0 0.7 copy-start.9

commit v4 on v3

v4 whole, which is shorter than its diff:
```python
import functools

import jax
import jax.numpy as jnp
from jax import lax
from jax.experimental import pallas as pl
from jax.experimental.pallas import tpu as pltpu
from jax.sharding import PartitionSpec as P

D = 128
G = 8
PLEN = 128
KV = 2
NPSG = 64
REQ = 32
P_REQ = 16
CB = 256
C = D ** -0.5
C2 = C * 1.4426950408889634
F32 = jnp.float32
BF16 = jnp.bfloat16


def stack(x):
    return jnp.concatenate([x[:, g * D:(g + 1) * D] for g in range(G)], axis=0)


def dot(a, b):
    return jnp.dot(a, b, preferred_element_type=F32)


def dot_t(a, b):
    return lax.dot_general(a, b, (((1,), (1,)), ((), ())), preferred_element_type=F32)


def causal_cols(shape):
    key = lax.broadcasted_iota(jnp.int32, shape, 0)
    qry = lax.broadcasted_iota(jnp.int32, shape, 1) % PLEN
    return key <= qry


def passage(q, k, v, do, dq_ref, rows, left):
    qs = stack(q)
    dos = stack(do)
    kt = k.T
    gk = jnp.zeros((PLEN, D), F32)
    gv = jnp.zeros((PLEN, D), F32)
    for b in range(G * PLEN // CB):
        cols = slice(b * CB, (b + 1) * CB)
        s = dot_t(k, qs[cols])
        s = jnp.where(causal_cols(s.shape), s, -1e30)
        e = jnp.exp2((s - jnp.max(s, axis=0, keepdims=True)) * C2)
        inv = 1.0 / jnp.sum(e, axis=0, keepdims=True)
        dp = dot_t(v, dos[cols])
        p = e * inv
        delta = jnp.sum(p * dp, axis=0, keepdims=True)
        ds = (p * (dp - delta)).astype(BF16)
        gk += dot(ds, qs[cols])
        gv += dot(p.astype(BF16), dos[cols])
        dqt = dot(kt, ds) * C
        for i in range(CB // PLEN):
            at = left + (b * (CB // PLEN) + i) * D
            dq_ref[rows, at:at + D] = dqt[:, i * PLEN:(i + 1) * PLEN].T.astype(BF16)
    return gk * C, gv


TK = 1024
TP = TK // PLEN
NT = P_REQ * PLEN // TK


def spot(slot):
    n = slot % 2
    c = slot // 2 % 2
    x = slot // 4 % 4
    z = slot // 16
    return n * 32 + jnp.where(n == 0, z * 4 + x, x * 4 + z) * 2 + c


def qry_kernel(
    req_ref, slot_ref, owner_ref, me_ref, kvg_ref, q_ref, do_ref, kq_ref, vq_ref,
    dq_ref, gk_ref, gv_ref, full_ref,
    kv, qs, dos, qst, dost, ktbuf, sbuf, dpbuf, dqt, gbuf, zeros, slots, mask,
    in_sem, out_sem, zero_sem,
):
    me = me_ref[0]
    zeros[...] = jnp.zeros_like(zeros)
    request = jnp.int32(0)
    for r in range(REQ):
        request = jnp.where(owner_ref[r] == me, r, request)

    def clear(i, carry):
        mask[i] = 0
        return carry

    lax.fori_loop(0, NPSG, clear, 0)

    def pick(j, carry):
        slot = spot(slot_ref[req_ref[request, j]])
        slots[j] = slot
        mask[slot] = 1
        pltpu.make_async_copy(kvg_ref.at[slot], kv.at[j], in_sem).start()
        return carry

    lax.fori_loop(0, P_REQ, pick, 0)

    def blank(wait):
        def one(i, carry):
            @pl.when(mask[i] == 0)
            def _():
                copy = pltpu.make_async_copy(zeros, full_ref.at[i], zero_sem)
                copy.wait() if wait else copy.start()

            return carry

        lax.fori_loop(0, NPSG, one, 0)

    blank(False)

    def land(j, carry):
        pltpu.make_async_copy(kvg_ref.at[slots[j]], kv.at[j], in_sem).wait()
        return carry

    blocks = [slice(i * CB, (i + 1) * CB) for i in range(G * PLEN // CB)]
    own = slice(P_REQ * PLEN, P_REQ * PLEN + PLEN)

    def tile(t, part, cols):
        return kv[pl.ds(t * TP, TP), part, :, cols].reshape(TK, D)

    def tile_rows(t):
        return pl.ds(pl.multiple_of(t * TK, TK), TK)

    def fold(x, op):
        return op(x.reshape(-1, 8, x.shape[1]), axis=0)

    for h in range(KV):
        cols = slice(h * D, (h + 1) * D)
        wide = slice(h * G * D, (h + 1) * G * D)
        qs[...] = stack(q_ref[:, wide])
        dos[...] = stack(do_ref[:, wide])
        qst[...] = qs[...].T
        dost[...] = dos[...].T
        kq = kq_ref[:, cols]
        vq = vq_ref[:, cols]

        def scores(keys, rows, masked, high):
            highs = []
            for b in blocks:
                s = dot(keys, qst[:, b])
                if masked:
                    s = jnp.where(causal_cols(s.shape), s, -1e30)
                sbuf[rows, b] = s
                highs.append(jnp.maximum(high[:, b], fold(s, jnp.max)))
            return jnp.concatenate(highs, axis=1)

        def score_tile(t, high):
            keys = tile(t, 0, cols)
            ktbuf[t] = keys.T
            return scores(keys, tile_rows(t), False, high)

        high = scores(kq, own, True, jnp.full((8, G * PLEN), -1e30, F32))
        if h == 0:
            lax.fori_loop(0, P_REQ, land, 0)
        high = lax.fori_loop(0, NT, score_tile, high)
        m2 = jnp.max(high, axis=0, keepdims=True) * C2

        def sums(values, rows, carry):
            l, num = carry
            ls, nums = [], []
            for b in blocks:
                dp = dot(values, dost[:, b])
                dpbuf[rows, b] = dp
                e = jnp.exp2(sbuf[rows, b] * C2 - m2[:, b])
                ls.append(l[:, b] + fold(e, jnp.sum))
                nums.append(num[:, b] + fold(e * dp, jnp.sum))
            return jnp.concatenate(ls, axis=1), jnp.concatenate(nums, axis=1)

        def sum_tile(t, carry):
            return sums(tile(t, 1, cols), tile_rows(t), carry)

        nothing = jnp.zeros((8, G * PLEN), F32)
        carry = sums(vq, own, (nothing, nothing))
        l, num = lax.fori_loop(0, NT, sum_tile, carry)
        l = jnp.sum(l, axis=0, keepdims=True)
        delta = jnp.sum(num, axis=0, keepdims=True) / l
        level = m2 + jnp.log2(l)

        def grads(kt, rows, first):
            gk = gv = None
            for b in blocks:
                p = jnp.exp2(sbuf[rows, b] * C2 - level[:, b])
                ds = (p * (dpbuf[rows, b] - delta[:, b])).astype(BF16)
                dk = dot(ds, qs[b, :])
                dv = dot(p.astype(BF16), dos[b, :])
                gk = dk if gk is None else gk + dk
                gv = dv if gv is None else gv + dv
                more = dot(kt, ds)
                dqt[:, b] = more if first else dqt[:, b] + more
            return (gk * C).astype(BF16), gv.astype(BF16)

        gk, gv = grads(kq.T, own, True)
        gk_ref[:, cols] = gk
        gv_ref[:, cols] = gv

        def grad_tile(t, carry):
            gk, gv = grads(ktbuf[t], tile_rows(t), False)
            for i in range(TP):
                j = t * TP + i
                gbuf[j, 0, :, cols] = gk[i * PLEN:(i + 1) * PLEN]
                gbuf[j, 1, :, cols] = gv[i * PLEN:(i + 1) * PLEN]
                if h == KV - 1:
                    pltpu.make_async_copy(gbuf.at[j], full_ref.at[slots[j]], out_sem).start()
            return carry

        lax.fori_loop(0, NT, grad_tile, 0)
        for g in range(G):
            left = h * G * D + g * D
            dq_ref[:, left:left + D] = (dqt[:, g * PLEN:(g + 1) * PLEN] * C).T.astype(BF16)

    def drain(j, carry):
        pltpu.make_async_copy(gbuf.at[j], full_ref.at[slots[j]], out_sem).wait()
        return carry

    lax.fori_loop(0, P_REQ, drain, 0)
    blank(True)


def qry_back(req, slot, owner, me, kvg, q, do, kq, vq):
    keys = P_REQ * PLEN + PLEN
    smem = pl.BlockSpec(memory_space=pltpu.SMEM)
    vmem = pl.BlockSpec(memory_space=pltpu.VMEM)
    return pl.pallas_call(
        qry_kernel,
        in_specs=[smem] * 4 + [pl.BlockSpec(memory_space=pl.ANY)] + [vmem] * 4,
        out_specs=[vmem, vmem, vmem, pl.BlockSpec(memory_space=pl.ANY)],
        out_shape=[
            jax.ShapeDtypeStruct(q.shape, BF16),
            jax.ShapeDtypeStruct(kq.shape, BF16),
            jax.ShapeDtypeStruct(vq.shape, BF16),
            jax.ShapeDtypeStruct((NPSG, 2, PLEN, KV * D), BF16),
        ],
        scratch_shapes=[
            pltpu.VMEM((P_REQ, 2, PLEN, KV * D), BF16),
            pltpu.VMEM((G * PLEN, D), BF16),
            pltpu.VMEM((G * PLEN, D), BF16),
            pltpu.VMEM((D, G * PLEN), BF16),
            pltpu.VMEM((D, G * PLEN), BF16),
            pltpu.VMEM((NT, D, TK), BF16),
            pltpu.VMEM((keys, G * PLEN), F32),
            pltpu.VMEM((keys, G * PLEN), F32),
            pltpu.VMEM((D, G * PLEN), F32),
            pltpu.VMEM((P_REQ, 2, PLEN, KV * D), BF16),
            pltpu.VMEM((2, PLEN, KV * D), BF16),
            pltpu.SMEM((P_REQ,), jnp.int32),
            pltpu.SMEM((NPSG,), jnp.int32),
            pltpu.SemaphoreType.DMA,
            pltpu.SemaphoreType.DMA,
            pltpu.SemaphoreType.DMA,
        ],
        compiler_params=pltpu.CompilerParams(vmem_limit_bytes=48 * 1024 * 1024),
        cost_estimate=pl.CostEstimate(flops=2 * 5 * 2 * 1024 * 2176 * 128, bytes_accessed=16 * 1024 * 1024, transcendentals=2 * 1024 * 2176),
        name="qry_back",
    )(req, slot, owner, me, kvg, q, do, kq, vq)


MESH = pl.DeviceIdType.MESH


def place():
    me = lax.axis_index("psg")
    return me // 8, lax.rem(me // 2, 4), lax.rem(me, 2)


def at_plane(z, x, c):
    return {"psg": (z * 4 + x) * 2 + c}


def turn(i, by):
    return lax.rem(i + by + 4, 4)


def greet(devices):
    barrier = pltpu.get_barrier_semaphore()
    for device in devices:
        pl.semaphore_signal(barrier, inc=1, device_id=device, device_id_type=MESH)
    pl.semaphore_wait(barrier, len(devices))


def plane_neighbours(z, x, c):
    return [
        at_plane(turn(z, 1), x, c),
        at_plane(turn(z, -1), x, c),
        at_plane(z, turn(x, 1), c),
        at_plane(z, turn(x, -1), c),
        at_plane(z, x, 1 - c),
    ]


class Sender:
    def __init__(self, sems):
        self.sems = sems
        self.started = []

    def __call__(self, src, dst, recv_sem, device):
        copy = pltpu.make_async_remote_copy(
            src_ref=src, dst_ref=dst, send_sem=self.sems.at[len(self.started)], recv_sem=recv_sem,
            device_id=device, device_id_type=MESH,
        )
        copy.start()
        self.started.append(copy)

    def finish(self):
        for copy in self.started:
            copy.wait_send()


def arrived(ref, sem):
    pltpu.make_async_copy(ref, ref, sem).wait()


def lane_device(a, b, c):
    return at_plane(a * (1 - c) + b * c, b * (1 - c) + a * c, c)


def gather_kernel(
    q_ref, k_ref, v_ref, do_ref, wk_ref, wv_ref, all_ref, near_ref, far_ref, dq_ref, own_k_ref, own_v_ref,
    lane, q_buf, do_buf,
    send_sem, recv_sem, core_sem, local_sem, swap_sem, near_sem, near_core_sem, far_sem, load_sem, keep_sem,
):
    z, x, c = place()
    y = lax.axis_index("head")
    a = z * (1 - c) + x * c
    b = x * (1 - c) + z * c
    half = k_ref.shape[0] // 2
    share = far_ref.shape[1]
    refs = (k_ref, v_ref)
    weights = (wk_ref, wv_ref)
    mine = [pltpu.make_async_copy(ref.at[pl.ds(c * half, half)], lane.at[a, b, c, i], local_sem.at[i]) for i, ref in enumerate(refs)]
    loads = [pltpu.make_async_copy(ref, buf, load_sem.at[i]) for i, (ref, buf) in enumerate(((q_ref, q_buf), (do_ref, do_buf)))]
    for copy in mine + loads:
        copy.start()
    greet(plane_neighbours(z, x, c) + [{"head": turn(y, 1)}, {"head": turn(y, -1)}])
    send = Sender(send_sem)
    partner = at_plane(z, x, 1 - c)
    for i, ref in enumerate(refs):
        send(ref.at[pl.ds((1 - c) * half, half)], lane.at[b, a, c, i], swap_sem.at[i], partner)

    def columns(head):
        return pl.ds((2 * head + c) * share, share)

    for i, ref in enumerate(weights):
        for s, by in ((1, 1), (0, -1)):
            to = turn(y, by)
            send(ref.at[columns(to)], near_ref.at[s, i, pl.ds(c * share, share)], near_sem.at[s, i], {"head": to})
    for copy in mine:
        copy.wait()
    for i in range(2):
        arrived(lane.at[a, b, 1 - c, i], swap_sem.at[i])

    def whole(i, j, to):
        send(lane.at[i, j], lane.at[i, j], recv_sem.at[0, i, j], to)

    def piece(i, j, part, to):
        send(lane.at[i, j, part], lane.at[i, j, part], recv_sem.at[part, i, j], to)

    def keep(i, j):
        return pltpu.make_async_copy(lane.at[i, j], all_ref.at[c, i, j], keep_sem.at[i, j])

    def core(i, j):
        send(lane.at[i, j], all_ref.at[c, i, j], core_sem.at[i, j], partner)
        keep(i, j).start()

    def wait_whole(i, j):
        arrived(lane.at[i, j], recv_sem.at[0, i, j])

    def wait_pieces(i, j):
        for part in range(2):
            arrived(lane.at[i, j, part], recv_sem.at[part, i, j])

    def along_a(i, j):
        for by in (1, -1):
            whole(i, j, lane_device(turn(a, by), b, c))

    def own_passage(n, h):
        rows = slice(n * PLEN, (n + 1) * PLEN)
        thin = slice(h * D, (h + 1) * D)
        wide = slice(h * G * D, (h + 1) * G * D)
        gk, gv = passage(q_buf[rows, wide], k_ref[rows, thin], v_ref[rows, thin], do_buf[rows, wide], dq_ref, rows, h * G * D)
        own_k_ref[rows, thin] = gk
        own_v_ref[rows, thin] = gv

    ways = ((-1, 0), (1, 1))
    for by in (1, -1):
        whole(a, b, lane_device(a, turn(b, by), c))
    along_a(a, b)
    across = [pltpu.make_async_copy(ref.at[columns(turn(y, 2))], far_ref.at[i], far_sem.at[i]) for i, ref in enumerate(weights)]
    for copy in across:
        copy.start()
    for copy in loads:
        copy.wait()
    own_passage(0, 0)
    own_passage(0, 1)
    for by, part in ways:
        j = turn(b, by)
        wait_whole(a, j)
        piece(a, j, part, lane_device(a, turn(b, -by), c))
    for by, part in ways:
        along_a(a, turn(b, by))
    own_passage(1, 0)

    def far(bo):
        j = turn(b, bo)
        for by, part in ways:
            i = turn(a, by)
            wait_whole(i, j)
            piece(i, j, part, lane_device(turn(a, -by), b, c))

    far(0)
    wait_pieces(a, turn(b, 2))
    along_a(a, turn(b, 2))
    own_passage(1, 1)
    for bo in (0, -1, 1, 2):
        core(a, turn(b, bo))
    for by, _ in ways:
        core(turn(a, by), b)
    for bo in (-1, 1, 2):
        far(bo)
        for by, _ in ways:
            core(turn(a, by), turn(b, bo))
    for s in range(2):
        for i in range(2):
            block = near_ref.at[s, i, pl.ds(c * share, share)]
            arrived(block, near_sem.at[s, i])
            send(block, block, near_core_sem.at[s, i], partner)
    for bo in (0, -1, 1, 2):
        wait_pieces(turn(a, 2), turn(b, bo))
        core(turn(a, 2), turn(b, bo))
    for i in range(4):
        for j in range(4):
            arrived(all_ref.at[1 - c, i, j], core_sem.at[i, j])
            keep(i, j).wait()
    for s in range(2):
        for i in range(2):
            arrived(near_ref.at[s, i, pl.ds((1 - c) * share, share)], near_core_sem.at[s, i])
    for copy in across:
        copy.wait()
    send.finish()


def gather_plane(q, k, v, do, w_key, w_value):
    rows, cols = k.shape
    width, depth = w_key.shape
    share = width // 8
    hbm = pl.BlockSpec(memory_space=pl.ANY)
    vmem = pl.BlockSpec(memory_space=pltpu.VMEM)
    dma = pltpu.SemaphoreType.DMA
    return pl.pallas_call(
        gather_kernel,
        in_specs=[hbm, vmem, vmem, hbm, hbm, hbm],
        out_specs=[hbm, hbm, hbm, vmem, vmem, vmem],
        out_shape=[
            jax.ShapeDtypeStruct((2, 4, 4, 2, 2, rows // 2, cols), BF16),
            jax.ShapeDtypeStruct((2, 2, 2 * share, depth), BF16),
            jax.ShapeDtypeStruct((2, share, depth), BF16),
            jax.ShapeDtypeStruct(q.shape, BF16),
            jax.ShapeDtypeStruct(k.shape, F32),
            jax.ShapeDtypeStruct(v.shape, F32),
        ],
        scratch_shapes=[
            pltpu.VMEM((4, 4, 2, 2, rows // 2, cols), BF16),
            pltpu.VMEM(q.shape, BF16),
            pltpu.VMEM(q.shape, BF16),
            dma((46,)), dma((2, 4, 4)), dma((4, 4)), dma((2,)), dma((2,)), dma((2, 2)), dma((2, 2)), dma((2,)), dma((2,)),
            dma((4, 4)),
        ],
        compiler_params=pltpu.CompilerParams(collective_id=0, has_side_effects=True, vmem_limit_bytes=40 * 1024 * 1024),
        name="gather_plane",
    )(q, k, v, do, w_key, w_value)


CUTS = 2
JOBS = CUTS + 1
ORDER = [
    ("f", 0), ("n", 0), (0, 0), ("f", 1), ("o", 0), ("w", 0), (0, 1), ("n", 1), ("o", 1), (1, 0), ("q", 0), (1, 1), (2, 0),
    (3, 0), (4, 0), (2, 1), (5, 0), (3, 1), (4, 1), (5, 1), (6, 0), (6, 1),
]


def tail_kernel(
    full_ref, own_k_ref, own_v_ref, qk_ref, qv_ref, wk_ref, wv_ref, near_ref, far_ref, dx_psg_ref, dx_qry_ref,
    mine, other, relay1, side1, part, relay2, side2, stage, swap, rows, weights, acc, terms,
    send_sem, core_sem, relay1_sem, side1_sem, relay2_sem, side2_sem, swap_sem, local_sem,
    load_sem, far_sem, rows_sem, out_sem,
):
    z, x, c = place()
    y = lax.axis_index("head")
    a = z * (1 - c) + x * c
    b = x * (1 - c) + z * c
    partner = at_plane(z, x, 1 - c)
    steps = (1, -1)
    halves = (pl.ds(0, 2), pl.ds(2, 2))
    quarter = dx_qry_ref.shape[0]
    width = dx_qry_ref.shape[1] // 4
    share = width // 2
    heads = [y, turn(y, 1), turn(y, -1), turn(y, 2)]
    mirror = (0, 2, 1, 3)
    few = dx_psg_ref.shape[0] // CUTS
    size = [few] * CUTS + [quarter]

    loads = {}
    for q in range(CUTS):
        for by in (2, 1, -1, 0):
            i = turn(a, by)
            loads[q, by] = pltpu.make_async_copy(full_ref.at[c, i, :, :, :, :, q], mine.at[q, i], local_sem.at[q, i])
            loads[q, by].start()
    weight_loads = []
    for i, ref in enumerate((wk_ref, wv_ref)):
        weight_loads.append(pltpu.make_async_copy(ref.at[pl.ds(y * width, width)], weights.at[0, i], load_sem.at[0, i]))
        for s in range(2):
            weight_loads.append(pltpu.make_async_copy(near_ref.at[s, i], weights.at[1 + s, i], load_sem.at[1 + s, i]))
        weight_loads.append(pltpu.make_async_copy(far_ref.at[i], weights.at[3, i, pl.ds(c * share, share)], load_sem.at[3, i]))
    for load in weight_loads:
        load.start()
    for i, ref in enumerate((qk_ref, qv_ref)):
        rows[CUTS, 0, i] = ref[...]
    greet(plane_neighbours(z, x, c) + [{"head": head} for head in heads[1:]])
    send = Sender(send_sem)

    def spread(job):
        used = pl.ds(0, 4 * size[job])
        for p in (3, 1, 2):
            for i in range(2):
                send(rows.at[job, 0, i, used], rows.at[job, mirror[p], i, used], rows_sem.at[job, mirror[p], i], {"head": heads[p]})

    spread(CUTS)

    def stage0(q, by):
        i = turn(b, by)
        send(full_ref.at[1 - c, i, :, :, :, :, q], other.at[q, i], core_sem.at[q, i], partner)

    def share_far():
        for i in range(2):
            send(far_ref.at[i], weights.at[3, i, pl.ds(c * share, share)], far_sem.at[i], partner)

    def pair(q, by):
        i = turn(a, by)
        loads[q, by].wait()
        arrived(other.at[q, i], core_sem.at[q, i])
        mine[q, i] = mine[q, i] + other[q, i]
        return i

    def ring1_far(q):
        i = pair(q, 2)
        for s in range(2):
            to = lane_device(turn(a, steps[s]), b, c)
            send(mine.at[q, i, halves[s]], relay1.at[q, s], relay1_sem.at[q, s], to)

    def ring1_near(q):
        for s in range(2):
            i = pair(q, steps[s])
            arrived(relay1.at[q, s], relay1_sem.at[q, s])
            mine[q, i, halves[s]] = mine[q, i, halves[s]] + relay1[q, s]
            send(mine.at[q, i], side1.at[q, s], side1_sem.at[q, s], lane_device(i, b, c))

    def join1(q, j):
        total = mine[q, a, j].astype(F32)
        for s in range(2):
            total = total + side1[q, s, j].astype(F32)
        part[q, j] = total.astype(BF16)

    def ring2_far(q):
        pair(q, 0)
        for s in range(2):
            arrived(side1.at[q, s], side1_sem.at[q, s])
        j = turn(b, 2)
        join1(q, j)
        for s in range(2):
            send(part.at[q, j, s], relay2.at[q, s], relay2_sem.at[q, s], lane_device(a, turn(b, steps[s]), c))
        for by in (1, -1, 0):
            join1(q, turn(b, by))

    def ring2_near(q):
        for s in range(2):
            j = turn(b, steps[s])
            arrived(relay2.at[q, s], relay2_sem.at[q, s])
            part[q, j, s] = part[q, j, s] + relay2[q, s]
            send(part.at[q, j], side2.at[q, s], side2_sem.at[q, s], lane_device(a, j, c))

    def ring2_last(q):
        total = part[q, b].astype(F32)
        for s in range(2):
            arrived(side2.at[q, s], side2_sem.at[q, s])
            total = total + side2[q, s].astype(F32)
        stage[q] = total.astype(BF16)
        send(stage.at[q, 1 - c], swap.at[q], swap_sem.at[q], partner)

    def close(q, n, total_of):
        for i, own_ref in enumerate((own_k_ref, own_v_ref)):
            for g in range(2):
                h = 2 * n + g
                top = pl.multiple_of((CUTS * h + q) * few, few)
                grad = own_ref[pl.ds(top, few), :] + total_of(i, g).astype(F32)
                rows[q, 0, i, pl.ds(pl.multiple_of(h * few, few), few), :] = grad.astype(BF16)

    def finish_rows(q):
        close(q, c, lambda i, g: stage[q, c, i, g])
        arrived(swap.at[q], swap_sem.at[q])
        close(q, 1 - c, lambda i, g: swap[q, i, g])
        spread(q)

    def product(job, p):
        used = pl.ds(0, 4 * size[job])
        for j in range(4):
            cols = pl.ds(j * (width // 4), width // 4)
            total = dot_t(rows[job, p, 0, used], weights[p, 0, cols, :]) + dot_t(rows[job, p, 1, used], weights[p, 1, cols, :])
            if p > 0:
                total = acc[used, cols] + total
            if p < 3:
                acc[used, cols] = total
            else:
                total = total.astype(BF16)
                for d in range(4):
                    terms[job, d, pl.ds(0, size[job]), cols] = total[d * size[job]:(d + 1) * size[job]]

    def target(job):
        return (dx_qry_ref, 0) if job == CUTS else (dx_psg_ref, job * few)

    def job_terms(job):
        out_ref, top = target(job)
        used = pl.ds(0, size[job])
        for p in range(4):
            if p > 0:
                for i in range(2):
                    block = rows.at[job, p, i, pl.ds(0, 4 * size[job])]
                    arrived(block, rows_sem.at[job, p, i])
            product(job, p)
        place_of = (pl.ds(top, size[job]), pl.ds(pl.multiple_of(y * width, width), width))
        for p in (3, 1, 2):
            send(terms.at[job, heads[p], used], out_ref.at[place_of], out_sem.at[job, mirror[p]], {"head": heads[p]})
        out_ref[place_of] = terms[job, y, used]

    def job_wait(job):
        out_ref, top = target(job)
        for p in (1, 2, 3):
            cols = pl.ds(pl.multiple_of(heads[p] * width, width), width)
            arrived(out_ref.at[pl.ds(top, size[job]), cols], out_sem.at[job, p])

    def query_job():
        for load in weight_loads:
            load.wait()
        for i in range(2):
            arrived(weights.at[3, i, pl.ds((1 - c) * share, share)], far_sem.at[i])
        job_terms(CUTS)

    steps_of = {
        "f": lambda q: stage0(q, 2),
        "n": lambda q: (stage0(q, 1), stage0(q, -1)),
        "o": lambda q: stage0(q, 0),
        "w": lambda q: share_far(),
        "q": lambda q: query_job(),
        0: ring1_far,
        1: ring1_near,
        2: ring2_far,
        3: ring2_near,
        4: ring2_last,
        5: finish_rows,
        6: job_terms,
    }
    for step, q in ORDER:
        steps_of[step](q)
    for job in [CUTS] + list(range(CUTS)):
        job_wait(job)
    send.finish()


def tail(full, own_k, own_v, gk_qry, gv_qry, w_key, w_value, near, far):
    rows, cols = own_k.shape
    width, depth = w_key.shape
    quarter = rows // 8
    few = rows // 4 // CUTS
    hbm = pl.BlockSpec(memory_space=pl.ANY)
    vmem = pl.BlockSpec(memory_space=pltpu.VMEM)
    dma = pltpu.SemaphoreType.DMA
    block = (2, 2, 2, few, cols)
    full = full.reshape(2, 4, 4, 2, 2, 2, CUTS, few, cols)
    return pl.pallas_call(
        tail_kernel,
        in_specs=[hbm, vmem, vmem, vmem, vmem, hbm, hbm, hbm, hbm],
        out_specs=[vmem, vmem],
        out_shape=[jax.ShapeDtypeStruct((2 * quarter, width), BF16), jax.ShapeDtypeStruct((quarter, width), BF16)],
        scratch_shapes=[
            pltpu.VMEM((CUTS, 4, 4) + block, BF16),
            pltpu.VMEM((CUTS, 4, 4) + block, BF16),
            pltpu.VMEM((CUTS, 2, 2) + block, BF16),
            pltpu.VMEM((CUTS, 2, 4) + block, BF16),
            pltpu.VMEM((CUTS, 4) + block, BF16),
            pltpu.VMEM((CUTS, 2) + block[1:], BF16),
            pltpu.VMEM((CUTS, 2) + block, BF16),
            pltpu.VMEM((CUTS,) + block, BF16),
            pltpu.VMEM((CUTS,) + block[1:], BF16),
            pltpu.VMEM((JOBS, 4, 2, 4 * quarter, cols), BF16),
            pltpu.VMEM((4, 2, width // 4, depth), BF16),
            pltpu.VMEM((4 * quarter, width // 4), F32),
            pltpu.VMEM((JOBS, 4, quarter, width // 4), BF16),
            dma((13 * CUTS + 2 + 9 * JOBS,)),
            dma((CUTS, 4)),
            dma((CUTS, 2)),
            dma((CUTS, 2)),
            dma((CUTS, 2)),
            dma((CUTS, 2)),
            dma((CUTS,)),
            dma((CUTS, 4)),
            dma((4, 2)),
            dma((2,)),
            dma((JOBS, 4, 2)),
            dma((JOBS, 4)),
        ],
        compiler_params=pltpu.CompilerParams(collective_id=3, has_side_effects=True, vmem_limit_bytes=48 * 1024 * 1024),
        name="tail",
    )(full, own_k, own_v, gk_qry, gv_qry, w_key, w_value, near, far)


def local(q_psg, k_psg, v_psg, do_psg, q_qry, k_qry, v_qry, do_qry, w_key, w_value, req_passages, passage_slot, query_owner):
    me = lax.axis_index("psg").astype(jnp.int32).reshape(1)
    every, near, far, dq_psg, own_k, own_v = gather_plane(q_psg, k_psg, v_psg, do_psg, w_key, w_value)
    far = lax.ppermute(far, "head", [(i, (i + 2) % 4) for i in range(4)])
    dq_qry, gk_qry, gv_qry, full = qry_back(
        req_passages, passage_slot, query_owner, me, every.reshape(NPSG, 2, PLEN, -1), q_qry, do_qry, k_qry, v_qry
    )
    dx_psg, dx_qry = tail(full, own_k, own_v, gk_qry, gv_qry, w_key, w_value, near, far)
    return dq_psg, dq_qry, dx_psg, dx_qry


def solution(mesh):
    rows = P("psg", "head")
    return jax.shard_map(
        local,
        mesh=mesh,
        in_specs=(rows,) * 8 + (P(None, "head"),) * 2 + (P(),) * 3,
        out_specs=(rows, rows, P(("psg", "head"), None), P(("psg", "head"), None)),
        check_vma=False,
    )
```

time: 148 us -> 134 us (0.905)
  Pallas kernels: 138 us -> 116 us
  local copies, waits for them, and re-layouts: 5.95 us -> 12.3 us
  waiting for transfers between devices: 0.01 us -> 3.12 us
    pallas_call x3 -> x2, Pallas kernels: 73.6 us -> 58.3 us  [the longest x1 37.7 us: gather_plane(): pl.pallas_call(gather_kernel, in_specs=[hbm, vmem, vmem, hbm, hbm, hbm],...]
    pallas_call x1, Pallas kernels: 64.5 us -> 57.2 us  [tail(): pl.pallas_call(tail_kernel, in_specs=[hbm, vmem, vmem, vmem, vmem, hbm, h...]
    unnamed x23 -> x30, local copies, waits for them, and re-layouts: 5.95 us -> 12.3 us
    ppermute x1, waiting for transfers between devices: 0.01 us -> 3.12 us  [local(): far = lax.ppermute(far, 'head', [(i, (i + 2) % 4) for i in range(4)])]
  transfers between devices with their start and end apart: 1 -> 1, of which waited for: 0 -> 1; matrix products, arithmetic and copies ran while one was open for 1% -> 0% of each run, Pallas kernels for 22% -> 15%
where the time goes in v4:
time: 134 us; the launch traced here: 133 us
  Pallas kernels  116 us (87%)
  local copies, waits for them, and re-layouts  12.3 us (9%)
  waiting for transfers between devices  3.12 us (2%)
  starting transfers between devices  1.54 us (1%)
    pallas_call x1, Pallas kernels, tail(): pl.pallas_call(tail_kernel, in_specs=[hbm, vmem, vmem, vmem, vmem, hbm, h...  57.2 us
    pallas_call x1, Pallas kernels, gather_plane(): pl.pallas_call(gather_kernel, in_specs=[hbm, vmem, vmem, hbm, hbm, hbm],...  37.7 us
    pallas_call x1, Pallas kernels, qry_back(): pl.pallas_call(qry_kernel, in_specs=[smem] * 4 + [pl.BlockSpec(memory_spa...  20.6 us
    unnamed x30, local copies, waits for them, and re-layouts  12.3 us
    ppermute x1, waiting for transfers between devices, local(): far = lax.ppermute(far, 'head', [(i, (i + 2) % 4) for i in range(4)])  3.12 us
  transfers between devices with their start and end apart: 1, of which 1 were waited for; matrix products, arithmetic and copies ran while one was open for 0% of the time, Pallas kernels for 15%

profile of v4, /device:TPU:1, one launch (start us, length us, event | category | flops | bytes accessed | tf_op | source)
XLA Modules:
  0.0 133.2 jit_solution(15873958127964254976)
XLA Ops:
  0.6 0.0 copy-start
  0.6 2.2 %copy-done = bf16[8192,256]{1,0:T(8,128)(2,1)S(1)} copy-done((bf16[8192,256]{1,0:T(8,128)(2,1)S(1)}, bf16[8192,256]{1,0:T(8,128)(2,1)}, u32[]{:S(2)}) %copy-start) | copy-done | bytes 4194328
  2.8 0.0 copy-start.2
  2.8 1.2 copy-done.2
  4.1 0.0 copy-start.3
  4.1 1.2 copy-done.3
  5.3 0.0 copy-start.4
  5.3 0.9 copy-done.4
  6.2 0.0 copy-start.5
  6.2 0.9 copy-done.5
  7.1 0.0 copy-start.12
  7.1 0.0 copy-start.10
  7.1 0.0 copy-start.11
  7.1 37.7 %gather_plane.1 = (bf16[2,4,4,2,2,128,256]{6,5,4,3,2,1,0:T(8,128)(2,1)}, bf16[2,2,2048,256]{3,2,1,0:T(8,128)(2,1)S(1)}, bf16[2,1024,256]{2,1,0:T(8,128)(2,1)}, b...) custom-call(bf16[256,2048]{1,0:T(8,128)(2,1)S(1)} %copy-done.2, ...), custom_call_target="tpu_custom_call" | custom-call | tf_op jit(solution)/shard_map/gather_plane/pallas_call | solution.py:457
  44.8 0.0 copy-start.1
  44.8 2.0 %copy-done.1 = bf16[2,2,2048,256]{3,2,1,0:T(8,128)(2,1)} copy-done((bf16[2,2,2048,256]{3,2,1,0:T(8,128)(2,1)}, bf16[2,2,2048,256]{3,2,1,0:T(8,128)(2,1)S(1)}, u32[]{:S(2)}) %copy-start.1) | copy-done | bytes 4194328
  46.8 1.5 %collective-permute-start = (bf16[2,1024,256]{2,1,0:T(8,128)(2,1)}, bf16[2,1024,256]{2,1,0:T(8,128)(2,1)S(1)}, u32[]{:S(2)}, u32[]{:S(2)}) collective-permute-start(bf16[2,1024,256]{2,1,0:T(8,128)(2,1)} %get-tuple-element.25), channel_id=1, source_target_pairs={{0,2},{1,3},{2,0},{3,1},{4,6},{5,7},{6,4},{7,5},{8,10},{9,11},{10,... | collective-permute-start | bytes 3145736 | tf_op jit(solution)/shard_map/ppermute | solution.py:726
  48.3 0.0 copy-done.12
  48.3 0.1 copy.17.req_ref
  48.4 0.0 copy-done.6
  48.4 0.0 copy-done.8
  48.4 0.0 copy-done.9
  48.4 0.0 copy-done.10
  48.4 0.0 copy-done.11
  48.4 0.0 copy-start.7
  48.4 1.0 copy-done.7
  49.5 20.6 %qry_back.1 = (bf16[128,2048]{1,0:T(8,128)(2,1)}, bf16[128,256]{1,0:T(8,128)(2,1)S(1)}, bf16[128,256]{1,0:T(8,128)(2,1)S(1)}, bf16[64,2,128,256]{3,2,1,0:T(8,128)(2,1)}) custom-call(s32[32,16]{1,0:T(8,128)S(1)} %copy.17.req_ref, s32[64]{0:T(128)S(1)} %copy-done.10, s32[32]{0:T(128)S(1)} %copy-done.11, s32[1]{0:T(128)} %bitcast.me_ref, ...), custom_call_target="tpu_custom_call" | custom-call | flops 5704253440 | bytes 16777216 | tf_op jit(solution)/shard_map/qry_back/pallas_call | solution.py:232
  70.1 3.1 %collective-permute-done.far_ref = bf16[2,1024,256]{2,1,0:T(8,128)(2,1)S(1)} collective-permute-done((bf16[2,1024,256]{2,1,0:T(8,128)(2,1)}, bf16[2,1024,256]{2,1,0:T(8,128)(2,1)S(1)}, u32[]{:S(2)}, u32[]{:S(2)}) %collective-permute-start) | collective-permute-done | bytes 1048608 | tf_op jit(solution)/shard_map/ppermute | solution.py:726
  73.2 57.2 %tail.1 = (bf16[64,8192]{1,0:T(8,128)(2,1)S(1)}, bf16[32,8192]{1,0:T(8,128)(2,1)S(1)}) custom-call(bf16[2,4,4,2,2,2,2,32,256]{8,7,6,5,4,3,2,1,0:T(8,128)(2,1)} %bitcast.3, f32[256,256]{1,0:T(8,128)S(1)} %get-tuple-element.20.own_k_ref, f32[256,256]{1,0:T(8,128)S(1)} %get-tuple-element.21.own_v_ref, bf16[128,256]{1,0:T(8,128)(2,1)S(1)} %get-tuple-element.22.qk_ref, ...), custom_call_target="tpu_custom_call" | custom-call | tf_op jit(solution)/shard_map/tail/pallas_call | solution.py:686
  130.5 1.0 copy.21
  131.5 1.0 copy.22
  132.4 0.8 copy.23
  (3 shorter events, 0.0 us)
Async XLA Ops:
  0.6 2.2 %copy-start = (bf16[8192,256]{1,0:T(8,128)(2,1)S(1)}, bf16[8192,256]{1,0:T(8,128)(2,1)}, u32[]{:S(2)}) copy-start(bf16[8192,256]{1,0:T(8,128)(2,1)} %wk_ref.3) | copy-start | bytes 12582916
  2.8 1.2 copy-start.2
  4.1 1.2 copy-start.3
  5.3 0.9 copy-start.4
  6.2 0.9 copy-start.5
  7.1 41.2 %copy-start.12 = (s32[32,16]{0,1:T(8,128)S(1)}, s32[32,16]{0,1:T(8,128)}, u32[]{:S(2)}) copy-start(s32[32,16]{0,1:T(8,128)} %param.23) | copy-start | bytes 6148
  7.1 41.3 %copy-start.6 = (bf16[128,2048]{1,0:T(8,128)(2,1)S(1)}, bf16[128,2048]{1,0:T(8,128)(2,1)}, u32[]{:S(2)}) copy-start(bf16[128,2048]{1,0:T(8,128)(2,1)} %q_ref.3) | copy-start | bytes 1572868
  7.1 41.3 %copy-start.8 = (bf16[128,256]{1,0:T(8,128)(2,1)S(1)}, bf16[128,256]{1,0:T(8,128)(2,1)}, u32[]{:S(2)}) copy-start(bf16[128,256]{1,0:T(8,128)(2,1)} %kq_ref.1) | copy-start | bytes 196612
  7.1 41.3 %copy-start.9 = (bf16[128,256]{1,0:T(8,128)(2,1)S(1)}, bf16[128,256]{1,0:T(8,128)(2,1)}, u32[]{:S(2)}) copy-start(bf16[128,256]{1,0:T(8,128)(2,1)} %vq_ref.1) | copy-start | bytes 196612
  7.1 41.3 %copy-start.10 = (s32[64]{0:T(128)S(1)}, s32[64]{0:T(128)}, u32[]{:S(2)}) copy-start(s32[64]{0:T(128)} %slot_ref.1) | copy-start | bytes 772
  7.1 41.3 %copy-start.11 = (s32[32]{0:T(128)S(1)}, s32[32]{0:T(128)}, u32[]{:S(2)}) copy-start(s32[32]{0:T(128)} %owner_ref.1) | copy-start | bytes 388
  44.8 2.0 %copy-start.1 = (bf16[2,2,2048,256]{3,2,1,0:T(8,128)(2,1)}, bf16[2,2,2048,256]{3,2,1,0:T(8,128)(2,1)S(1)}, u32[]{:S(2)}) copy-start(bf16[2,2,2048,256]{3,2,1,0:T(8,128)(2,1)S(1)} %get-tuple-element.24.near_ref) | copy-start | bytes 12582916
  46.8 26.5 %collective-permute-start = (bf16[2,1024,256]{2,1,0:T(8,128)(2,1)}, bf16[2,1024,256]{2,1,0:T(8,128)(2,1)S(1)}, u32[]{:S(2)}, u32[]{:S(2)}) collective-permute-start(bf16[2,1024,256]{2,1,0:T(8,128)(2,1)} %get-tuple-element.25), channel_id=1, source_target_pairs={{0,2},{1,3},{2,0},{3,1},{4,6},{5,7},{6,4},{7,5},{8,10},{9,11},{10,... | collective-permute-start | bytes 3145736 | tf_op jit(solution)/shard_map/ppermute | solution.py:726
  48.4 1.0 copy-start.7

commit v5 on v4

--- a/solution.py
+++ b/solution.py
@@ -17,6 +17,7 @@
 CB = 256
 C = D ** -0.5
 C2 = C * 1.4426950408889634
+VMEM = 62 * 1024 * 1024
 F32 = jnp.float32
 BF16 = jnp.bfloat16
 
@@ -78,12 +79,17 @@
 
 
 def qry_kernel(
-    req_ref, slot_ref, owner_ref, me_ref, kvg_ref, q_ref, do_ref, kq_ref, vq_ref,
-    dq_ref, gk_ref, gv_ref, full_ref,
-    kv, qs, dos, qst, dost, ktbuf, sbuf, dpbuf, dqt, gbuf, zeros, slots, mask,
-    in_sem, out_sem, zero_sem,
+    req_ref, slot_ref, owner_ref, me_ref, kvg_ref, q_any, do_any, kq_any, vq_any, dq_in_ref,
+    dq_ref, gk_ref, gv_ref, full_ref, dq_out_ref,
+    kv, q_ref, do_ref, kq_ref, vq_ref, qs, dos, qst, dost, ktbuf, sbuf, dpbuf, dqt, gbuf, zeros, slots, mask,
+    load_sem, in_sem, out_sem, zero_sem, hand_sem,
 ):
     me = me_ref[0]
+    hand_on = pltpu.make_async_copy(dq_in_ref, dq_out_ref, hand_sem)
+    pairs = ((q_any, q_ref), (do_any, do_ref), (kq_any, kq_ref), (vq_any, vq_ref))
+    loads = [pltpu.make_async_copy(ref, buf, load_sem.at[i]) for i, (ref, buf) in enumerate(pairs)]
+    for copy in loads:
+        copy.start()
     zeros[...] = jnp.zeros_like(zeros)
     request = jnp.int32(0)
     for r in range(REQ):
@@ -116,6 +122,9 @@
         lax.fori_loop(0, NPSG, one, 0)
 
     blank(False)
+    for copy in loads:
+        copy.wait()
+    hand_on.start()
 
     def land(j, carry):
         pltpu.make_async_copy(kvg_ref.at[slots[j]], kv.at[j], in_sem).wait()
@@ -223,24 +232,31 @@
 
     lax.fori_loop(0, P_REQ, drain, 0)
     blank(True)
-
-
-def qry_back(req, slot, owner, me, kvg, q, do, kq, vq):
+    hand_on.wait()
+
+
+def qry_back(req, slot, owner, me, kvg, q, do, kq, vq, dq_psg):
     keys = P_REQ * PLEN + PLEN
     smem = pl.BlockSpec(memory_space=pltpu.SMEM)
+    hbm = pl.BlockSpec(memory_space=pltpu.HBM)
     vmem = pl.BlockSpec(memory_space=pltpu.VMEM)
     return pl.pallas_call(
         qry_kernel,
-        in_specs=[smem] * 4 + [pl.BlockSpec(memory_space=pl.ANY)] + [vmem] * 4,
-        out_specs=[vmem, vmem, vmem, pl.BlockSpec(memory_space=pl.ANY)],
+        in_specs=[smem] * 4 + [hbm] * 6,
+        out_specs=[vmem, vmem, vmem, hbm, hbm],
         out_shape=[
             jax.ShapeDtypeStruct(q.shape, BF16),
             jax.ShapeDtypeStruct(kq.shape, BF16),
             jax.ShapeDtypeStruct(vq.shape, BF16),
             jax.ShapeDtypeStruct((NPSG, 2, PLEN, KV * D), BF16),
+            jax.ShapeDtypeStruct(dq_psg.shape, BF16),
         ],
         scratch_shapes=[
             pltpu.VMEM((P_REQ, 2, PLEN, KV * D), BF16),
+            pltpu.VMEM(q.shape, BF16),
+            pltpu.VMEM(q.shape, BF16),
+            pltpu.VMEM(kq.shape, BF16),
+            pltpu.VMEM(kq.shape, BF16),
             pltpu.VMEM((G * PLEN, D), BF16),
             pltpu.VMEM((G * PLEN, D), BF16),
             pltpu.VMEM((D, G * PLEN), BF16),
@@ -253,14 +269,16 @@
             pltpu.VMEM((2, PLEN, KV * D), BF16),
             pltpu.SMEM((P_REQ,), jnp.int32),
             pltpu.SMEM((NPSG,), jnp.int32),
+            pltpu.SemaphoreType.DMA((4,)),
+            pltpu.SemaphoreType.DMA,
             pltpu.SemaphoreType.DMA,
             pltpu.SemaphoreType.DMA,
             pltpu.SemaphoreType.DMA,
         ],
-        compiler_params=pltpu.CompilerParams(vmem_limit_bytes=48 * 1024 * 1024),
+        compiler_params=pltpu.CompilerParams(vmem_limit_bytes=VMEM),
         cost_estimate=pl.CostEstimate(flops=2 * 5 * 2 * 1024 * 2176 * 128, bytes_accessed=16 * 1024 * 1024, transcendentals=2 * 1024 * 2176),
         name="qry_back",
-    )(req, slot, owner, me, kvg, q, do, kq, vq)
+    )(req, slot, owner, me, kvg, q, do, kq, vq, dq_psg)
 
 
 MESH = pl.DeviceIdType.MESH
@@ -323,23 +341,23 @@
 
 
 def gather_kernel(
-    q_ref, k_ref, v_ref, do_ref, wk_ref, wv_ref, all_ref, near_ref, far_ref, dq_ref, own_k_ref, own_v_ref,
-    lane, q_buf, do_buf,
-    send_sem, recv_sem, core_sem, local_sem, swap_sem, near_sem, near_core_sem, far_sem, load_sem, keep_sem,
+    q_ref, k_ref, v_ref, do_ref, wk_ref, wv_ref, all_ref, near_ref, far_ref, first_ref, dq_ref, own_k_ref, own_v_ref,
+    lane, q_buf, do_buf, k_buf, v_buf, dq_buf, own_k_buf, own_v_buf,
+    send_sem, recv_sem, core_sem, local_sem, swap_sem, near_sem, near_core_sem, far_sem, load_sem, keep_sem, first_sem, out_sem,
 ):
     z, x, c = place()
     y = lax.axis_index("head")
     a = z * (1 - c) + x * c
     b = x * (1 - c) + z * c
     half = k_ref.shape[0] // 2
-    share = far_ref.shape[1]
+    share = 2 * first_ref.shape[0]
     refs = (k_ref, v_ref)
     weights = (wk_ref, wv_ref)
     mine = [pltpu.make_async_copy(ref.at[pl.ds(c * half, half)], lane.at[a, b, c, i], local_sem.at[i]) for i, ref in enumerate(refs)]
-    loads = [pltpu.make_async_copy(ref, buf, load_sem.at[i]) for i, (ref, buf) in enumerate(((q_ref, q_buf), (do_ref, do_buf)))]
+    loads = [pltpu.make_async_copy(ref, buf, load_sem.at[i]) for i, (ref, buf) in enumerate(((q_ref, q_buf), (do_ref, do_buf), (k_ref, k_buf), (v_ref, v_buf)))]
     for copy in mine + loads:
         copy.start()
-    greet(plane_neighbours(z, x, c) + [{"head": turn(y, 1)}, {"head": turn(y, -1)}])
+    greet(plane_neighbours(z, x, c) + [{"head": turn(y, by)} for by in (1, -1, 2)])
     send = Sender(send_sem)
     partner = at_plane(z, x, 1 - c)
     for i, ref in enumerate(refs):
@@ -354,8 +372,6 @@
             send(ref.at[columns(to)], near_ref.at[s, i, pl.ds(c * share, share)], near_sem.at[s, i], {"head": to})
     for copy in mine:
         copy.wait()
-    for i in range(2):
-        arrived(lane.at[a, b, 1 - c, i], swap_sem.at[i])
 
     def whole(i, j, to):
         send(lane.at[i, j], lane.at[i, j], recv_sem.at[0, i, j], to)
@@ -385,15 +401,27 @@
         rows = slice(n * PLEN, (n + 1) * PLEN)
         thin = slice(h * D, (h + 1) * D)
         wide = slice(h * G * D, (h + 1) * G * D)
-        gk, gv = passage(q_buf[rows, wide], k_ref[rows, thin], v_ref[rows, thin], do_buf[rows, wide], dq_ref, rows, h * G * D)
-        own_k_ref[rows, thin] = gk
-        own_v_ref[rows, thin] = gv
+        gk, gv = passage(q_buf[rows, wide], k_buf[rows, thin], v_buf[rows, thin], do_buf[rows, wide], dq_buf, rows, h * G * D)
+        own_k_buf[rows, thin] = gk
+        own_v_buf[rows, thin] = gv
 
     ways = ((-1, 0), (1, 1))
-    for by in (1, -1):
-        whole(a, b, lane_device(a, turn(b, by), c))
-    along_a(a, b)
-    across = [pltpu.make_async_copy(ref.at[columns(turn(y, 2))], far_ref.at[i], far_sem.at[i]) for i, ref in enumerate(weights)]
+    for part in (c, 1 - c):
+        if part is not c:
+            for i in range(2):
+                arrived(lane.at[a, b, part, i], swap_sem.at[i])
+        for by in (1, -1):
+            piece(a, b, part, lane_device(a, turn(b, by), c))
+        for by in (1, -1):
+            piece(a, b, part, lane_device(turn(a, by), b, c))
+    opposite = turn(y, 2)
+    few = share // 2
+    left = (2 * opposite + c) * share
+    send(wk_ref.at[pl.ds(left, few)], first_ref, first_sem, {"head": opposite})
+    across = [
+        pltpu.make_async_copy(wk_ref.at[pl.ds(left + few, few)], far_ref.at[pl.ds(0, few)], far_sem.at[0]),
+        pltpu.make_async_copy(wv_ref.at[pl.ds(left, share)], far_ref.at[pl.ds(few, share)], far_sem.at[1]),
+    ]
     for copy in across:
         copy.start()
     for copy in loads:
@@ -402,7 +430,7 @@
     own_passage(0, 1)
     for by, part in ways:
         j = turn(b, by)
-        wait_whole(a, j)
+        wait_pieces(a, j)
         piece(a, j, part, lane_device(a, turn(b, -by), c))
     for by, part in ways:
         along_a(a, turn(b, by))
@@ -412,13 +440,17 @@
         j = turn(b, bo)
         for by, part in ways:
             i = turn(a, by)
-            wait_whole(i, j)
+            (wait_pieces if bo == 0 else wait_whole)(i, j)
             piece(i, j, part, lane_device(turn(a, -by), b, c))
 
     far(0)
     wait_pieces(a, turn(b, 2))
     along_a(a, turn(b, 2))
     own_passage(1, 1)
+    results = ((dq_buf, dq_ref), (own_k_buf, own_k_ref), (own_v_buf, own_v_ref))
+    stores = [pltpu.make_async_copy(buf, ref, out_sem.at[i]) for i, (buf, ref) in enumerate(results)]
+    for copy in stores:
+        copy.start()
     for bo in (0, -1, 1, 2):
         core(a, turn(b, bo))
     for by, _ in ways:
@@ -442,8 +474,9 @@
     for s in range(2):
         for i in range(2):
             arrived(near_ref.at[s, i, pl.ds((1 - c) * share, share)], near_core_sem.at[s, i])
-    for copy in across:
+    for copy in across + stores:
         copy.wait()
+    arrived(first_ref, first_sem)
     send.finish()
 
 
@@ -451,17 +484,17 @@
     rows, cols = k.shape
     width, depth = w_key.shape
     share = width // 8
-    hbm = pl.BlockSpec(memory_space=pl.ANY)
-    vmem = pl.BlockSpec(memory_space=pltpu.VMEM)
+    hbm = pl.BlockSpec(memory_space=pltpu.HBM)
     dma = pltpu.SemaphoreType.DMA
     return pl.pallas_call(
         gather_kernel,
-        in_specs=[hbm, vmem, vmem, hbm, hbm, hbm],
-        out_specs=[hbm, hbm, hbm, vmem, vmem, vmem],
+        in_specs=[hbm] * 6,
+        out_specs=[hbm] * 7,
         out_shape=[
             jax.ShapeDtypeStruct((2, 4, 4, 2, 2, rows // 2, cols), BF16),
             jax.ShapeDtypeStruct((2, 2, 2 * share, depth), BF16),
-            jax.ShapeDtypeStruct((2, share, depth), BF16),
+            jax.ShapeDtypeStruct((3 * share // 2, depth), BF16),
+            jax.ShapeDtypeStruct((share // 2, depth), BF16),
             jax.ShapeDtypeStruct(q.shape, BF16),
             jax.ShapeDtypeStruct(k.shape, F32),
             jax.ShapeDtypeStruct(v.shape, F32),
@@ -470,10 +503,15 @@
             pltpu.VMEM((4, 4, 2, 2, rows // 2, cols), BF16),
             pltpu.VMEM(q.shape, BF16),
             pltpu.VMEM(q.shape, BF16),
-            dma((46,)), dma((2, 4, 4)), dma((4, 4)), dma((2,)), dma((2,)), dma((2, 2)), dma((2, 2)), dma((2,)), dma((2,)),
-            dma((4, 4)),
+            pltpu.VMEM(k.shape, BF16),
+            pltpu.VMEM(k.shape, BF16),
+            pltpu.VMEM(q.shape, BF16),
+            pltpu.VMEM(k.shape, F32),
+            pltpu.VMEM(k.shape, F32),
+            dma((51,)), dma((2, 4, 4)), dma((4, 4)), dma((2,)), dma((2,)), dma((2, 2)), dma((2, 2)), dma((2,)), dma((4,)),
+            dma((4, 4)), dma, dma((3,)),
         ],
-        compiler_params=pltpu.CompilerParams(collective_id=0, has_side_effects=True, vmem_limit_bytes=40 * 1024 * 1024),
+        compiler_params=pltpu.CompilerParams(collective_id=0, has_side_effects=True, vmem_limit_bytes=VMEM),
         name="gather_plane",
     )(q, k, v, do, w_key, w_value)
 
@@ -481,16 +519,16 @@
 CUTS = 2
 JOBS = CUTS + 1
 ORDER = [
-    ("f", 0), ("n", 0), (0, 0), ("f", 1), ("o", 0), ("w", 0), (0, 1), ("n", 1), ("o", 1), (1, 0), ("q", 0), (1, 1), (2, 0),
-    (3, 0), (4, 0), (2, 1), (5, 0), (3, 1), (4, 1), (5, 1), (6, 0), (6, 1),
+    ("f", 0), ("n", 0), (0, 0), ("f", 1), ("o", 0), ("w", 0), (0, 1), ("n", 1), ("o", 1), (1, 0), (1, 1),
+    (2, 0), ("q", 0), (3, 0), (2, 1), (3, 1), (4, 0), (4, 1),
 ]
 
 
 def tail_kernel(
-    full_ref, own_k_ref, own_v_ref, qk_ref, qv_ref, wk_ref, wv_ref, near_ref, far_ref, dx_psg_ref, dx_qry_ref,
-    mine, other, relay1, side1, part, relay2, side2, stage, swap, rows, weights, acc, terms,
-    send_sem, core_sem, relay1_sem, side1_sem, relay2_sem, side2_sem, swap_sem, local_sem,
-    load_sem, far_sem, rows_sem, out_sem,
+    full_ref, own_k_ref, own_v_ref, qk_ref, qv_ref, wk_ref, wv_ref, near_ref, far_ref, first_ref, dx_psg_ref, dx_qry_ref,
+    mine, other, relay1, side1, part, got, rows, weights, acc, terms,
+    send_sem, core_sem, relay1_sem, side1_sem, got_sem, local_sem,
+    load_sem, far_sem, rows_sem, out_sem, query_sem,
 ):
     z, x, c = place()
     y = lax.axis_index("head")
@@ -518,12 +556,22 @@
         weight_loads.append(pltpu.make_async_copy(ref.at[pl.ds(y * width, width)], weights.at[0, i], load_sem.at[0, i]))
         for s in range(2):
             weight_loads.append(pltpu.make_async_copy(near_ref.at[s, i], weights.at[1 + s, i], load_sem.at[1 + s, i]))
-        weight_loads.append(pltpu.make_async_copy(far_ref.at[i], weights.at[3, i, pl.ds(c * share, share)], load_sem.at[3, i]))
+    cut = share // 2
+    far_parts = (
+        (first_ref, (3, 0, pl.ds(c * share, cut))),
+        (far_ref.at[pl.ds(0, cut)], (3, 0, pl.ds(c * share + cut, cut))),
+        (far_ref.at[pl.ds(cut, share)], (3, 1, pl.ds(c * share, share))),
+    )
+    for i, (ref, to) in enumerate(far_parts):
+        weight_loads.append(pltpu.make_async_copy(ref, weights.at[to], load_sem.at[3, i]))
     for load in weight_loads:
         load.start()
-    for i, ref in enumerate((qk_ref, qv_ref)):
-        rows[CUTS, 0, i] = ref[...]
-    greet(plane_neighbours(z, x, c) + [{"head": head} for head in heads[1:]])
+    query_loads = [pltpu.make_async_copy(ref, rows.at[CUTS, 0, i], query_sem.at[i]) for i, ref in enumerate((qk_ref, qv_ref))]
+    for load in query_loads:
+        load.start()
+    senders = [partner, lane_device(turn(a, 1), b, c), lane_device(turn(a, -1), b, c)]
+    senders += [at_plane(z, turn(x, by), 0) for by in (1, -1, 2)] + [at_plane(turn(z, by), x, 1) for by in (1, -1, 2)]
+    greet(senders + [{"head": head} for head in heads[1:]])
     send = Sender(send_sem)
 
     def spread(job):
@@ -532,6 +580,8 @@
             for i in range(2):
                 send(rows.at[job, 0, i, used], rows.at[job, mirror[p], i, used], rows_sem.at[job, mirror[p], i], {"head": heads[p]})
 
+    for load in query_loads:
+        load.wait()
     spread(CUTS)
 
     def stage0(q, by):
@@ -539,8 +589,8 @@
         send(full_ref.at[1 - c, i, :, :, :, :, q], other.at[q, i], core_sem.at[q, i], partner)
 
     def share_far():
-        for i in range(2):
-            send(far_ref.at[i], weights.at[3, i, pl.ds(c * share, share)], far_sem.at[i], partner)
+        for i, (ref, to) in enumerate(far_parts):
+            send(ref, weights.at[to], far_sem.at[i], partner)
 
     def pair(q, by):
         i = turn(a, by)
@@ -568,47 +618,37 @@
             total = total + side1[q, s, j].astype(F32)
         part[q, j] = total.astype(BF16)
 
-    def ring2_far(q):
+    def ring2(q):
         pair(q, 0)
         for s in range(2):
             arrived(side1.at[q, s], side1_sem.at[q, s])
-        j = turn(b, 2)
-        join1(q, j)
-        for s in range(2):
-            send(part.at[q, j, s], relay2.at[q, s], relay2_sem.at[q, s], lane_device(a, turn(b, steps[s]), c))
-        for by in (1, -1, 0):
-            join1(q, turn(b, by))
-
-    def ring2_near(q):
-        for s in range(2):
-            j = turn(b, steps[s])
-            arrived(relay2.at[q, s], relay2_sem.at[q, s])
-            part[q, j, s] = part[q, j, s] + relay2[q, s]
-            send(part.at[q, j], side2.at[q, s], side2_sem.at[q, s], lane_device(a, j, c))
-
-    def ring2_last(q):
-        total = part[q, b].astype(F32)
-        for s in range(2):
-            arrived(side2.at[q, s], side2_sem.at[q, s])
-            total = total + side2[q, s].astype(F32)
-        stage[q] = total.astype(BF16)
-        send(stage.at[q, 1 - c], swap.at[q], swap_sem.at[q], partner)
-
-    def close(q, n, total_of):
-        for i, own_ref in enumerate((own_k_ref, own_v_ref)):
-            for g in range(2):
-                h = 2 * n + g
-                top = pl.multiple_of((CUTS * h + q) * few, few)
-                grad = own_ref[pl.ds(top, few), :] + total_of(i, g).astype(F32)
-                rows[q, 0, i, pl.ds(pl.multiple_of(h * few, few), few), :] = grad.astype(BF16)
+        for r, by in enumerate((2, 1, -1, 0)):
+            j = turn(b, by)
+            join1(q, j)
+            for core in range(2):
+                if by != 0:
+                    to = at_plane(a * (1 - c) + j * c, j * (1 - c) + a * c, core)
+                    send(part.at[q, j, core], got.at[q, c, r], got_sem.at[q, c, r], to)
+        send(part.at[q, b, 1 - c], got.at[q, c, 3], got_sem.at[q, c, 3], partner)
 
     def finish_rows(q):
-        close(q, c, lambda i, g: stage[q, c, i, g])
-        arrived(swap.at[q], swap_sem.at[q])
-        close(q, 1 - c, lambda i, g: swap[q, i, g])
+        for n in range(2):
+            for r in range(3):
+                arrived(got.at[q, n, r], got_sem.at[q, n, r])
+        arrived(got.at[q, 1 - c, 3], got_sem.at[q, 1 - c, 3])
+        got[q, c, 3] = part[q, b, c]
+        for n in range(2):
+            for i, own_ref in enumerate((own_k_ref, own_v_ref)):
+                total = got[q, n, 0, i].astype(F32)
+                for r in range(1, 4):
+                    total = total + got[q, n, r, i].astype(F32)
+                for g in range(2):
+                    h = 2 * n + g
+                    top = (CUTS * h + q) * few
+                    rows[q, 0, i, h * few:(h + 1) * few, :] = (own_ref[top:top + few, :] + total[g]).astype(BF16)
         spread(q)
 
-    def product(job, p):
+    def product(job, p, done):
         used = pl.ds(0, 4 * size[job])
         for j in range(4):
             cols = pl.ds(j * (width // 4), width // 4)
@@ -621,35 +661,44 @@
                 total = total.astype(BF16)
                 for d in range(4):
                     terms[job, d, pl.ds(0, size[job]), cols] = total[d * size[job]:(d + 1) * size[job]]
+                done(j)
 
     def target(job):
         return (dx_qry_ref, 0) if job == CUTS else (dx_psg_ref, job * few)
 
+    def piece_of(job, head, j):
+        out_ref, top = target(job)
+        left = head * width + j * (width // 4)
+        return out_ref.at[pl.ds(top, size[job]), pl.ds(pl.multiple_of(left, width // 4), width // 4)]
+
     def job_terms(job):
-        out_ref, top = target(job)
         used = pl.ds(0, size[job])
+
+        def done(j):
+            cols = pl.ds(j * (width // 4), width // 4)
+            for p in (3, 1, 2):
+                send(terms.at[job, heads[p], used, cols], piece_of(job, y, j), out_sem.at[job, mirror[p], j], {"head": heads[p]})
+
         for p in range(4):
             if p > 0:
                 for i in range(2):
                     block = rows.at[job, p, i, pl.ds(0, 4 * size[job])]
                     arrived(block, rows_sem.at[job, p, i])
-            product(job, p)
-        place_of = (pl.ds(top, size[job]), pl.ds(pl.multiple_of(y * width, width), width))
-        for p in (3, 1, 2):
-            send(terms.at[job, heads[p], used], out_ref.at[place_of], out_sem.at[job, mirror[p]], {"head": heads[p]})
-        out_ref[place_of] = terms[job, y, used]
+            product(job, p, done)
+        out_ref, top = target(job)
+        out_ref[pl.ds(top, size[job]), pl.ds(pl.multiple_of(y * width, width), width)] = terms[job, y, used]
 
     def job_wait(job):
-        out_ref, top = target(job)
         for p in (1, 2, 3):
-            cols = pl.ds(pl.multiple_of(heads[p] * width, width), width)
-            arrived(out_ref.at[pl.ds(top, size[job]), cols], out_sem.at[job, p])
+            for j in range(4):
+                arrived(piece_of(job, heads[p], j), out_sem.at[job, p, j])
 
     def query_job():
         for load in weight_loads:
             load.wait()
-        for i in range(2):
-            arrived(weights.at[3, i, pl.ds((1 - c) * share, share)], far_sem.at[i])
+        there = (1 - c) * share
+        for i, to in enumerate(((3, 0, pl.ds(there, cut)), (3, 0, pl.ds(there + cut, cut)), (3, 1, pl.ds(there, share)))):
+            arrived(weights.at[to], far_sem.at[i])
         job_terms(CUTS)
 
     steps_of = {
@@ -660,11 +709,9 @@
         "q": lambda q: query_job(),
         0: ring1_far,
         1: ring1_near,
-        2: ring2_far,
-        3: ring2_near,
-        4: ring2_last,
-        5: finish_rows,
-        6: job_terms,
+        2: ring2,
+        3: finish_rows,
+        4: job_terms,
     }
     for step, q in ORDER:
         steps_of[step](q)
@@ -673,19 +720,19 @@
     send.finish()
 
 
-def tail(full, own_k, own_v, gk_qry, gv_qry, w_key, w_value, near, far):
+def tail(full, own_k, own_v, gk_qry, gv_qry, w_key, w_value, near, far, first):
     rows, cols = own_k.shape
     width, depth = w_key.shape
     quarter = rows // 8
     few = rows // 4 // CUTS
-    hbm = pl.BlockSpec(memory_space=pl.ANY)
+    hbm = pl.BlockSpec(memory_space=pltpu.HBM)
     vmem = pl.BlockSpec(memory_space=pltpu.VMEM)
     dma = pltpu.SemaphoreType.DMA
     block = (2, 2, 2, few, cols)
     full = full.reshape(2, 4, 4, 2, 2, 2, CUTS, few, cols)
     return pl.pallas_call(
         tail_kernel,
-        in_specs=[hbm, vmem, vmem, vmem, vmem, hbm, hbm, hbm, hbm],
+        in_specs=[hbm, vmem, vmem, hbm, hbm, hbm, hbm, hbm, pl.BlockSpec(memory_space=pl.ANY), hbm],
         out_specs=[vmem, vmem],
         out_shape=[jax.ShapeDtypeStruct((2 * quarter, width), BF16), jax.ShapeDtypeStruct((quarter, width), BF16)],
         scratch_shapes=[
@@ -694,40 +741,36 @@
             pltpu.VMEM((CUTS, 2, 2) + block, BF16),
             pltpu.VMEM((CUTS, 2, 4) + block, BF16),
             pltpu.VMEM((CUTS, 4) + block, BF16),
-            pltpu.VMEM((CUTS, 2) + block[1:], BF16),
-            pltpu.VMEM((CUTS, 2) + block, BF16),
-            pltpu.VMEM((CUTS,) + block, BF16),
-            pltpu.VMEM((CUTS,) + block[1:], BF16),
+            pltpu.VMEM((CUTS, 2, 4) + block[1:], BF16),
             pltpu.VMEM((JOBS, 4, 2, 4 * quarter, cols), BF16),
             pltpu.VMEM((4, 2, width // 4, depth), BF16),
             pltpu.VMEM((4 * quarter, width // 4), F32),
             pltpu.VMEM((JOBS, 4, quarter, width // 4), BF16),
-            dma((13 * CUTS + 2 + 9 * JOBS,)),
+            dma((15 * CUTS + 3 + 18 * JOBS,)),
             dma((CUTS, 4)),
             dma((CUTS, 2)),
             dma((CUTS, 2)),
-            dma((CUTS, 2)),
-            dma((CUTS, 2)),
-            dma((CUTS,)),
+            dma((CUTS, 2, 4)),
             dma((CUTS, 4)),
-            dma((4, 2)),
+            dma((4, 3)),
+            dma((3,)),
+            dma((JOBS, 4, 2)),
+            dma((JOBS, 4, 4)),
             dma((2,)),
-            dma((JOBS, 4, 2)),
-            dma((JOBS, 4)),
         ],
         compiler_params=pltpu.CompilerParams(collective_id=3, has_side_effects=True, vmem_limit_bytes=48 * 1024 * 1024),
         name="tail",
-    )(full, own_k, own_v, gk_qry, gv_qry, w_key, w_value, near, far)
+    )(full, own_k, own_v, gk_qry, gv_qry, w_key, w_value, near, far, first)
 
 
 def local(q_psg, k_psg, v_psg, do_psg, q_qry, k_qry, v_qry, do_qry, w_key, w_value, req_passages, passage_slot, query_owner):
     me = lax.axis_index("psg").astype(jnp.int32).reshape(1)
-    every, near, far, dq_psg, own_k, own_v = gather_plane(q_psg, k_psg, v_psg, do_psg, w_key, w_value)
+    every, near, far, first, dq_psg, own_k, own_v = gather_plane(q_psg, k_psg, v_psg, do_psg, w_key, w_value)
     far = lax.ppermute(far, "head", [(i, (i + 2) % 4) for i in range(4)])
-    dq_qry, gk_qry, gv_qry, full = qry_back(
-        req_passages, passage_slot, query_owner, me, every.reshape(NPSG, 2, PLEN, -1), q_qry, do_qry, k_qry, v_qry
+    dq_qry, gk_qry, gv_qry, full, dq_psg = qry_back(
+        req_passages, passage_slot, query_owner, me, every.reshape(NPSG, 2, PLEN, -1), q_qry, do_qry, k_qry, v_qry, dq_psg
     )
-    dx_psg, dx_qry = tail(full, own_k, own_v, gk_qry, gv_qry, w_key, w_value, near, far)
+    dx_psg, dx_qry = tail(full, own_k, own_v, gk_qry, gv_qry, w_key, w_value, near, far, first)
     return dq_psg, dq_qry, dx_psg, dx_qry
 
 

time: 134 us -> 138 us (1.030)
  Pallas kernels: 116 us -> 128 us
  local copies, waits for them, and re-layouts: 12.3 us -> 4.13 us
  starting transfers between devices: 1.54 us -> 5.02 us
  waiting for transfers between devices: 3.12 us -> 0.01 us
    pallas_call x3, Pallas kernels: 116 us -> 128 us  [the longest x1 54.4 us: tail(): pl.pallas_call(tail_kernel, in_specs=[hbm, vmem, vmem, hbm, hbm, hbm, hbm...]
    unnamed x30 -> x15, local copies, waits for them, and re-layouts: 12.3 us -> 4.13 us
    ppermute x1, starting transfers between devices: 1.54 us -> 5.02 us  [local(): far = lax.ppermute(far, 'head', [(i, (i + 2) % 4) for i in range(4)])]
    ppermute x1, waiting for transfers between devices: 3.12 us -> 0.01 us  [local(): far = lax.ppermute(far, 'head', [(i, (i + 2) % 4) for i in range(4)])]
  transfers between devices with their start and end apart: 1 -> 1, of which waited for: 1 -> 0; matrix products, arithmetic and copies ran while one was open for 0% -> 0% of each run, Pallas kernels for 15% -> 26%
where the time goes in v5:
time: 138 us
  Pallas kernels  128 us (93%)
  starting transfers between devices  5.02 us (4%)
  local copies, waits for them, and re-layouts  4.13 us (3%)
    pallas_call x1, Pallas kernels, tail(): pl.pallas_call(tail_kernel, in_specs=[hbm, vmem, vmem, hbm, hbm, hbm, hbm...  54.4 us
    pallas_call x1, Pallas kernels, gather_plane(): pl.pallas_call(gather_kernel, in_specs=[hbm] * 6, out_specs=[hbm] * 7, ou...  37.4 us
    pallas_call x1, Pallas kernels, qry_back(): pl.pallas_call(qry_kernel, in_specs=[smem] * 4 + [hbm] * 6, out_specs=[vm...  36.2 us
    ppermute x1, starting transfers between devices, local(): far = lax.ppermute(far, 'head', [(i, (i + 2) % 4) for i in range(4)])  5.02 us
    unnamed x15, local copies, waits for them, and re-layouts  4.13 us
  transfers between devices with their start and end apart: 1, of which 0 were waited for; matrix products, arithmetic and copies ran while one was open for 0% of the time, Pallas kernels for 26%

profile of v5, /device:TPU:1, one launch (start us, length us, event | category | flops | bytes accessed | tf_op | source)
XLA Modules:
  0.0 137.9 jit_solution(15941476275029705980)
XLA Ops:
  0.6 0.0 copy-start.5
  0.6 37.4 %gather_plane.1 = (bf16[2,4,4,2,2,128,256]{6,5,4,3,2,1,0:T(8,128)(2,1)}, bf16[2,2,2048,256]{3,2,1,0:T(8,128)(2,1)}, bf16[1536,256]{1,0:T(8,128)(2,1)}, bf16[512,...) custom-call(bf16[256,2048]{1,0:T(8,128)(2,1)} %q_ref.1, ...), custom_call_target="tpu_custom_call" | custom-call | tf_op jit(solution)/shard_map/gather_plane/pallas_call | solution.py:489
  38.1 5.0 %collective-permute-start = (bf16[1536,256]{1,0:T(8,128)(2,1)}, bf16[1536,256]{1,0:T(8,128)(2,1)S(1)}, u32[]{:S(2)}, u32[]{:S(2)}) collective-permute-start(bf16[1536,256]{1,0:T(8,128)(2,1)} %get-tuple-element.28), channel_id=1, source_target_pairs={{0,2},{1,3},{2,0},{3,1},{4,6},{5,7},{6,4},{7,5},{8,10},{9,11},{10,... | collective-permute-start | bytes 2359304 | tf_op jit(solution)/shard_map/ppermute | solution.py:769
  43.1 0.0 copy-done.5
  43.1 0.7 copy.17.req_ref
  43.8 0.0 copy-start
  43.8 0.0 copy-start.1
  43.8 0.0 copy-start.2
  43.8 36.2 %qry_back.1 = (bf16[128,2048]{1,0:T(8,128)(2,1)}, bf16[128,256]{1,0:T(8,128)(2,1)}, bf16[128,256]{1,0:T(8,128)(2,1)}, bf16[64,2,128,256]{3,2,1,0:T(8,128)(2,1)}, bf16[256,2048]{1,0:T(8,128)(2,1)}) custom-call(s32[32,16]{1,0:T(8,128)} %copy.17.req_ref, s32[64]{0:T(128)} %slot_ref.1, s32[32]{0:T(128)} %owner_ref.1, s32[1]{0:T(128)} %bitcast.me_ref, ...), custom_call_target="tpu_custom_call" | custom-call | flops 5704253440 | bytes 16777216 | tf_op jit(solution)/shard_map/qry_back/pallas_call | solution.py:243
  80.0 0.0 collective-permute-done.far_ref
  80.0 0.0 copy-done
  80.0 0.0 copy-done.1
  80.0 0.0 copy-done.2
  80.0 0.0 copy-start.3
  80.1 0.8 copy-done.3
  80.9 0.0 copy-start.4
  80.9 0.8 copy-done.4
  81.7 54.4 %tail.1 = (bf16[64,8192]{1,0:T(8,128)(2,1)S(1)}, bf16[32,8192]{1,0:T(8,128)(2,1)S(1)}) custom-call(bf16[2,4,4,2,2,2,2,32,256]{8,7,6,5,4,3,2,1,0:T(8,128)(2,1)} %bitcast.3, f32[256,256]{1,0:T(8,128)S(1)} %copy-done.1, f32[256,256]{1,0:T(8,128)S(1)} %copy-done.2, bf16[128,256]{1,0:T(8,128)(2,1)S(1)} %copy-done.3, bf16[128,256]{1,0:T(8,128)(2,1)S(1)} %copy-done.4, ...), custom_call_target="tpu_custom_call" | custom-call | tf_op jit(solution)/shard_map/tail/pallas_call | solution.py:733
  136.1 1.0 copy.20
  137.1 0.8 copy.21
Async XLA Ops:
  0.6 42.5 %copy-start.5 = (s32[32,16]{0,1:T(8,128)S(1)}, s32[32,16]{0,1:T(8,128)}, u32[]{:S(2)}) copy-start(s32[32,16]{0,1:T(8,128)} %param.23) | copy-start | bytes 6148
  38.1 41.9 %collective-permute-start = (bf16[1536,256]{1,0:T(8,128)(2,1)}, bf16[1536,256]{1,0:T(8,128)(2,1)S(1)}, u32[]{:S(2)}, u32[]{:S(2)}) collective-permute-start(bf16[1536,256]{1,0:T(8,128)(2,1)} %get-tuple-element.28), channel_id=1, source_target_pairs={{0,2},{1,3},{2,0},{3,1},{4,6},{5,7},{6,4},{7,5},{8,10},{9,11},{10,... | collective-permute-start | bytes 2359304 | tf_op jit(solution)/shard_map/ppermute | solution.py:769
  43.8 36.2 %copy-start = (bf16[512,256]{1,0:T(8,128)(2,1)S(1)}, bf16[512,256]{1,0:T(8,128)(2,1)}, u32[]{:S(2)}) copy-start(bf16[512,256]{1,0:T(8,128)(2,1)} %get-tuple-element.29.first_ref) | copy-start | bytes 786436
  43.8 36.2 %copy-start.1 = (f32[256,256]{1,0:T(8,128)S(1)}, f32[256,256]{1,0:T(8,128)}, u32[]{:S(2)}) copy-start(f32[256,256]{1,0:T(8,128)} %get-tuple-element.23.own_k_ref) | copy-start | bytes 786436
  43.8 36.2 %copy-start.2 = (f32[256,256]{1,0:T(8,128)S(1)}, f32[256,256]{1,0:T(8,128)}, u32[]{:S(2)}) copy-start(f32[256,256]{1,0:T(8,128)} %get-tuple-element.24.own_v_ref) | copy-start | bytes 786436
  80.0 0.8 copy-start.3
  80.9 0.8 copy-start.4

commit v6 on v5

--- a/solution.py
+++ b/solution.py
@@ -80,12 +80,13 @@
 
 def qry_kernel(
     req_ref, slot_ref, owner_ref, me_ref, kvg_ref, q_any, do_any, kq_any, vq_any, dq_in_ref,
-    dq_ref, gk_ref, gv_ref, full_ref, dq_out_ref,
-    kv, q_ref, do_ref, kq_ref, vq_ref, qs, dos, qst, dost, ktbuf, sbuf, dpbuf, dqt, gbuf, zeros, slots, mask,
+    dq_ref, g_ref, full_ref, dq_out_ref,
+    held, kv, q_ref, do_ref, kq_ref, vq_ref, qs, dos, qst, dost, ktbuf, sbuf, dpbuf, dqt, gbuf, zeros, slots, mask,
     load_sem, in_sem, out_sem, zero_sem, hand_sem,
 ):
     me = me_ref[0]
-    hand_on = pltpu.make_async_copy(dq_in_ref, dq_out_ref, hand_sem)
+    take = pltpu.make_async_copy(dq_in_ref, held, hand_sem.at[0])
+    give = pltpu.make_async_copy(held, dq_out_ref, hand_sem.at[1])
     pairs = ((q_any, q_ref), (do_any, do_ref), (kq_any, kq_ref), (vq_any, vq_ref))
     loads = [pltpu.make_async_copy(ref, buf, load_sem.at[i]) for i, (ref, buf) in enumerate(pairs)]
     for copy in loads:
@@ -124,7 +125,7 @@
     blank(False)
     for copy in loads:
         copy.wait()
-    hand_on.start()
+    take.start()
 
     def land(j, carry):
         pltpu.make_async_copy(kvg_ref.at[slots[j]], kv.at[j], in_sem).wait()
@@ -207,9 +208,12 @@
                 dqt[:, b] = more if first else dqt[:, b] + more
             return (gk * C).astype(BF16), gv.astype(BF16)
 
+        if h == 0:
+            take.wait()
+            give.start()
         gk, gv = grads(kq.T, own, True)
-        gk_ref[:, cols] = gk
-        gv_ref[:, cols] = gv
+        g_ref[0, :, cols] = gk
+        g_ref[1, :, cols] = gv
 
         def grad_tile(t, carry):
             gk, gv = grads(ktbuf[t], tile_rows(t), False)
@@ -232,7 +236,7 @@
 
     lax.fori_loop(0, P_REQ, drain, 0)
     blank(True)
-    hand_on.wait()
+    give.wait()
 
 
 def qry_back(req, slot, owner, me, kvg, q, do, kq, vq, dq_psg):
@@ -243,15 +247,15 @@
     return pl.pallas_call(
         qry_kernel,
         in_specs=[smem] * 4 + [hbm] * 6,
-        out_specs=[vmem, vmem, vmem, hbm, hbm],
+        out_specs=[vmem, vmem, hbm, hbm],
         out_shape=[
             jax.ShapeDtypeStruct(q.shape, BF16),
-            jax.ShapeDtypeStruct(kq.shape, BF16),
-            jax.ShapeDtypeStruct(vq.shape, BF16),
+            jax.ShapeDtypeStruct((2,) + kq.shape, BF16),
             jax.ShapeDtypeStruct((NPSG, 2, PLEN, KV * D), BF16),
             jax.ShapeDtypeStruct(dq_psg.shape, BF16),
         ],
         scratch_shapes=[
+            pltpu.VMEM(dq_psg.shape, BF16),
             pltpu.VMEM((P_REQ, 2, PLEN, KV * D), BF16),
             pltpu.VMEM(q.shape, BF16),
             pltpu.VMEM(q.shape, BF16),
@@ -273,7 +277,7 @@
             pltpu.SemaphoreType.DMA,
             pltpu.SemaphoreType.DMA,
             pltpu.SemaphoreType.DMA,
-            pltpu.SemaphoreType.DMA,
+            pltpu.SemaphoreType.DMA((2,)),
         ],
         compiler_params=pltpu.CompilerParams(vmem_limit_bytes=VMEM),
         cost_estimate=pl.CostEstimate(flops=2 * 5 * 2 * 1024 * 2176 * 128, bytes_accessed=16 * 1024 * 1024, transcendentals=2 * 1024 * 2176),
@@ -342,7 +346,7 @@
 
 def gather_kernel(
     q_ref, k_ref, v_ref, do_ref, wk_ref, wv_ref, all_ref, near_ref, far_ref, first_ref, dq_ref, own_k_ref, own_v_ref,
-    lane, q_buf, do_buf, k_buf, v_buf, dq_buf, own_k_buf, own_v_buf,
+    lane, q_buf, do_buf, k_buf, v_buf, dq_buf, own_k_buf, own_v_buf, far_buf,
     send_sem, recv_sem, core_sem, local_sem, swap_sem, near_sem, near_core_sem, far_sem, load_sem, keep_sem, first_sem, out_sem,
 ):
     z, x, c = place()
@@ -419,8 +423,8 @@
     left = (2 * opposite + c) * share
     send(wk_ref.at[pl.ds(left, few)], first_ref, first_sem, {"head": opposite})
     across = [
-        pltpu.make_async_copy(wk_ref.at[pl.ds(left + few, few)], far_ref.at[pl.ds(0, few)], far_sem.at[0]),
-        pltpu.make_async_copy(wv_ref.at[pl.ds(left, share)], far_ref.at[pl.ds(few, share)], far_sem.at[1]),
+        pltpu.make_async_copy(wk_ref.at[pl.ds(left + few, few)], far_buf.at[pl.ds(0, few)], far_sem.at[0]),
+        pltpu.make_async_copy(wv_ref.at[pl.ds(left, share)], far_buf.at[pl.ds(few, share)], far_sem.at[1]),
     ]
     for copy in across:
         copy.start()
@@ -447,7 +451,9 @@
     wait_pieces(a, turn(b, 2))
     along_a(a, turn(b, 2))
     own_passage(1, 1)
-    results = ((dq_buf, dq_ref), (own_k_buf, own_k_ref), (own_v_buf, own_v_ref))
+    for copy in across:
+        copy.wait()
+    results = ((dq_buf, dq_ref), (own_k_buf, own_k_ref), (own_v_buf, own_v_ref), (far_buf, far_ref))
     stores = [pltpu.make_async_copy(buf, ref, out_sem.at[i]) for i, (buf, ref) in enumerate(results)]
     for copy in stores:
         copy.start()
@@ -474,7 +480,7 @@
     for s in range(2):
         for i in range(2):
             arrived(near_ref.at[s, i, pl.ds((1 - c) * share, share)], near_core_sem.at[s, i])
-    for copy in across + stores:
+    for copy in stores:
         copy.wait()
     arrived(first_ref, first_sem)
     send.finish()
@@ -508,8 +514,9 @@
             pltpu.VMEM(q.shape, BF16),
             pltpu.VMEM(k.shape, F32),
             pltpu.VMEM(k.shape, F32),
+            pltpu.VMEM((3 * share // 2, depth), BF16),
             dma((51,)), dma((2, 4, 4)), dma((4, 4)), dma((2,)), dma((2,)), dma((2, 2)), dma((2, 2)), dma((2,)), dma((4,)),
-            dma((4, 4)), dma, dma((3,)),
+            dma((4, 4)), dma, dma((4,)),
         ],
         compiler_params=pltpu.CompilerParams(collective_id=0, has_side_effects=True, vmem_limit_bytes=VMEM),
         name="gather_plane",
@@ -525,7 +532,7 @@
 
 
 def tail_kernel(
-    full_ref, own_k_ref, own_v_ref, qk_ref, qv_ref, wk_ref, wv_ref, near_ref, far_ref, first_ref, dx_psg_ref, dx_qry_ref,
+    full_ref, own_k_ref, own_v_ref, query_ref, wk_ref, wv_ref, near_ref, far_ref, first_ref, dx_psg_ref, dx_qry_ref,
     mine, other, relay1, side1, part, got, rows, weights, acc, terms,
     send_sem, core_sem, relay1_sem, side1_sem, got_sem, local_sem,
     load_sem, far_sem, rows_sem, out_sem, query_sem,
@@ -566,9 +573,8 @@
         weight_loads.append(pltpu.make_async_copy(ref, weights.at[to], load_sem.at[3, i]))
     for load in weight_loads:
         load.start()
-    query_loads = [pltpu.make_async_copy(ref, rows.at[CUTS, 0, i], query_sem.at[i]) for i, ref in enumerate((qk_ref, qv_ref))]
-    for load in query_loads:
-        load.start()
+    query_load = pltpu.make_async_copy(query_ref, rows.at[CUTS, 0], query_sem)
+    query_load.start()
     senders = [partner, lane_device(turn(a, 1), b, c), lane_device(turn(a, -1), b, c)]
     senders += [at_plane(z, turn(x, by), 0) for by in (1, -1, 2)] + [at_plane(turn(z, by), x, 1) for by in (1, -1, 2)]
     greet(senders + [{"head": head} for head in heads[1:]])
@@ -580,8 +586,7 @@
             for i in range(2):
                 send(rows.at[job, 0, i, used], rows.at[job, mirror[p], i, used], rows_sem.at[job, mirror[p], i], {"head": heads[p]})
 
-    for load in query_loads:
-        load.wait()
+    query_load.wait()
     spread(CUTS)
 
     def stage0(q, by):
@@ -720,7 +725,7 @@
     send.finish()
 
 
-def tail(full, own_k, own_v, gk_qry, gv_qry, w_key, w_value, near, far, first):
+def tail(full, own_k, own_v, g_qry, w_key, w_value, near, far, first):
     rows, cols = own_k.shape
     width, depth = w_key.shape
     quarter = rows // 8
@@ -732,7 +737,7 @@
     full = full.reshape(2, 4, 4, 2, 2, 2, CUTS, few, cols)
     return pl.pallas_call(
         tail_kernel,
-        in_specs=[hbm, vmem, vmem, hbm, hbm, hbm, hbm, hbm, pl.BlockSpec(memory_space=pl.ANY), hbm],
+        in_specs=[hbm, vmem, vmem, hbm, hbm, hbm, hbm, pl.BlockSpec(memory_space=pl.ANY), hbm],
         out_specs=[vmem, vmem],
         out_shape=[jax.ShapeDtypeStruct((2 * quarter, width), BF16), jax.ShapeDtypeStruct((quarter, width), BF16)],
         scratch_shapes=[
@@ -756,21 +761,21 @@
             dma((3,)),
             dma((JOBS, 4, 2)),
             dma((JOBS, 4, 4)),
-            dma((2,)),
+            dma,
         ],
         compiler_params=pltpu.CompilerParams(collective_id=3, has_side_effects=True, vmem_limit_bytes=48 * 1024 * 1024),
         name="tail",
-    )(full, own_k, own_v, gk_qry, gv_qry, w_key, w_value, near, far, first)
+    )(full, own_k, own_v, g_qry, w_key, w_value, near, far, first)
 
 
 def local(q_psg, k_psg, v_psg, do_psg, q_qry, k_qry, v_qry, do_qry, w_key, w_value, req_passages, passage_slot, query_owner):
     me = lax.axis_index("psg").astype(jnp.int32).reshape(1)
     every, near, far, first, dq_psg, own_k, own_v = gather_plane(q_psg, k_psg, v_psg, do_psg, w_key, w_value)
     far = lax.ppermute(far, "head", [(i, (i + 2) % 4) for i in range(4)])
-    dq_qry, gk_qry, gv_qry, full, dq_psg = qry_back(
+    dq_qry, g_qry, full, dq_psg = qry_back(
         req_passages, passage_slot, query_owner, me, every.reshape(NPSG, 2, PLEN, -1), q_qry, do_qry, k_qry, v_qry, dq_psg
     )
-    dx_psg, dx_qry = tail(full, own_k, own_v, gk_qry, gv_qry, w_key, w_value, near, far, first)
+    dx_psg, dx_qry = tail(full, own_k, own_v, g_qry, w_key, w_value, near, far, first)
     return dq_psg, dq_qry, dx_psg, dx_qry
 
 

time: 138 us -> 122 us (0.88)
  Pallas kernels: 128 us -> 113 us
    pallas_call x1, Pallas kernels: 36.2 us -> 20.7 us  [qry_back(): pl.pallas_call(qry_kernel, in_specs=[smem] * 4 + [hbm] * 6, out_specs=[vm...]
    unnamed x15 -> x13, local copies, waits for them, and re-layouts: 4.13 us -> 3.36 us
  transfers between devices with their start and end apart: 1 -> 1, of which waited for: 0 -> 0; matrix products, arithmetic and copies ran while one was open for 0% -> 1% of each run, Pallas kernels for 26% -> 17%
where the time goes in v6:
time: 122 us
  Pallas kernels  113 us (93%)
  starting transfers between devices  5.02 us (4%)
  local copies, waits for them, and re-layouts  3.36 us (3%)
    pallas_call x1, Pallas kernels, tail(): pl.pallas_call(tail_kernel, in_specs=[hbm, vmem, vmem, hbm, hbm, hbm, hbm...  54.4 us
    pallas_call x1, Pallas kernels, gather_plane(): pl.pallas_call(gather_kernel, in_specs=[hbm] * 6, out_specs=[hbm] * 7, ou...  37.5 us
    pallas_call x1, Pallas kernels, qry_back(): pl.pallas_call(qry_kernel, in_specs=[smem] * 4 + [hbm] * 6, out_specs=[vm...  20.7 us
    ppermute x1, starting transfers between devices, local(): far = lax.ppermute(far, 'head', [(i, (i + 2) % 4) for i in range(4)])  5.02 us
    unnamed x13, local copies, waits for them, and re-layouts  3.36 us
  transfers between devices with their start and end apart: 1, of which 0 were waited for; matrix products, arithmetic and copies ran while one was open for 1% of the time, Pallas kernels for 17%

profile of v6, /device:TPU:1, one launch (start us, length us, event | category | flops | bytes accessed | tf_op | source)
XLA Modules:
  0.0 121.6 jit_solution(13070775305146602685)
XLA Ops:
  0.6 0.0 copy-start.4
  0.6 37.5 %gather_plane.1 = (bf16[2,4,4,2,2,128,256]{6,5,4,3,2,1,0:T(8,128)(2,1)}, bf16[2,2,2048,256]{3,2,1,0:T(8,128)(2,1)}, bf16[1536,256]{1,0:T(8,128)(2,1)}, bf16[512,...) custom-call(bf16[256,2048]{1,0:T(8,128)(2,1)} %q_ref.1, ...), custom_call_target="tpu_custom_call" | custom-call | tf_op jit(solution)/shard_map/gather_plane/pallas_call | solution.py:495
  38.1 5.0 %collective-permute-start = (bf16[1536,256]{1,0:T(8,128)(2,1)}, bf16[1536,256]{1,0:T(8,128)(2,1)S(1)}, u32[]{:S(2)}, u32[]{:S(2)}) collective-permute-start(bf16[1536,256]{1,0:T(8,128)(2,1)} %get-tuple-element.26), channel_id=1, source_target_pairs={{0,2},{1,3},{2,0},{3,1},{4,6},{5,7},{6,4},{7,5},{8,10},{9,11},{10,... | collective-permute-start | bytes 2359304 | tf_op jit(solution)/shard_map/ppermute | solution.py:774
  43.1 0.0 copy-done.4
  43.1 0.7 copy.17.req_ref
  43.8 0.0 copy-start
  43.8 0.0 copy-start.1
  43.8 0.0 copy-start.2
  43.8 20.7 %qry_back.1 = (bf16[128,2048]{1,0:T(8,128)(2,1)}, bf16[2,128,256]{2,1,0:T(8,128)(2,1)}, bf16[64,2,128,256]{3,2,1,0:T(8,128)(2,1)}, bf16[256,2048]{1,0:T(8,128)(2,1)}) custom-call(s32[32,16]{1,0:T(8,128)} %copy.17.req_ref, s32[64]{0:T(128)} %slot_ref.1, s32[32]{0:T(128)} %owner_ref.1, s32[1]{0:T(128)} %bitcast.me_ref, bf16[64,2,128,256]{3,2,1,0:T(8,128)(2,1)} %bitcast.4, ...), custom_call_target="tpu_custom_call" | custom-call | flops 5704253440 | bytes 16777216 | tf_op jit(solution)/shard_map/qry_back/pallas_call | solution.py:247
  64.5 0.0 collective-permute-done.far_ref
  64.6 0.0 copy-done
  64.6 0.0 copy-done.1
  64.6 0.0 copy-done.2
  64.6 0.0 copy-start.3
  64.6 0.9 copy-done.3
  65.5 54.4 %tail.1 = (bf16[64,8192]{1,0:T(8,128)(2,1)S(1)}, bf16[32,8192]{1,0:T(8,128)(2,1)S(1)}) custom-call(bf16[2,4,4,2,2,2,2,32,256]{8,7,6,5,4,3,2,1,0:T(8,128)(2,1)} %bitcast.3, f32[256,256]{1,0:T(8,128)S(1)} %copy-done.1, f32[256,256]{1,0:T(8,128)S(1)} %copy-done.2, bf16[2,128,256]{2,1,0:T(8,128)(2,1)S(1)} %copy-done.3, bf16[8192,256]{1,0:T(8,128)(2,1)} %wk_ref.3, ...), custom_call_target="tpu_custom_call" | custom-call | tf_op jit(solution)/shard_map/tail/pallas_call | solution.py:738
  119.9 1.0 copy.20
  120.8 0.8 copy.21
Async XLA Ops:
  0.6 42.5 %copy-start.4 = (s32[32,16]{0,1:T(8,128)S(1)}, s32[32,16]{0,1:T(8,128)}, u32[]{:S(2)}) copy-start(s32[32,16]{0,1:T(8,128)} %param.23) | copy-start | bytes 6148
  38.1 26.5 %collective-permute-start = (bf16[1536,256]{1,0:T(8,128)(2,1)}, bf16[1536,256]{1,0:T(8,128)(2,1)S(1)}, u32[]{:S(2)}, u32[]{:S(2)}) collective-permute-start(bf16[1536,256]{1,0:T(8,128)(2,1)} %get-tuple-element.26), channel_id=1, source_target_pairs={{0,2},{1,3},{2,0},{3,1},{4,6},{5,7},{6,4},{7,5},{8,10},{9,11},{10,... | collective-permute-start | bytes 2359304 | tf_op jit(solution)/shard_map/ppermute | solution.py:774
  43.8 20.8 %copy-start = (bf16[512,256]{1,0:T(8,128)(2,1)S(1)}, bf16[512,256]{1,0:T(8,128)(2,1)}, u32[]{:S(2)}) copy-start(bf16[512,256]{1,0:T(8,128)(2,1)} %get-tuple-element.27.first_ref) | copy-start | bytes 786436
  43.8 20.8 %copy-start.1 = (f32[256,256]{1,0:T(8,128)S(1)}, f32[256,256]{1,0:T(8,128)}, u32[]{:S(2)}) copy-start(f32[256,256]{1,0:T(8,128)} %get-tuple-element.22.own_k_ref) | copy-start | bytes 786436
  43.8 20.8 %copy-start.2 = (f32[256,256]{1,0:T(8,128)S(1)}, f32[256,256]{1,0:T(8,128)}, u32[]{:S(2)}) copy-start(f32[256,256]{1,0:T(8,128)} %get-tuple-element.23.own_v_ref) | copy-start | bytes 786436
  64.6 0.9 copy-start.3

commit v7 on v6

--- a/solution.py
+++ b/solution.py
@@ -79,10 +79,10 @@
 
 
 def qry_kernel(
-    req_ref, slot_ref, owner_ref, me_ref, kvg_ref, q_any, do_any, kq_any, vq_any, dq_in_ref,
+    req_ref, slot_ref, owner_ref, me_ref, kvg_ref, q_any, do_any, kq_any, vq_any, dq_in_ref, cleared_ref,
     dq_ref, g_ref, full_ref, dq_out_ref,
-    held, kv, q_ref, do_ref, kq_ref, vq_ref, qs, dos, qst, dost, ktbuf, sbuf, dpbuf, dqt, gbuf, zeros, slots, mask,
-    load_sem, in_sem, out_sem, zero_sem, hand_sem,
+    held, kv, q_ref, do_ref, kq_ref, vq_ref, qs, dos, qst, dost, ktbuf, sbuf, dpbuf, dqt, gbuf, slots,
+    load_sem, in_sem, out_sem, hand_sem,
 ):
     me = me_ref[0]
     take = pltpu.make_async_copy(dq_in_ref, held, hand_sem.at[0])
@@ -91,38 +91,18 @@
     loads = [pltpu.make_async_copy(ref, buf, load_sem.at[i]) for i, (ref, buf) in enumerate(pairs)]
     for copy in loads:
         copy.start()
-    zeros[...] = jnp.zeros_like(zeros)
     request = jnp.int32(0)
     for r in range(REQ):
         request = jnp.where(owner_ref[r] == me, r, request)
 
-    def clear(i, carry):
-        mask[i] = 0
-        return carry
-
-    lax.fori_loop(0, NPSG, clear, 0)
-
     def pick(j, carry):
         slot = spot(slot_ref[req_ref[request, j]])
         slots[j] = slot
-        mask[slot] = 1
         pltpu.make_async_copy(kvg_ref.at[slot], kv.at[j], in_sem).start()
         return carry
 
     lax.fori_loop(0, P_REQ, pick, 0)
 
-    def blank(wait):
-        def one(i, carry):
-            @pl.when(mask[i] == 0)
-            def _():
-                copy = pltpu.make_async_copy(zeros, full_ref.at[i], zero_sem)
-                copy.wait() if wait else copy.start()
-
-            return carry
-
-        lax.fori_loop(0, NPSG, one, 0)
-
-    blank(False)
     for copy in loads:
         copy.wait()
     take.start()
@@ -235,18 +215,18 @@
         return carry
 
     lax.fori_loop(0, P_REQ, drain, 0)
-    blank(True)
     give.wait()
 
 
-def qry_back(req, slot, owner, me, kvg, q, do, kq, vq, dq_psg):
+def qry_back(req, slot, owner, me, kvg, q, do, kq, vq, dq_psg, cleared):
     keys = P_REQ * PLEN + PLEN
     smem = pl.BlockSpec(memory_space=pltpu.SMEM)
     hbm = pl.BlockSpec(memory_space=pltpu.HBM)
     vmem = pl.BlockSpec(memory_space=pltpu.VMEM)
     return pl.pallas_call(
         qry_kernel,
-        in_specs=[smem] * 4 + [hbm] * 6,
+        in_specs=[smem] * 4 + [hbm] * 7,
+        input_output_aliases={10: 2},
         out_specs=[vmem, vmem, hbm, hbm],
         out_shape=[
             jax.ShapeDtypeStruct(q.shape, BF16),
@@ -270,11 +250,8 @@
             pltpu.VMEM((keys, G * PLEN), F32),
             pltpu.VMEM((D, G * PLEN), F32),
             pltpu.VMEM((P_REQ, 2, PLEN, KV * D), BF16),
-            pltpu.VMEM((2, PLEN, KV * D), BF16),
             pltpu.SMEM((P_REQ,), jnp.int32),
-            pltpu.SMEM((NPSG,), jnp.int32),
             pltpu.SemaphoreType.DMA((4,)),
-            pltpu.SemaphoreType.DMA,
             pltpu.SemaphoreType.DMA,
             pltpu.SemaphoreType.DMA,
             pltpu.SemaphoreType.DMA((2,)),
@@ -282,7 +259,7 @@
         compiler_params=pltpu.CompilerParams(vmem_limit_bytes=VMEM),
         cost_estimate=pl.CostEstimate(flops=2 * 5 * 2 * 1024 * 2176 * 128, bytes_accessed=16 * 1024 * 1024, transcendentals=2 * 1024 * 2176),
         name="qry_back",
-    )(req, slot, owner, me, kvg, q, do, kq, vq, dq_psg)
+    )(req, slot, owner, me, kvg, q, do, kq, vq, dq_psg, cleared)
 
 
 MESH = pl.DeviceIdType.MESH
@@ -345,9 +322,9 @@
 
 
 def gather_kernel(
-    q_ref, k_ref, v_ref, do_ref, wk_ref, wv_ref, all_ref, near_ref, far_ref, first_ref, dq_ref, own_k_ref, own_v_ref,
-    lane, q_buf, do_buf, k_buf, v_buf, dq_buf, own_k_buf, own_v_buf, far_buf,
-    send_sem, recv_sem, core_sem, local_sem, swap_sem, near_sem, near_core_sem, far_sem, load_sem, keep_sem, first_sem, out_sem,
+    q_ref, k_ref, v_ref, do_ref, wk_ref, wv_ref, all_ref, near_ref, far_ref, first_ref, dq_ref, own_k_ref, own_v_ref, full_ref,
+    lane, q_buf, do_buf, k_buf, v_buf, dq_buf, own_k_buf, own_v_buf, far_buf, zeros,
+    send_sem, recv_sem, core_sem, local_sem, swap_sem, near_sem, near_core_sem, far_sem, load_sem, keep_sem, first_sem, out_sem, zero_sem,
 ):
     z, x, c = place()
     y = lax.axis_index("head")
@@ -428,8 +405,13 @@
     ]
     for copy in across:
         copy.start()
+    zeros[...] = jnp.zeros_like(zeros)
+    some = zeros.shape[0]
+    clears = [pltpu.make_async_copy(zeros, full_ref.at[pl.ds(i * some, some)], zero_sem.at[i]) for i in range(NPSG // some)]
     for copy in loads:
         copy.wait()
+    for copy in clears:
+        copy.start()
     own_passage(0, 0)
     own_passage(0, 1)
     for by, part in ways:
@@ -480,7 +462,7 @@
     for s in range(2):
         for i in range(2):
             arrived(near_ref.at[s, i, pl.ds((1 - c) * share, share)], near_core_sem.at[s, i])
-    for copy in stores:
+    for copy in stores + clears:
         copy.wait()
     arrived(first_ref, first_sem)
     send.finish()
@@ -495,7 +477,7 @@
     return pl.pallas_call(
         gather_kernel,
         in_specs=[hbm] * 6,
-        out_specs=[hbm] * 7,
+        out_specs=[hbm] * 8,
         out_shape=[
             jax.ShapeDtypeStruct((2, 4, 4, 2, 2, rows // 2, cols), BF16),
             jax.ShapeDtypeStruct((2, 2, 2 * share, depth), BF16),
@@ -504,6 +486,7 @@
             jax.ShapeDtypeStruct(q.shape, BF16),
             jax.ShapeDtypeStruct(k.shape, F32),
             jax.ShapeDtypeStruct(v.shape, F32),
+            jax.ShapeDtypeStruct((NPSG, 2, PLEN, KV * D), BF16),
         ],
         scratch_shapes=[
             pltpu.VMEM((4, 4, 2, 2, rows // 2, cols), BF16),
@@ -515,8 +498,9 @@
             pltpu.VMEM(k.shape, F32),
             pltpu.VMEM(k.shape, F32),
             pltpu.VMEM((3 * share // 2, depth), BF16),
+            pltpu.VMEM((8, 2, PLEN, KV * D), BF16),
             dma((51,)), dma((2, 4, 4)), dma((4, 4)), dma((2,)), dma((2,)), dma((2, 2)), dma((2, 2)), dma((2,)), dma((4,)),
-            dma((4, 4)), dma, dma((4,)),
+            dma((4, 4)), dma, dma((4,)), dma((8,)),
         ],
         compiler_params=pltpu.CompilerParams(collective_id=0, has_side_effects=True, vmem_limit_bytes=VMEM),
         name="gather_plane",
@@ -770,10 +754,10 @@
 
 def local(q_psg, k_psg, v_psg, do_psg, q_qry, k_qry, v_qry, do_qry, w_key, w_value, req_passages, passage_slot, query_owner):
     me = lax.axis_index("psg").astype(jnp.int32).reshape(1)
-    every, near, far, first, dq_psg, own_k, own_v = gather_plane(q_psg, k_psg, v_psg, do_psg, w_key, w_value)
+    every, near, far, first, dq_psg, own_k, own_v, cleared = gather_plane(q_psg, k_psg, v_psg, do_psg, w_key, w_value)
     far = lax.ppermute(far, "head", [(i, (i + 2) % 4) for i in range(4)])
     dq_qry, g_qry, full, dq_psg = qry_back(
-        req_passages, passage_slot, query_owner, me, every.reshape(NPSG, 2, PLEN, -1), q_qry, do_qry, k_qry, v_qry, dq_psg
+        req_passages, passage_slot, query_owner, me, every.reshape(NPSG, 2, PLEN, -1), q_qry, do_qry, k_qry, v_qry, dq_psg, cleared
     )
     dx_psg, dx_qry = tail(full, own_k, own_v, g_qry, w_key, w_value, near, far, first)
     return dq_psg, dq_qry, dx_psg, dx_qry

time: 122 us -> 121 us (level)
  transfers between devices with their start and end apart: 1 -> 1, of which waited for: 0 -> 0; matrix products, arithmetic and copies ran while one was open for 1% -> 1% of each run, Pallas kernels for 17% -> 16%
where the time goes in v7:
time: 121 us
  Pallas kernels  112 us (93%)
  starting transfers between devices  5.02 us (4%)
  local copies, waits for them, and re-layouts  3.36 us (3%)
    pallas_call x1, Pallas kernels, tail(): pl.pallas_call(tail_kernel, in_specs=[hbm, vmem, vmem, hbm, hbm, hbm, hbm...  54.3 us
    pallas_call x1, Pallas kernels, gather_plane(): pl.pallas_call(gather_kernel, in_specs=[hbm] * 6, out_specs=[hbm] * 8, ou...  37.5 us
    pallas_call x1, Pallas kernels, qry_back(): pl.pallas_call(qry_kernel, in_specs=[smem] * 4 + [hbm] * 7, input_output_...  19.9 us
    ppermute x1, starting transfers between devices, local(): far = lax.ppermute(far, 'head', [(i, (i + 2) % 4) for i in range(4)])  5.02 us
    unnamed x13, local copies, waits for them, and re-layouts  3.36 us
  transfers between devices with their start and end apart: 1, of which 0 were waited for; matrix products, arithmetic and copies ran while one was open for 1% of the time, Pallas kernels for 16%

profile of v7, /device:TPU:1, one launch (start us, length us, event | category | flops | bytes accessed | tf_op | source)
XLA Modules:
  0.0 120.9 jit_solution(11222063697946248827)
XLA Ops:
  0.6 0.0 copy-start.4
  0.6 37.5 %gather_plane.1 = (bf16[2,4,4,2,2,128,256]{6,5,4,3,2,1,0:T(8,128)(2,1)}, bf16[2,2,2048,256]{3,2,1,0:T(8,128)(2,1)}, bf16[1536,256]{1,0:T(8,128)(2,1)}, bf16[512,...) custom-call(bf16[256,2048]{1,0:T(8,128)(2,1)} %q_ref.1, ...), custom_call_target="tpu_custom_call" | custom-call | tf_op jit(solution)/shard_map/gather_plane/pallas_call | solution.py:477
  38.2 5.0 %collective-permute-start = (bf16[1536,256]{1,0:T(8,128)(2,1)}, bf16[1536,256]{1,0:T(8,128)(2,1)S(1)}, u32[]{:S(2)}, u32[]{:S(2)}) collective-permute-start(bf16[1536,256]{1,0:T(8,128)(2,1)} %get-tuple-element.28), channel_id=1, source_target_pairs={{0,2},{1,3},{2,0},{3,1},{4,6},{5,7},{6,4},{7,5},{8,10},{9,11},{10,... | collective-permute-start | bytes 2359304 | tf_op jit(solution)/shard_map/ppermute | solution.py:758
  43.2 0.0 copy-done.4
  43.2 0.7 copy.18.req_ref
  43.9 0.0 copy-start
  43.9 0.0 copy-start.1
  43.9 0.0 copy-start.2
  43.9 19.9 %qry_back.1 = (bf16[128,2048]{1,0:T(8,128)(2,1)}, bf16[2,128,256]{2,1,0:T(8,128)(2,1)}, bf16[64,2,128,256]{3,2,1,0:T(8,128)(2,1)}, bf16[256,2048]{1,0:T(8,128)(2,1)}) custom-call(s32[32,16]{1,0:T(8,128)} %copy.18.req_ref, s32[64]{0:T(128)} %slot_ref.1, s32[32]{0:T(128)} %owner_ref.1, s32[1]{0:T(128)} %bitcast.me_ref, ...), custom_call_target="tpu_custom_call", output_to_operand_aliasing={{2}: (10, {})} | custom-call | flops 5704253440 | bytes 16777216 | tf_op jit(solution)/shard_map/qry_back/pallas_call | solution.py:226
  63.8 0.0 collective-permute-done.far_ref
  63.8 0.0 copy-done
  63.8 0.0 copy-done.1
  63.9 0.0 copy-done.2
  63.9 0.0 copy-start.3
  63.9 0.9 copy-done.3
  64.8 54.3 %tail.1 = (bf16[64,8192]{1,0:T(8,128)(2,1)S(1)}, bf16[32,8192]{1,0:T(8,128)(2,1)S(1)}) custom-call(bf16[2,4,4,2,2,2,2,32,256]{8,7,6,5,4,3,2,1,0:T(8,128)(2,1)} %bitcast.3, f32[256,256]{1,0:T(8,128)S(1)} %copy-done.1, f32[256,256]{1,0:T(8,128)S(1)} %copy-done.2, bf16[2,128,256]{2,1,0:T(8,128)(2,1)S(1)} %copy-done.3, bf16[8192,256]{1,0:T(8,128)(2,1)} %wk_ref.3, ...), custom_call_target="tpu_custom_call" | custom-call | tf_op jit(solution)/shard_map/tail/pallas_call | solution.py:722
  119.1 1.0 copy.22
  120.1 0.8 copy.23
Async XLA Ops:
  0.6 42.6 %copy-start.4 = (s32[32,16]{0,1:T(8,128)S(1)}, s32[32,16]{0,1:T(8,128)}, u32[]{:S(2)}) copy-start(s32[32,16]{0,1:T(8,128)} %param.23) | copy-start | bytes 6148
  38.2 25.6 %collective-permute-start = (bf16[1536,256]{1,0:T(8,128)(2,1)}, bf16[1536,256]{1,0:T(8,128)(2,1)S(1)}, u32[]{:S(2)}, u32[]{:S(2)}) collective-permute-start(bf16[1536,256]{1,0:T(8,128)(2,1)} %get-tuple-element.28), channel_id=1, source_target_pairs={{0,2},{1,3},{2,0},{3,1},{4,6},{5,7},{6,4},{7,5},{8,10},{9,11},{10,... | collective-permute-start | bytes 2359304 | tf_op jit(solution)/shard_map/ppermute | solution.py:758
  43.9 19.9 %copy-start = (bf16[512,256]{1,0:T(8,128)(2,1)S(1)}, bf16[512,256]{1,0:T(8,128)(2,1)}, u32[]{:S(2)}) copy-start(bf16[512,256]{1,0:T(8,128)(2,1)} %get-tuple-element.29.first_ref) | copy-start | bytes 786436
  43.9 20.0 %copy-start.1 = (f32[256,256]{1,0:T(8,128)S(1)}, f32[256,256]{1,0:T(8,128)}, u32[]{:S(2)}) copy-start(f32[256,256]{1,0:T(8,128)} %get-tuple-element.24.own_k_ref) | copy-start | bytes 786436
  43.9 20.0 %copy-start.2 = (f32[256,256]{1,0:T(8,128)S(1)}, f32[256,256]{1,0:T(8,128)}, u32[]{:S(2)}) copy-start(f32[256,256]{1,0:T(8,128)} %get-tuple-element.25.own_v_ref) | copy-start | bytes 786436
  63.9 0.9 copy-start.3

commit v8 on v7

--- a/solution.py
+++ b/solution.py
@@ -65,7 +65,7 @@
     return gk * C, gv
 
 
-TK = 1024
+TK = 2048
 TP = TK // PLEN
 NT = P_REQ * PLEN // TK
 
@@ -201,8 +201,7 @@
                 j = t * TP + i
                 gbuf[j, 0, :, cols] = gk[i * PLEN:(i + 1) * PLEN]
                 gbuf[j, 1, :, cols] = gv[i * PLEN:(i + 1) * PLEN]
-                if h == KV - 1:
-                    pltpu.make_async_copy(gbuf.at[j], full_ref.at[slots[j]], out_sem).start()
+                pltpu.make_async_copy(gbuf.at[j, :, :, cols], full_ref.at[slots[j], :, :, cols], out_sem).start()
             return carry
 
         lax.fori_loop(0, NT, grad_tile, 0)

time: 121 us -> 120 us (level)
  no operation moved by 1% of the time
where the time goes in v8:
time: 120 us
  Pallas kernels  111 us (92%)
  starting transfers between devices  4.84 us (4%)
  local copies, waits for them, and re-layouts  3.36 us (3%)
    pallas_call x1, Pallas kernels, tail(): pl.pallas_call(tail_kernel, in_specs=[hbm, vmem, vmem, hbm, hbm, hbm, hbm...  54.3 us
    pallas_call x1, Pallas kernels, gather_plane(): pl.pallas_call(gather_kernel, in_specs=[hbm] * 6, out_specs=[hbm] * 8, ou...  37.5 us
    pallas_call x1, Pallas kernels, qry_back(): pl.pallas_call(qry_kernel, in_specs=[smem] * 4 + [hbm] * 7, input_output_...  19.3 us
    ppermute x1, starting transfers between devices, local(): far = lax.ppermute(far, 'head', [(i, (i + 2) % 4) for i in range(4)])  4.84 us
    unnamed x13, local copies, waits for them, and re-layouts  3.36 us
  transfers between devices with their start and end apart: 1, of which 0 were waited for; matrix products, arithmetic and copies ran while one was open for 1% of the time, Pallas kernels for 16%

profile of v8, /device:TPU:1, one launch (start us, length us, event | category | flops | bytes accessed | tf_op | source)
XLA Modules:
  0.0 120.1 jit_solution(9488016454287186821)
XLA Ops:
  0.6 0.0 copy-start.4
  0.6 37.5 %gather_plane.1 = (bf16[2,4,4,2,2,128,256]{6,5,4,3,2,1,0:T(8,128)(2,1)}, bf16[2,2,2048,256]{3,2,1,0:T(8,128)(2,1)}, bf16[1536,256]{1,0:T(8,128)(2,1)}, bf16[512,...) custom-call(bf16[256,2048]{1,0:T(8,128)(2,1)} %q_ref.1, ...), custom_call_target="tpu_custom_call" | custom-call | tf_op jit(solution)/shard_map/gather_plane/pallas_call | solution.py:476
  38.2 4.8 %collective-permute-start = (bf16[1536,256]{1,0:T(8,128)(2,1)}, bf16[1536,256]{1,0:T(8,128)(2,1)S(1)}, u32[]{:S(2)}, u32[]{:S(2)}) collective-permute-start(bf16[1536,256]{1,0:T(8,128)(2,1)} %get-tuple-element.28), channel_id=1, source_target_pairs={{0,2},{1,3},{2,0},{3,1},{4,6},{5,7},{6,4},{7,5},{8,10},{9,11},{10,... | collective-permute-start | bytes 2359304 | tf_op jit(solution)/shard_map/ppermute | solution.py:757
  43.0 0.0 copy-done.4
  43.0 0.7 copy.18.req_ref
  43.7 0.0 copy-start
  43.7 0.0 copy-start.1
  43.7 0.0 copy-start.2
  43.7 19.3 %qry_back.1 = (bf16[128,2048]{1,0:T(8,128)(2,1)}, bf16[2,128,256]{2,1,0:T(8,128)(2,1)}, bf16[64,2,128,256]{3,2,1,0:T(8,128)(2,1)}, bf16[256,2048]{1,0:T(8,128)(2,1)}) custom-call(s32[32,16]{1,0:T(8,128)} %copy.18.req_ref, s32[64]{0:T(128)} %slot_ref.1, s32[32]{0:T(128)} %owner_ref.1, s32[1]{0:T(128)} %bitcast.me_ref, ...), custom_call_target="tpu_custom_call", output_to_operand_aliasing={{2}: (10, {})} | custom-call | flops 5704253440 | bytes 16777216 | tf_op jit(solution)/shard_map/qry_back/pallas_call | solution.py:225
  63.1 0.0 collective-permute-done.far_ref
  63.1 0.0 copy-done
  63.1 0.0 copy-done.1
  63.1 0.0 copy-done.2
  63.1 0.0 copy-start.3
  63.1 0.9 copy-done.3
  64.0 54.3 %tail.1 = (bf16[64,8192]{1,0:T(8,128)(2,1)S(1)}, bf16[32,8192]{1,0:T(8,128)(2,1)S(1)}) custom-call(bf16[2,4,4,2,2,2,2,32,256]{8,7,6,5,4,3,2,1,0:T(8,128)(2,1)} %bitcast.3, f32[256,256]{1,0:T(8,128)S(1)} %copy-done.1, f32[256,256]{1,0:T(8,128)S(1)} %copy-done.2, bf16[2,128,256]{2,1,0:T(8,128)(2,1)S(1)} %copy-done.3, bf16[8192,256]{1,0:T(8,128)(2,1)} %wk_ref.3, ...), custom_call_target="tpu_custom_call" | custom-call | tf_op jit(solution)/shard_map/tail/pallas_call | solution.py:721
  118.4 1.0 copy.22
  119.3 0.8 copy.23
Async XLA Ops:
  0.6 42.4 %copy-start.4 = (s32[32,16]{0,1:T(8,128)S(1)}, s32[32,16]{0,1:T(8,128)}, u32[]{:S(2)}) copy-start(s32[32,16]{0,1:T(8,128)} %param.23) | copy-start | bytes 6148
  38.2 24.9 %collective-permute-start = (bf16[1536,256]{1,0:T(8,128)(2,1)}, bf16[1536,256]{1,0:T(8,128)(2,1)S(1)}, u32[]{:S(2)}, u32[]{:S(2)}) collective-permute-start(bf16[1536,256]{1,0:T(8,128)(2,1)} %get-tuple-element.28), channel_id=1, source_target_pairs={{0,2},{1,3},{2,0},{3,1},{4,6},{5,7},{6,4},{7,5},{8,10},{9,11},{10,... | collective-permute-start | bytes 2359304 | tf_op jit(solution)/shard_map/ppermute | solution.py:757
  43.7 19.4 %copy-start = (bf16[512,256]{1,0:T(8,128)(2,1)S(1)}, bf16[512,256]{1,0:T(8,128)(2,1)}, u32[]{:S(2)}) copy-start(bf16[512,256]{1,0:T(8,128)(2,1)} %get-tuple-element.29.first_ref) | copy-start | bytes 786436
  43.7 19.4 %copy-start.1 = (f32[256,256]{1,0:T(8,128)S(1)}, f32[256,256]{1,0:T(8,128)}, u32[]{:S(2)}) copy-start(f32[256,256]{1,0:T(8,128)} %get-tuple-element.24.own_k_ref) | copy-start | bytes 786436
  43.7 19.4 %copy-start.2 = (f32[256,256]{1,0:T(8,128)S(1)}, f32[256,256]{1,0:T(8,128)}, u32[]{:S(2)}) copy-start(f32[256,256]{1,0:T(8,128)} %get-tuple-element.25.own_v_ref) | copy-start | bytes 786436
  63.1 0.9 copy-start.3
